TPU v7x, 32 devices: a whole 2x2x4 slice. The times are simulated.
32 devices in a mesh: seq: 2 (over x), fsdp: 16 (over z, y, core).
Axes of the slice: x: 2, y: 2, z: 4, core: 2. Of those that a mesh axis runs over, the one named last changes fastest.
Arguments:
- incoming_state: bfloat16 [16, 512, 768], P('fsdp', 'seq'), may hold values from -6 to 6
- projection_matrix_triple: bfloat16 [768, 2304], P(('seq', 'fsdp')), may hold values from -0.3125 to 0.3125
- merge_matrix: bfloat16 [768, 768], P(('seq', 'fsdp')), may hold values from -1.75 to 1.75
- widen_matrix: bfloat16 [768, 3072], P(('seq', 'fsdp')), may hold values from -0.21875 to 0.21875
- shrink_matrix: bfloat16 [3072, 768], P(('seq', 'fsdp')), may hold values from -0.109375 to 0.109375
- offset_table: bfloat16 [6, 768], P(None, ('seq', 'fsdp')), may hold values from -1.5 to 1.5
- norm_scales: bfloat16 [2, 768], P(None, ('seq', 'fsdp')), may hold values from 0.25 to 1.75
- widen_offset: bfloat16 [3072], P(('seq', 'fsdp')), may hold values from -1.5 to 1.5
- trainable_gate_scores: float32 [12, 512, 512], P('seq', 'fsdp'), may hold values from -8 to 8
- gate_perturbation: float32 [12, 512, 512], P('seq', 'fsdp'), may hold values from -6 to 6
- softening_scale: float32 [12], P('seq'), may hold values from 0.5 to 2
- passage_extents: int32 [32], replicated, may hold values from 1 to 512, 8192 in all
- result_cotangent: bfloat16 [16, 512, 768], P('fsdp', 'seq'), may hold values from -6 to 6
Outputs:
- layer_out: bfloat16 [16, 512, 768], P('fsdp', 'seq')
- input_grad: float32 [16, 512, 768], P('fsdp', 'seq')
- grad_w_qkv: float32 [768, 2304], P(('seq', 'fsdp'))
- grad_w_out: float32 [768, 768], P(('seq', 'fsdp'))
- grad_w_up: float32 [768, 3072], P(('seq', 'fsdp'))
- grad_w_down: float32 [3072, 768], P(('seq', 'fsdp'))
- grad_biases: float32 [6, 768], P(None, ('seq', 'fsdp'))
- grad_gains: float32 [2, 768], P(None, ('seq', 'fsdp'))
- grad_bias_up: float32 [3072], P(('seq', 'fsdp'))
- mask_logit_gradient: float32 [12, 512, 512], P('seq', 'fsdp')
Inputs may be any that keep to these rules, and one draw needn't show every extreme that they name: `passage_extents`: they sum to 8192, and the longest is exactly 512.
All inputs are finite; a program needn't handle non-finite values.
Results may differ from a plain program's by a relative error of at most 0.013.
Values may be sent and summed in bfloat16 or wider, within the bound.
No kernel may reach another device: no remote copies, remote signals or barrier semaphores. Data moves between devices by JAX's collectives and lax.ppermute only.
A program may use at most 192 MiB of HBM per device.

v0:
```python
from functools import partial

import jax
import jax.numpy as jnp
from jax import lax
from jax.experimental import pallas as pl
from jax.experimental.pallas import tpu as pltpu
from jax.sharding import PartitionSpec as P

D = 768
FF = 3072
HEADS = 12
HDIM = 64
MPOS = 512
EPS = 1e-05
GROUP = 512
HALF = 256
WINDOW = 3 * GROUP
OWN = 384
CHUNK = 256
NEG = -1e30
BF = jnp.bfloat16
F32 = jnp.float32
HIGH = lax.Precision.HIGHEST
PART_TOTALS = 144
PART_SUMS = 160
PART_OUT = 192
PART = 240
PART_TABLE = 256


def nn(left, right):
    return jnp.dot(left, right, preferred_element_type=F32)


def nt(left, right, precision=None):
    return lax.dot_general(
        left, right, (((1,), (1,)), ((), ())), precision=precision, preferred_element_type=F32
    )


def tn(left, right):
    return lax.dot_general(left, right, (((0,), (0,)), ((), ())), preferred_element_type=F32)


def load_projection(gathered, w, sem):
    copies = []
    for f in range(16):
        row = (f % 2) * OWN + (f // 2) * 48
        copies.append(
            pltpu.make_async_copy(gathered.at[f, 16:25], w.at[:, row : row + 48, :], sem.at[f])
        )
    for copy in copies:
        copy.start()
    return copies


def table_of(table, head):
    return jnp.concatenate(
        [table[:, 4 * head + part].reshape(MPOS, 128) for part in range(4)], axis=1
    )


def spread_out(values, spread, owner, group):
    return jnp.sum(jnp.where(owner == group, nn(values, spread), 0.0), axis=0, keepdims=True)


def columns_of(w, first, count=3):
    return jnp.concatenate([w[first + part] for part in range(count)], axis=1)


def place_of(t, cr, scal):
    unit = ((t >> 2) ^ (scal[0] & 1)) | ((t & 3) << 1)
    return 2 * unit + (scal[1] ^ cr)


def near_place_of(t, cr, scal):
    unit = ((t >> 2) | (t & 2) | ((t & 1) << 2)) ^ scal[0]
    return 2 * unit + (scal[1] ^ cr)


def project_kernel(
    scal,
    x1,
    x0,
    x2,
    y1,
    y0,
    y2,
    gathered,
    near,
    owner,
    spread,
    group,
    q_ref,
    k_ref,
    v_ref,
    xw,
    k_turned,
    x_turned,
    w,
    sem,
):
    copies = load_projection(gathered, w, sem)
    side = scal[2]
    for g, (mine, other) in enumerate(((x0, y0), (x1, y1), (x2, y2))):
        xw[pl.ds(pl.multiple_of(g * GROUP + side * HALF, HALF), HALF), :] = mine[...]
        xw[pl.ds(pl.multiple_of(g * GROUP + (1 - side) * HALF, HALF), HALF), :] = other[...]
    bias = [
        spread_out(near[i], spread[:, :OWN], owner[...], group[:, :OWN]) for i in range(2)
    ]
    for copy in copies:
        copy.wait()
    for blk in range(6):
        rows = slice(blk * HALF, (blk + 1) * HALF)
        here = xw[rows, :]
        key = nn(here, columns_of(w, 3))
        k_ref[rows, :] = key.astype(BF)
        k_turned[blk] = key.T.astype(BF)
        x_turned[:, rows] = here.astype(F32).T.astype(BF)
        v_ref[rows, :] = (nn(here, columns_of(w, 6)) + bias[1]).astype(BF)
        if blk in (2, 3):
            local = slice((blk - 2) * HALF, (blk - 1) * HALF)
            query = (nn(here, columns_of(w, 0)) + bias[0]).astype(BF)
            q_ref[local, :] = query * jnp.asarray(0.125, BF)


def head_lanes():
    return lax.broadcasted_iota(jnp.int32, (1, 128), 1) < HDIM


def fill_hot(pos_col, hot):
    for blk in range(6):
        rows = slice(blk * 256, (blk + 1) * 256)
        column = lax.broadcasted_iota(jnp.int32, (256, MPOS), 1)
        hot[rows, :] = jnp.where(pos_col[rows, :] == column, 1.0, 0.0).astype(BF)


def fill_hot_turned(pos_row, hot):
    for blk in range(6):
        rows = lax.broadcasted_iota(jnp.int32, (MPOS, 256), 0)
        hot[blk] = jnp.where(pos_row[blk] == rows, 1.0, 0.0).astype(BF)


def set_pair(low, value, target):
    blank = jnp.zeros_like(value)
    target[:HALF, :] = jnp.where(low, value, blank)
    target[HALF:, :] = jnp.where(low, blank, value)


def fold(values, how):
    rows, columns = values.shape
    return how(values.reshape(rows // 8, 8, columns), axis=0)


def attend_kernel(
    scal,
    pos_col,
    pos_row,
    doc_col,
    doc_row,
    q,
    k,
    v,
    table,
    ctx,
    inverses,
    weights,
    mixes,
    hot_turned,
    hot,
    sbuf,
    looks,
    queries,
    acc,
):
    @pl.when(pl.program_id(0) == 0)
    def _():
        fill_hot(pos_col, hot)
        fill_hot_turned(pos_row, hot_turned)

    low = head_lanes()
    for qb in range(2):
        lo, hi = scal[3 + 2 * qb], scal[4 + 2 * qb]
        here = slice(qb * HALF, (qb + 1) * HALF)
        set_pair(low, q[here, :], queries)
        q_doc = jnp.concatenate([doc_row[2 + qb]] * 2, axis=1)
        q_hot = hot[GROUP + qb * HALF : GROUP + (qb + 1) * HALF, :]
        for h in range(2):
            looks[h * HALF : (h + 1) * HALF, :] = nn(q_hot, table_of(table, h)).astype(BF)

        def score_step(c, top, q_doc=q_doc):
            rows = pl.ds(pl.multiple_of(c * CHUNK, CHUNK), CHUNK)
            s = jnp.where(doc_col[rows, :] == q_doc, nt(k[rows, :], queries[...]), NEG)
            sbuf[c] = s
            return jnp.maximum(top, fold(s, jnp.max))

        top = lax.fori_loop(lo, hi, score_step, jnp.full((8, 2 * HALF), NEG, F32))
        top = jnp.max(top, axis=0, keepdims=True)
        acc[...] = jnp.zeros_like(acc)

        def mix_step(c, total, top=top, qb=qb):
            rows = pl.ds(pl.multiple_of(c * CHUNK, CHUNK), CHUNK)
            e = jnp.exp(sbuf[c] - top)
            mixed = (e * nt(hot[rows, :], looks[...])).astype(BF)
            weights[0, qb, c] = e.astype(BF)
            mixes[0, qb, c] = mixed
            acc[...] += tn(mixed, v[rows, :])
            return total + fold(e, jnp.sum)

        total = lax.fori_loop(lo, hi, mix_step, jnp.zeros((8, 2 * HALF), F32))
        total = jnp.sum(total, axis=0, keepdims=True)
        inverse = 1.0 / total
        inverses[0, 0:1, here] = inverse[:, :HALF]
        inverses[0, 1:2, here] = inverse[:, HALF:]
        inverses[0, 2:8, here] = jnp.zeros((6, HALF), F32)
        scale = jnp.concatenate(
            [
                jnp.broadcast_to(inverse[:, :HALF], (HDIM, HALF)),
                jnp.broadcast_to(inverse[:, HALF:], (HDIM, HALF)),
            ],
            axis=0,
        ).T
        ctx[qb] = (jnp.where(low, acc[:HALF, :], acc[HALF:, :]) * scale).astype(BF)


def attend_back_kernel(
    carried,
    scal,
    q,
    k,
    v,
    weights,
    mixes,
    hot_turned,
    xw,
    sums,
    ctx,
    ctx_all,
    dctx0,
    dctx1,
    dattn0,
    dattn1,
    inverses,
    *refs,
):
    outs = refs[carried : carried + 8]
    dq, own, halo_low, halo_high, part_keep, part_send, table_keep, table_send = outs
    queries, grads, dk, dv, dq_acc, tt, tg, gw, gout = refs[carried + 8 :]
    low = head_lanes()
    dk[...] = jnp.zeros_like(dk)
    dv[...] = jnp.zeros_like(dv)
    lane = lax.broadcasted_iota(jnp.int32, (8, 128), 1)
    row8 = lax.broadcasted_iota(jnp.int32, (8, 128), 0)
    pick = jnp.where((lane < HDIM) == (row8 == 0), 1.0, 0.0)
    for qb in range(2):
        lo, hi = scal[3 + 2 * qb], scal[4 + 2 * qb]
        here = slice(qb * HALF, (qb + 1) * HALF)
        inverse = inverses[0, 0:2, here]
        d_pair = (dctx0, dctx1)[qb][...].astype(F32)
        deltas = nt(pick, d_pair * ctx[qb].astype(F32), HIGH)[0:2, :] * inverse
        delta = jnp.concatenate([deltas[0:1, :], deltas[1:2, :]], axis=1)
        scale = jnp.concatenate(
            [
                jnp.broadcast_to(inverse[0:1, :], (HDIM, HALF)),
                jnp.broadcast_to(inverse[1:2, :], (HDIM, HALF)),
            ],
            axis=0,
        ).T
        set_pair(low, q[here, :], queries)
        set_pair(low, (d_pair * scale).astype(BF), grads)
        dq_acc[...] = jnp.zeros_like(dq_acc)
        tt[...] = jnp.zeros_like(tt)

        def step(c, carry, delta=delta, qb=qb):
            rows = pl.ds(pl.multiple_of(c * CHUNK, CHUNK), CHUNK)
            mixed = mixes[0, qb, c]
            e = weights[0, qb, c].astype(F32)
            dm = nt(v[rows, :], grads[...])
            ds = (mixed.astype(F32) * dm - e * delta).astype(BF)
            dv[rows, :] += nn(mixed, grads[...])
            dk[rows, :] += nn(ds, queries[...])
            dq_acc[...] += nn(k[c], ds)
            tt[...] += nn(hot_turned[c], (e * dm).astype(BF))
            return carry

        lax.fori_loop(lo, hi, step, 0)
        for h in range(2):
            piece = nt(hot_turned[2 + qb], tt[:, h * HALF : (h + 1) * HALF].astype(BF))
            if qb == 0:
                tg[h] = piece
            else:
                tg[h] += piece
        both = jnp.concatenate([dq_acc[:HDIM, :HALF], dq_acc[HDIM:, HALF:]], axis=0)
        dq[here, :] = (both.T * 0.125).astype(BF)
    own[0] = dk[GROUP : 2 * GROUP, :]
    own[1] = dv[GROUP : 2 * GROUP, :]
    halo_low[0] = dk[:GROUP, :].astype(BF)
    halo_low[1] = dv[:GROUP, :].astype(BF)
    halo_high[0] = dk[2 * GROUP :, :].astype(BF)
    halo_high[1] = dv[2 * GROUP :, :].astype(BF)
    query_grad = dq[...]
    pair_grad = jnp.concatenate([dk[...].astype(BF), dv[...].astype(BF)], axis=1)
    gw[:, 0:128] = nn(xw[:, GROUP : 2 * GROUP], query_grad)
    gw[:, 128:384] = nn(xw[...], pair_grad)
    gout[...] = tn(ctx_all[0], dattn0[...]) + tn(ctx_all[1], dattn1[...])
    totals = jnp.concatenate(
        [
            column_sum(query_grad.astype(F32)),
            column_sum(pair_grad[:, 128:].astype(F32)),
            jnp.zeros((14, 128), F32),
            sums[:, 0:128],
            sums[:, 128:256],
        ],
        axis=0,
    ).astype(BF)
    for cr in range(2):
        out, table = (part_keep, table_keep) if cr == 0 else (part_send, table_send)
        for t in range(8):
            place = place_of(t, cr, scal)
            rows = [
                gw[pl.ds(pl.multiple_of(part * OWN + place * 24, 8), 24), :] for part in range(2)
            ]
            both = jnp.concatenate(rows, axis=0).astype(BF)
            for i in range(3):
                out[t, i * 48 : i * 48 + 48, :] = both[:, i * 128 : (i + 1) * 128]
            out[t, PART_TOTALS:PART_OUT, :] = totals
            rows = gout[pl.ds(pl.multiple_of(place * 24, 8), 24), :]
            out[t, PART_OUT:PART, :] = jnp.concatenate(
                [rows[:, 0:128], rows[:, 128:256]], axis=0
            ).astype(BF)
            for h in range(2):
                mask = tg[h, pl.ds(pl.multiple_of(place * 32, 32), 32), :].astype(BF)
                for i in range(4):
                    at = (4 * h + i) * 32
                    table[t, at : at + 32, :] = mask[:, i * 128 : (i + 1) * 128]


def norm_stats(values):
    center = values - jnp.mean(values, axis=-1, keepdims=True)
    rstd = lax.rsqrt(jnp.mean(center * center, axis=-1, keepdims=True) + EPS)
    return center * rstd, rstd


def norm_back(grad, unit, rstd, gain):
    scaled = grad * gain
    return rstd * (
        scaled
        - jnp.mean(scaled, axis=-1, keepdims=True)
        - unit * jnp.mean(scaled * unit, axis=-1, keepdims=True)
    )


def column_sum(values):
    return jnp.sum(values, axis=0, keepdims=True)


def load_feed(wg, sem, wm=None, wu=None, wd=None):
    copies = []

    def bring(source, target):
        copies.append(pltpu.make_async_copy(source, target, sem.at[len(copies)]))
        copies[-1].start()

    for c in range(2):
        for s in range(2):
            if wm is not None:
                bring(
                    wg.at[:, c, 192:240, s * OWN : (s + 1) * OWN],
                    wm.at[s, :, :, c * OWN : (c + 1) * OWN],
                )
    for c in range(2):
        for s in range(2):
            if wu is not None:
                bring(wg.at[:, c, 96 + 48 * s : 144 + 48 * s, :], wu.at[c, s])
    for c in range(2):
        if wd is not None:
            bring(wg.at[:, c, 0:96, :], wd.at[:, c])
    return copies


def shrink_rows(wd, i):
    return wd[pl.ds(4 * i, 4)].reshape(D, D)


def wait_for(copies):
    for copy in copies:
        copy.wait()


def feed_up_kernel(
    scal,
    x,
    ctx_mine,
    ctx_other,
    smalls,
    owner,
    near,
    near_owner,
    spread,
    group,
    spread_up,
    group_up,
    wg,
    unit1,
    rstd1,
    nlow,
    base,
    send,
    act,
    slope,
    wm,
    wu,
    wd,
    ctxt,
    bup,
    sem,
):
    copies = load_feed(wg, sem, wm, wu, wd)
    vector = lambda i: spread_out(smalls[i], spread[...], owner[...], group[...])
    bias_out, bias_down, shift1, gain1 = [vector(i) for i in (2, 3, 4, 6)]
    for n in range(2):
        bup[n] = spread_out(
            near[8], spread_up[...], near_owner[...], group_up[...] + n * (near.shape[1] // 2)
        )
    even = scal[2] == 0
    mine, other = ctx_mine[0], ctx_other[0]
    ctxt[:, :OWN] = jnp.where(even, mine, other)
    ctxt[:, OWN:] = jnp.where(even, other, mine)
    wait_for(copies[:4])
    attn = nn(ctxt[...], wm[...].reshape(D, D)) + bias_out
    unit, rstd = norm_stats(x[...].astype(F32) + attn)
    unit1[...] = unit
    rstd1[...] = jnp.broadcast_to(rstd, (HALF, 128))
    normed = unit * gain1 + shift1
    nlow[...] = normed.astype(BF)
    base[...] = normed + bias_down
    wait_for(copies[4:8])

    def widen(n, carry):
        up = nn(nlow[...], wu[n].reshape(D, D)) + bup[n]
        half_cdf = 0.5 * (1.0 + lax.erf(up * 0.7071067811865476))
        act[n] = (up * half_cdf).astype(BF)
        slope[n] = half_cdf + up * (0.3989422804014327 * jnp.exp(-0.5 * up * up))
        return carry

    lax.fori_loop(0, 2, widen, 0)
    wait_for(copies[8:])
    part = nn(act[0], shrink_rows(wd, 0)) + nn(act[1], shrink_rows(wd, 1))
    base[...] += part
    send[...] = part.astype(BF)


def feed_back_kernel(
    index,
    scal,
    base,
    got,
    cot_mine,
    cot_other,
    slope,
    smalls,
    owner,
    spread,
    group,
    wg,
    lay,
    ddown,
    dup,
    base2,
    send,
    sums,
    wu,
    wd,
    sem,
):
    copies = load_feed(wg, sem, None, wu, wd)
    vector = lambda i: spread_out(smalls[i], spread[...], owner[...], group[...])
    shift2, gain2 = vector(5), vector(7)
    sums[...] = jnp.zeros_like(sums)
    unit, rstd = norm_stats(base[...] + got[...].astype(F32))
    lay[...] = (unit * gain2 + shift2).astype(BF)
    dy = jnp.where(scal[2] == index, cot_mine[...], cot_other[...]).astype(F32)
    sums[3:4, :] = column_sum(dy)
    sums[5:6, :] = column_sum(dy * unit)
    grad = norm_back(dy, unit, rstd, gain2)
    ddown[...] = grad.astype(BF)
    sums[1:2, :] = column_sum(ddown[...].astype(F32))
    base2[...] = grad
    wait_for(copies)

    def back(n, carry):
        low = (nt(ddown[...], shrink_rows(wd, n)) * slope[n]).astype(BF)
        dup[n] = low
        sums[pl.ds(8 + n, 1), :] = column_sum(low.astype(F32))
        return carry

    lax.fori_loop(0, 2, back, 0)
    part = nt(dup[0], wu[0].reshape(D, D)) + nt(dup[1], wu[1].reshape(D, D))
    base2[...] += part
    send[...] = part.astype(BF)


def feed_close_kernel(
    scal,
    base,
    got,
    unit1,
    rstd1,
    sums_in,
    smalls,
    owner,
    spread,
    group,
    wg,
    dh1,
    dattn,
    dctx,
    sums,
    wm,
    sem,
):
    copies = load_feed(wg, sem, wm)
    gain1 = spread_out(smalls[6], spread[...], owner[...], group[...])
    sums[...] = sums_in[...]
    grad = base[...] + got[...].astype(F32)
    unit = unit1[...]
    sums[2:3, :] += column_sum(grad)
    sums[4:5, :] += column_sum(grad * unit)
    grad = norm_back(grad, unit, rstd1[:, 0:1], gain1)
    dh1[...] = grad
    dattn[...] = grad.astype(BF)
    sums[0:1, :] += column_sum(dattn[...].astype(F32))
    wait_for(copies)
    dctx[...] = nt(dattn[...], wm[scal[2]].reshape(OWN, D)).astype(BF)


def weight_grad_kernel(
    scal, act0, ddown0, nlow0, dup0, act1, ddown1, nlow1, dup1, keep, send, down, up
):
    for n in range(2):
        up[n] = tn(nlow0[...], dup0[n]) + tn(nlow1[...], dup1[n])
        down[n * D : (n + 1) * D, :] = tn(act0[n], ddown0[...]) + tn(act1[n], ddown1[...])
    for cr, out in enumerate((keep, send)):
        for t in range(8):
            place = near_place_of(t, cr, scal)
            out[t, 0:96, :] = down[pl.ds(pl.multiple_of(place * 96, 8), 96), :].astype(BF)
            parts = [
                up[n, pl.ds(pl.multiple_of(s * OWN + place * 24, 8), 24), :]
                for s in range(2)
                for n in range(2)
            ]
            out[t, 96:192, :] = jnp.concatenate(parts, axis=0).astype(BF)


def project_back_kernel(scal, parts, dh1s, gathered, dx, dx_send, w, dqkv, sem):
    copies = load_projection(gathered, w, sem)
    dq, own, left, right = parts
    dqkv[:, :OWN] = dq[...]
    for i in range(2):
        total = own[i] + left[i].astype(F32) + right[i].astype(F32)
        dqkv[:, (1 + i) * OWN : (2 + i) * OWN] = total.astype(BF)
    for copy in copies:
        copy.wait()
    side = scal[2]
    mine = dqkv[pl.ds(pl.multiple_of(side * HALF, HALF), HALF), :]
    other = dqkv[pl.ds(pl.multiple_of((1 - side) * HALF, HALF), HALF), :]
    for part in range(3):
        cols = slice(part * 256, (part + 1) * 256)
        rows = jnp.concatenate([w[j, cols, :] for j in range(9)], axis=1)
        dh1 = jnp.where(side == 0, dh1s[0][:, cols], dh1s[1][:, cols])
        dx[:, cols] = dh1 + nt(mine, rows)
        dx_send[:, cols] = nt(other, rows).astype(BF)


SMEM = pl.BlockSpec(memory_space=pltpu.SMEM)
VM = pl.BlockSpec()
HBM = pl.BlockSpec(memory_space=pl.ANY)


def params():
    return pltpu.CompilerParams(vmem_limit_bytes=60 * 1024 * 1024)


def cost(microseconds):
    return pl.CostEstimate(
        flops=int(microseconds * 1.15e9), bytes_accessed=1000, transcendentals=0
    )


def shape(dims, kind):
    return jax.ShapeDtypeStruct(dims, kind)


def project(scal, pieces, gathered, near, owner, spread, group):
    return pl.pallas_call(
        project_kernel,
        name="project",
        out_shape=(
            shape((GROUP, OWN), BF),
            shape((WINDOW, OWN), BF),
            shape((WINDOW, OWN), BF),
            shape((WINDOW, D), BF),
            shape((6, OWN, CHUNK), BF),
            shape((D, WINDOW), BF),
        ),
        in_specs=[SMEM] + [VM] * 6 + [HBM] + [VM] * 4,
        out_specs=[VM] * 6,
        scratch_shapes=[
            pltpu.VMEM((9, D, 128), BF),
            pltpu.SemaphoreType.DMA((16,)),
        ],
        compiler_params=params(),
        cost_estimate=cost(9),
    )(scal, *pieces, gathered, near, owner, spread, group)


def whole(*dims):
    return pl.BlockSpec(dims, lambda p: (0,) * len(dims))


def attend(scal, pos_col, pos_row, doc_col, doc_row, q, k, v, table):
    return pl.pallas_call(
        attend_kernel,
        name="attend",
        grid=(3,),
        out_shape=(
            shape((2, HALF, OWN), BF),
            shape((3, 8, GROUP), F32),
            shape((3, 2, 6, CHUNK, 2 * HALF), BF),
            shape((3, 2, 6, CHUNK, 2 * HALF), BF),
            shape((6, MPOS, CHUNK), BF),
        ),
        in_specs=[
            SMEM,
            whole(WINDOW, 1),
            whole(6, 1, CHUNK),
            whole(WINDOW, 1),
            whole(6, 1, CHUNK),
            pl.BlockSpec((GROUP, 128), lambda p: (0, p)),
            pl.BlockSpec((WINDOW, 128), lambda p: (0, p)),
            pl.BlockSpec((WINDOW, 128), lambda p: (0, p)),
            pl.BlockSpec((16, 8, 32, 128), lambda p: (0, p, 0, 0)),
        ],
        out_specs=[
            pl.BlockSpec((2, HALF, 128), lambda p: (0, 0, p)),
            pl.BlockSpec((1, 8, GROUP), lambda p: (p, 0, 0)),
            pl.BlockSpec((1, 2, 6, CHUNK, 2 * HALF), lambda p: (p, 0, 0, 0, 0)),
            pl.BlockSpec((1, 2, 6, CHUNK, 2 * HALF), lambda p: (p, 0, 0, 0, 0)),
            whole(6, MPOS, CHUNK),
        ],
        scratch_shapes=[
            pltpu.VMEM((WINDOW, MPOS), BF),
            pltpu.VMEM((6, CHUNK, 2 * HALF), F32),
            pltpu.VMEM((2 * HALF, MPOS), BF),
            pltpu.VMEM((2 * HALF, 128), BF),
            pltpu.VMEM((2 * HALF, 128), F32),
        ],
        compiler_params=params(),
        cost_estimate=cost(26),
    )(scal, pos_col, pos_row, doc_col, doc_row, q, k, v, table)


def attend_back(
    first, pairs, before, scal, q, k, v, kept, xw, sums, ctx, dctx, dattn, inverses
):
    columns = lambda rows: pl.BlockSpec((rows, 128), lambda p: (0, first + p))
    tiles = pl.BlockSpec((1, 2, 6, CHUNK, 2 * HALF), lambda p: (first + p, 0, 0, 0, 0))
    blocks = lambda rows: pl.BlockSpec((8, rows, 128), lambda p: (0, first + p, 0))
    both = pl.BlockSpec((2, GROUP, 128), lambda p: (0, 0, first + p))
    return pl.pallas_call(
        partial(attend_back_kernel, len(before)),
        name=f"attend_back_{first}",
        grid=(pairs,),
        input_output_aliases={16 + i: i for i in range(len(before))},
        out_shape=(
            shape((GROUP, OWN), BF),
            shape((2, GROUP, OWN), F32),
            shape((2, GROUP, OWN), BF),
            shape((2, GROUP, OWN), BF),
            shape((8, 3 * PART, 128), BF),
            shape((8, 3 * PART, 128), BF),
            shape((8, 3 * PART_TABLE, 128), BF),
            shape((8, 3 * PART_TABLE, 128), BF),
        ),
        in_specs=[
            SMEM,
            columns(GROUP),
            pl.BlockSpec((6, 128, CHUNK), lambda p: (0, first + p, 0)),
            columns(WINDOW),
            tiles,
            tiles,
            whole(6, MPOS, CHUNK),
            whole(D, WINDOW),
            pl.BlockSpec((16, 256), lambda p: (0, first + p)),
            pl.BlockSpec((2, HALF, 128), lambda p: (0, 0, first + p)),
            whole(2, HALF, OWN),
            columns(HALF),
            columns(HALF),
            pl.BlockSpec((HALF, 256), lambda p: (0, first + p)),
            pl.BlockSpec((HALF, 256), lambda p: (0, first + p)),
            pl.BlockSpec((1, 8, GROUP), lambda p: (first + p, 0, 0)),
        ]
        + [HBM] * len(before),
        out_specs=[
            columns(GROUP),
            both,
            both,
            both,
            blocks(PART),
            blocks(PART),
            blocks(PART_TABLE),
            blocks(PART_TABLE),
        ],
        scratch_shapes=[
            pltpu.VMEM((2 * HALF, 128), BF),
            pltpu.VMEM((2 * HALF, 128), BF),
            pltpu.VMEM((WINDOW, 128), F32),
            pltpu.VMEM((WINDOW, 128), F32),
            pltpu.VMEM((128, 2 * HALF), F32),
            pltpu.VMEM((MPOS, 2 * HALF), F32),
            pltpu.VMEM((2, MPOS, MPOS), F32),
            pltpu.VMEM((D, OWN), F32),
            pltpu.VMEM((OWN, 256), F32),
        ],
        compiler_params=params(),
        cost_estimate=cost(10 * pairs),
    )(scal, q, k, v, *kept, xw, sums, ctx, ctx, *dctx, *dattn, inverses, *before)


WIDEN = pltpu.VMEM((2, 2, 8, 48, D), BF)
SHRINK = pltpu.VMEM((8, 2, 96, D), BF)
MERGE = pltpu.VMEM((2, 8, 48, D), BF)


def feed_up(index, scal, xw, mine, other, smalls, owner, near, near_owner, spreads, wg):
    arrays = (smalls, owner, near, near_owner, *spreads)
    ctx = pl.BlockSpec((1, HALF, OWN), lambda p: (index, 0, 0))
    outs = (
        shape((HALF, D), F32),
        shape((HALF, 128), F32),
        shape((HALF, D), BF),
        shape((HALF, D), F32),
        shape((HALF, D), BF),
        shape((2, HALF, D), BF),
        shape((2, HALF, D), F32),
    )
    return pl.pallas_call(
        feed_up_kernel,
        name=f"feed_up_{index}",
        grid=(1,),
        out_shape=outs,
        in_specs=[SMEM, pl.BlockSpec((HALF, D), lambda p: (2 + index, 0)), ctx, ctx]
        + [whole(*a.shape) for a in arrays]
        + [HBM],
        out_specs=[whole(*out.shape) for out in outs],
        scratch_shapes=[
            MERGE,
            WIDEN,
            SHRINK,
            pltpu.VMEM((HALF, D), BF),
            pltpu.VMEM((2, 1, D), F32),
            pltpu.SemaphoreType.DMA((10,)),
        ],
        compiler_params=params(),
        cost_estimate=cost(8),
    )(scal, xw, mine, other, *arrays, wg)


def feed_back(index, scal, base, got, cot, cot_other, slope, smalls, owner, spread, group, wg):
    return pl.pallas_call(
        partial(feed_back_kernel, index),
        name=f"feed_back_{index}",
        out_shape=(
            shape((HALF, D), BF),
            shape((HALF, D), BF),
            shape((2, HALF, D), BF),
            shape((HALF, D), F32),
            shape((HALF, D), BF),
            shape((16, D), F32),
        ),
        in_specs=[SMEM] + [VM] * 9 + [HBM],
        out_specs=[VM] * 6,
        scratch_shapes=[WIDEN, SHRINK, pltpu.SemaphoreType.DMA((6,))],
        compiler_params=params(),
        cost_estimate=cost(7),
    )(scal, base, got, cot, cot_other, slope, smalls, owner, spread, group, wg)


def feed_close(index, scal, base, got, unit1, rstd1, sums, smalls, owner, spread, group, wg):
    return pl.pallas_call(
        feed_close_kernel,
        name=f"feed_close_{index}",
        out_shape=(
            shape((HALF, D), F32),
            shape((HALF, D), BF),
            shape((HALF, OWN), BF),
            shape((16, D), F32),
        ),
        in_specs=[SMEM] + [VM] * 9 + [HBM],
        out_specs=[VM] * 4,
        scratch_shapes=[MERGE, pltpu.SemaphoreType.DMA((4,))],
        compiler_params=params(),
        cost_estimate=cost(4),
    )(scal, base, got, unit1, rstd1, sums, smalls, owner, spread, group, wg)


def weight_grads(scal, *halves):
    return pl.pallas_call(
        weight_grad_kernel,
        name="weight_grads",
        out_shape=(shape((8, 192, D), BF), shape((8, 192, D), BF)),
        in_specs=[SMEM] + [VM] * 8,
        out_specs=[VM] * 2,
        scratch_shapes=[pltpu.VMEM((2 * D, D), F32), pltpu.VMEM((2, D, D), F32)],
        compiler_params=params(),
        cost_estimate=cost(7),
    )(scal, *halves)


def project_back(scal, parts, dh1, gathered):
    def kernel(scal, *refs):
        project_back_kernel(scal, refs[:4], refs[4:6], *refs[6:])

    return pl.pallas_call(
        kernel,
        name="project_back",
        out_shape=(shape((HALF, D), F32), shape((HALF, D), BF)),
        in_specs=[SMEM] + [VM] * 6 + [HBM],
        out_specs=[VM] * 2,
        scratch_shapes=[
            pltpu.VMEM((9, D, 128), BF),
            pltpu.VMEM((GROUP, 3 * OWN), BF),
            pltpu.SemaphoreType.DMA((16,)),
        ],
        compiler_params=params(),
        cost_estimate=cost(6),
    )(scal, *parts, *dh1, gathered)


def swap(value, axis, bit):
    count = lax.axis_size(axis)
    return lax.ppermute(value, axis, [(i, i ^ bit) for i in range(count)])


def shifted(value, axis, steps):
    count = lax.axis_size(axis)
    leading, last = (max(0, -steps), min(count, count - steps))
    return lax.ppermute(value, axis, [(source, source + steps) for source in range(leading, last)])


def tie(*values):
    return lax.optimization_barrier(values)


CORE, ALONG_Y, SIDE = ("fsdp", 1), ("fsdp", 2), ("seq", 1)


def along_z(values):
    groups = [[4 * z + i for z in range(4)] for i in range(4)]
    return lax.all_to_all(values, "fsdp", 0, 0, axis_index_groups=groups, tiled=True)


def add(mine, got):
    return (mine.astype(F32) + got.astype(F32)).astype(mine.dtype)


def by_core(value):
    return value.reshape(2, 4, *value.shape[1:])


def sum_core(keep, got):
    keep = by_core(keep)
    return add(keep[0], got[0]), add(keep[1], got[1])


def sum_z(got):
    return jnp.sum(got.astype(F32), axis=0).astype(got.dtype)


def in_order(flag, mine, other, axis):
    first = jnp.where(flag == 0, mine, other)
    second = jnp.where(flag == 0, other, mine)
    return jnp.concatenate([first, second], axis=axis)


def locate(index, opening, finish, stream_rows):
    document = jnp.sum((finish[None, :] <= index[:, None]).astype(jnp.int32), axis=1)
    begin = jnp.max(jnp.where(opening[None, :] <= index[:, None], opening[None, :], 0), axis=1)
    inside = (index >= 0) & (index < stream_rows)
    document = jnp.where(inside, document, -1)
    position = (index - begin) % MPOS
    return document, position


def own_columns(weight, nf, side, place):
    rows = weight.shape[0]
    weight = weight.reshape(rows, 3, 2, OWN)
    core = place % 2
    keep = lax.dynamic_index_in_dim(weight, side, 2, False).reshape(rows, 3 * OWN)
    give = lax.dynamic_index_in_dim(weight, 1 - side, 2, False).reshape(rows, 3 * OWN)
    straight, crossed, near = [], [], []
    for s in range(2):
        for f in range(nf):
            here = s * nf + f
            if f % 2 == s:
                straight.append((here, (1 - s) * nf + f))
            else:
                crossed.append((here, (1 - s) * nf + (f ^ 1)))
                near.append((here, s * nf + (f ^ 1)))
    axes = ("seq", "fsdp")
    same = core == side
    mine = jnp.where(same, keep, lax.ppermute(give, axes, straight))
    other = jnp.where(same, lax.ppermute(keep, axes, near), lax.ppermute(give, axes, crossed))
    return in_order(core, mine, other, 0)


def per_device(
    incoming_state,
    projection_matrix_triple,
    merge_matrix,
    widen_matrix,
    shrink_matrix,
    offset_table,
    norm_scales,
    widen_offset,
    trainable_gate_scores,
    gate_perturbation,
    softening_scale,
    passage_extents,
    result_cotangent,
):
    BOTH = ("seq", "fsdp")
    ns, nf = lax.axis_size("seq"), lax.axis_size("fsdp")
    count = ns * nf
    fast = nf == 16
    side, place = lax.axis_index("seq"), lax.axis_index("fsdp")
    tokens = incoming_state.reshape(HALF, D)
    cot = result_cotangent.reshape(HALF, D)
    stream_rows = GROUP * nf
    rows = projection_matrix_triple.shape[0]
    zero = jnp.zeros((), jnp.int32)
    core, unit = (place % 2, place // 2) if fast else (zero, zero)

    relaxed = jax.nn.sigmoid(
        (trainable_gate_scores + gate_perturbation) / softening_scale[:, None, None]
    )
    relaxed_low = relaxed.astype(BF)
    wide_cols, up_cols = D // count, FF // count
    pad_to = lambda value: jnp.pad(value, ((0, 0), (0, 128 - value.shape[1])))
    packed = jnp.concatenate(
        [
            pad_to(offset_table),
            pad_to(norm_scales),
            pad_to(widen_offset.reshape(1, up_cols)),
            jnp.zeros((7, 128), BF),
        ],
        axis=0,
    )
    lane, row = jnp.arange(D, dtype=jnp.int32)[None, :], jnp.arange(128, dtype=jnp.int32)[:, None]
    spread, group = (lane % wide_cols == row).astype(BF), lane // wide_cols
    spread_up, group_up = (lane % up_cols == row).astype(BF), lane // up_cols

    finish = jnp.cumsum(passage_extents)
    opening = finish - passage_extents
    base = place * GROUP - GROUP
    doc, pos = locate(base + jnp.arange(WINDOW, dtype=jnp.int32), opening, finish, stream_rows)
    edges = base + GROUP + jnp.asarray([0, HALF - 1, HALF, GROUP - 1], jnp.int32)
    edge_begin = jnp.max(jnp.where(opening[None, :] <= edges[:, None], opening[None, :], 0), axis=1)
    edge_end = jnp.min(
        jnp.where(finish[None, :] > edges[:, None], finish[None, :], stream_rows), axis=1
    )
    lows = jnp.clip((edge_begin - base) // CHUNK, 0, 6)
    highs = jnp.clip((edge_end - base + CHUNK - 1) // CHUNK, 0, 6)
    scal = jnp.stack(
        [unit, core, side, lows[0], highs[1], lows[2], highs[3], zero]
    ).astype(jnp.int32)
    before = shifted(tokens, "fsdp", 1)
    after = shifted(tokens, "fsdp", -1)
    other_tokens = swap(tokens, "seq", 1)
    if fast:
        halves = widen_matrix.reshape(rows, 2, FF // 2)
        keep = lax.dynamic_index_in_dim(halves, side, 1, False)
        give = lax.dynamic_index_in_dim(halves, 1 - side, 1, False)
        mine = jnp.concatenate([keep, merge_matrix], axis=1)[None]
        got = swap(jnp.concatenate([give, merge_matrix], axis=1)[None], *SIDE)
        wide = in_order(side, mine, got, 0)
        wide = jnp.concatenate(
            [wide[:, :, : FF // 2].reshape(2, rows, 2, D), wide[:, :, FF // 2 :].reshape(2, rows, 2, OWN)],
            axis=3,
        )
        mine = lax.dynamic_index_in_dim(wide, core, 2, False)
        sent = lax.dynamic_index_in_dim(wide, 1 - core, 2, False)
        wide = in_order(core, mine, swap(sent, *CORE), 1)
        shard = jnp.concatenate(
            [
                shrink_matrix,
                wide[:, :, :D].reshape(96, D),
                wide[:, :, D:].transpose(1, 0, 2).reshape(48, D),
            ],
            axis=0,
        )
        wq = own_columns(projection_matrix_triple, nf, side, place)
        pack = jnp.concatenate(
            [
                relaxed_low.reshape(6, 32, 4, 128).transpose(0, 2, 1, 3).reshape(768, 128),
                wq.reshape(48, 9, 128).transpose(1, 0, 2).reshape(432, 128),
                packed,
                jnp.zeros((32, 128), BF),
            ],
            axis=0,
        )
        gathered = lax.all_gather(pack, "fsdp", axis=0, tiled=True)
        other_tokens, before, after, scal, pos, doc = tie(
            other_tokens, before, after, scal, pos, doc
        )
        other_before = swap(before, *SIDE)
        other_after = swap(after, *SIDE)
        other_before, other_after, shard, cot = tie(other_before, other_after, shard, cot)
        wg = lax.all_gather(shard, "fsdp", axis=0, tiled=True).reshape(8, 2, 240, D)
        cot_other = swap(cot, *SIDE)
        cot_other, gathered = tie(cot_other, gathered)
        weights, table = gathered.reshape(16, 26, 48, 128), gathered.reshape(16, 39, 32, 128)
        near_owner = jnp.arange(nf, dtype=jnp.int32)[:, None]
        near = weights[:, 25, 0:16].transpose(1, 0, 2)
    else:
        other_before = swap(before, "seq", 1)
        other_after = swap(after, "seq", 1)
        full = lax.all_gather(projection_matrix_triple, BOTH, axis=0, tiled=True)
        full = lax.dynamic_index_in_dim(full.reshape(D, 3, 2, OWN), side, 2, False)
        full = full.reshape(2, 8, 48, 9, 128).transpose(1, 0, 3, 2, 4).reshape(16, 9, 48, 128)
        table = lax.all_gather(relaxed_low, "fsdp", axis=1, tiled=True)
        table = table.reshape(6, 16, 32, 4, 128).transpose(1, 0, 3, 2, 4).reshape(16, 24, 32, 128)
        weights = jnp.concatenate([table.reshape(16, 16, 48, 128), full], axis=1)
        smalls = lax.all_gather(packed[None], BOTH, axis=0, tiled=True).transpose(1, 0, 2)
        near = lax.dynamic_slice_in_dim(smalls, side * nf, nf, 1)
        near_owner = jnp.arange(nf, dtype=jnp.int32)[:, None]
        owner = jnp.arange(count, dtype=jnp.int32)[:, None]
        cot_other = swap(cot, *SIDE)
        up = lax.all_gather(widen_matrix, BOTH, axis=0, tiled=True)
        up = lax.dynamic_slice_in_dim(up, side * (FF // 2), FF // 2, 1)
        up = up.reshape(2, 8, 48, 2, D).transpose(1, 3, 0, 2, 4).reshape(8, 2, 96, D)
        down = lax.all_gather(shrink_matrix, "fsdp", axis=0, tiled=True).reshape(8, 2, 96, D)
        out = lax.all_gather(merge_matrix, BOTH, axis=0, tiled=True)
        out = out.reshape(2, 8, 48, 2, OWN).transpose(1, 3, 2, 0, 4).reshape(8, 2, 48, D)
        wg = jnp.concatenate([down, up, out], axis=2)

    pos_col, doc_col = pos.reshape(WINDOW, 1), doc.reshape(WINDOW, 1)
    pos_row, doc_row = pos.reshape(6, 1, CHUNK), doc.reshape(6, 1, CHUNK)
    pieces = (tokens, before, after, other_tokens, other_before, other_after)
    q, k, v, xw, k_turned, x_turned = project(scal, pieces, weights, near, near_owner, spread, group)
    if fast:
        far = swap(near, "seq", 1)
        smalls = jnp.concatenate([near, far], axis=1)
        owner = jnp.concatenate([side * nf + near_owner, (1 - side) * nf + near_owner], axis=0)
        q, smalls = tie(q, smalls)
    ctx, inverses, *kept = attend(scal, pos_col, pos_row, doc_col, doc_row, q, k, v, table)
    ctx_other = swap(ctx, *SIDE)
    params_of = (smalls, owner, spread, group, wg)
    up = lambda i: feed_up(
        i, scal, xw, ctx, ctx_other, smalls, owner, near, near_owner,
        (spread, group, spread_up, group_up), wg,
    )
    down = lambda i, base, got, slope: feed_back(
        i, scal, base, got, cot, cot_other, slope, *params_of
    )
    close = lambda i, base, got, unit, rstd, sums: feed_close(
        i, scal, base, got, unit, rstd, sums, *params_of
    )
    up0 = up(0)
    got0 = swap(up0[4], *SIDE)
    up1, got0 = tie(up(1), got0)
    got1 = swap(up1[4], *SIDE)
    down0, got1 = tie(down(0, up0[3], got0, up0[6]), got1)
    got0 = swap(down0[4], *SIDE)
    down1, got0 = tie(down(1, up1[3], got1, up1[6]), got0)
    got1 = swap(down1[4], *SIDE)
    closed0 = close(0, down0[3], got0, up0[0], up0[1], down0[5] + down1[5])
    feed = weight_grads(
        scal, up0[5], down0[1], up0[2], down0[2], up1[5], down1[1], up1[2], down1[2]
    )
    closed0, feed, got1 = tie(closed0, feed, got1)
    if fast:
        feed_got = swap(by_core(feed[1]), *CORE)
    closed1 = close(1, down1[3], got1, up1[0], up1[1], closed0[3])
    if fast:
        closed1, feed_got = tie(closed1, feed_got)
        feed = sum_core(feed[0], feed_got)
        feed_got = swap(feed[1], *ALONG_Y)
    dh1, dattn, dctx = [[c[i] for c in (closed0, closed1)] for i in range(3)]
    sums = closed1[3]
    lay = jnp.where(side == 0, down0[0], down1[0])
    back = lambda first, pairs, before: attend_back(
        first, pairs, before, scal, q, k_turned, v, kept, x_turned, sums, ctx, dctx, dattn, inverses
    )
    outs = back(0, 3, ())
    if fast:
        outs, feed_got = tie(outs, feed_got)
        feed = add(feed[0][:2], feed_got[:2]), add(feed[0][2:], feed_got[2:])
        outs, feed = tie(outs, feed)
    dq, own, low, high, *parts = outs

    own_cols = lambda values, at, size: lax.dynamic_slice_in_dim(values, at * size, size, 1)
    if fast:
        feed_got = swap(feed[1], "fsdp", 4)
        part_got = swap(by_core(parts[1]), *CORE)
        table_got = swap(by_core(parts[3]), *CORE)
        part_got, table_got, feed_got = tie(part_got, table_got, feed_got)
        feed = add(feed[0][0], feed_got[0]), add(feed[0][1], feed_got[1])
        part, table_part = sum_core(parts[0], part_got), sum_core(parts[2], table_got)
        part, feed = tie(part, feed)
        part_got, feed_got = swap(part[1], *ALONG_Y), swap(feed[1], "fsdp", 8)
        part_got, feed_got, table_part, low, high = tie(
            part_got, feed_got, table_part, low, high
        )
        part_got = along_z(add(part[0], part_got))
        table_got = swap(table_part[1], *ALONG_Y)
        left, right = shifted(high, "fsdp", 1), shifted(low, "fsdp", -1)
        table_got, left, right = tie(table_got, left, right)
        table_got, left, right = tie(add(table_part[0], table_got), left, right)
        table_got = along_z(table_got)
        dx, dx_send = project_back(scal, (dq, own, left, right), dh1, weights)
        dx_got = swap(dx_send, *SIDE)
        shard = add(feed[0], feed_got)
        part = sum_z(part_got)
        table_total = sum_z(table_got)
        table_total = table_total.reshape(3, 2, 4, 32, 128).transpose(0, 1, 3, 2, 4)
        table_total = table_total.reshape(6, 32, MPOS).astype(F32)
        blocks = part.reshape(3, PART, 128)
        weight = blocks[:, :PART_TOTALS].reshape(3, 3, 2, rows, 128).transpose(1, 0, 2, 3, 4)
        mine = lax.dynamic_index_in_dim(weight, side, 2, False)
        sent = lax.dynamic_index_in_dim(weight, 1 - side, 2, False)
        sums = blocks[:, PART_SUMS:PART_OUT].reshape(6, 16, 128)
        sums = sums.transpose(1, 0, 2).reshape(16, D).astype(F32)
        outs = blocks[:, PART_OUT:].reshape(6, rows, 128)
        grad_w_out = outs.transpose(1, 0, 2).reshape(rows, D).astype(F32)
        got = swap(sent.reshape(-1, 128), *SIDE)
        got = got.reshape(3, 3, rows, 128)
        mine = mine.transpose(2, 0, 1, 3).reshape(rows, 3, 1, OWN)
        got = got.transpose(2, 0, 1, 3).reshape(rows, 3, 1, OWN)
        grad_w_qkv = in_order(side, mine, got, 2).reshape(rows, 3 * D).astype(F32)
        head_sums = blocks[:, PART_TOTALS : PART_TOTALS + 2].transpose(1, 0, 2).reshape(2, OWN)
        head_sums = head_sums.astype(F32)
        head_grads = own_cols(head_sums, place, wide_cols)
        grad_w_down = shard[:96].astype(F32)
        wide = shard[96:192].reshape(2, 2, rows, D).transpose(0, 2, 1, 3).reshape(2, rows, FF // 2)
        mine = lax.dynamic_index_in_dim(wide, side, 0, False)
        got = swap(lax.dynamic_index_in_dim(wide, 1 - side, 0, False), *SIDE)
        grad_w_up = in_order(side, mine, got, 1).astype(F32)
    else:
        scatter = partial(lax.psum_scatter, axis_name=BOTH, scatter_dimension=0, tiled=True)
        left, right = shifted(high, "fsdp", 1), shifted(low, "fsdp", -1)
        dx, dx_send = project_back(scal, (dq, own, left, right), dh1, weights)
        dx_got = swap(dx_send, "seq", 1)

        def plain(pair, at=lambda u: 4 * (u & 1) + (u >> 1)):
            both = jnp.stack(pair, axis=1)
            return jnp.stack([both[at(u)] for u in range(8)], axis=0)

        blocks = plain(parts[:2]).reshape(8, 2, 3, PART, 128)
        table_grad = plain(parts[2:]).reshape(8, 2, 3, 2, 4, 32, 128).transpose(2, 3, 0, 1, 5, 4, 6)
        table_total = lax.psum_scatter(
            table_grad.reshape(6, MPOS, MPOS), "fsdp", scatter_dimension=1, tiled=True
        ).astype(F32)
        head_rows = blocks[:, :, :, :PART_TOTALS].reshape(8, 2, 3, 3, 2, 24, 128)
        head_rows = head_rows.transpose(4, 0, 1, 5, 3, 2, 6).reshape(D, 3, 1, OWN)
        blank = jnp.zeros_like(head_rows)
        both = jnp.concatenate(
            [jnp.where(side == 0, head_rows, blank), jnp.where(side == 0, blank, head_rows)], axis=2
        )
        grad_w_qkv = scatter(both.reshape(D, 3 * D)).astype(F32)
        head_sums = blocks[0, 0, :, PART_TOTALS : PART_TOTALS + 2].transpose(1, 0, 2)
        head_sums = lax.psum(head_sums.reshape(2, OWN).astype(F32), "fsdp")
        head_grads = own_cols(head_sums, place, wide_cols)
        def placed(value, axis):
            blank = jnp.zeros_like(value)
            sides = [jnp.where(side == 0, value, blank), jnp.where(side == 0, blank, value)]
            return jnp.concatenate(sides, axis=axis)

        gg = plain(feed, lambda u: 4 * (u & 1) + (u & 2) + (u >> 2)).reshape(16, 192, D)
        grad_w_down = scatter(placed(gg[:, :96].reshape(FF // 2, D), 0)).astype(F32)
        up = gg[:, 96:192].reshape(16, 2, 2, 24, D).transpose(1, 0, 3, 2, 4).reshape(D, FF // 2)
        grad_w_up = scatter(placed(up, 1)).astype(F32)
        out = blocks[:, :, :, PART_OUT:].reshape(8, 2, 3, 2, 24, 128).transpose(0, 1, 4, 2, 3, 5)
        out = out.reshape(OWN, D)
        grad_w_out = scatter(placed(out, 0)).astype(F32)
        sums = lax.psum(sums, "fsdp")
    ours = own_cols(sums[:6], side * nf + place, wide_cols)
    grad_biases = jnp.concatenate([head_grads, ours[:4]], axis=0)
    grad_gains = ours[4:]
    grad_bias_up = lax.dynamic_slice_in_dim(
        sums[8:10].reshape(-1), place * up_cols, up_cols, 0
    )
    input_grad = dx + dx_got.astype(F32)
    mask_logit_gradient = (
        table_total * relaxed * (1.0 - relaxed) / softening_scale[:, None, None]
    )
    return (
        lay.reshape(1, HALF, D),
        input_grad.reshape(1, HALF, D),
        grad_w_qkv,
        grad_w_out,
        grad_w_up,
        grad_w_down,
        grad_biases,
        grad_gains,
        grad_bias_up,
        mask_logit_gradient,
    )


def solution(mesh):
    rows = P(("seq", "fsdp"), None)
    columns = P(None, ("seq", "fsdp"))
    block = P("fsdp", "seq", None)
    table = P("seq", "fsdp", None)
    return jax.shard_map(
        per_device,
        mesh=mesh,
        in_specs=(
            block, rows, rows, rows, rows, columns, columns, P(("seq", "fsdp")),
            table, table, P("seq"), P(), block,
        ),
        out_specs=(
            block, block, rows, rows, rows, rows, columns, columns, P(("seq", "fsdp")), table,
        ),
        check_vma=False,
    )
```

profile of v0, /device:TPU:1, one launch (start us, length us, event | category | flops | bytes accessed | tf_op | source)
XLA Modules:
  0.0 337.9 jit_solution(17223846898663329278)
XLA Ops:
  7.3 0.9 reshape.390
  8.9 1.3 collective-permute-start.8
  10.2 4.5 %collective-permute-start.10 = (bf16[24,1152]{1,0:T(8,128)(2,1)S(1)}, bf16[24,1152]{1,0:T(8,128)(2,1)S(1)}, u32[]{:S(2)}, u32[]{:S(2)}) collective-permute-start(bf16[24,1152]{1,0:T(8,128)(2,1)S(1)} %bitcast.155), channel_id=1, source_target_pairs={{1,16},{3,18},{5,20},{7,22},{9,24},{11,26},{13,28},{15,30},{16,1},... | collective-permute-start | bytes 165896 | tf_op jit(solution)/shard_map/ppermute | solution.py:914
  14.8 1.7 collective-permute-start.9
  16.4 2.1 fusion.28
  18.9 3.2 concatenate.46
  22.3 3.1 collective-permute-start.1
  25.4 1.9 collective-permute-start.2
  27.8 1.1 collective-permute-start.5
  30.3 5.5 %collective-permute-done.5 = bf16[1,24,2304]{2,1,0:T(8,128)(2,1)S(1)} collective-permute-done((bf16[1,24,2304]{2,1,0:T(8,128)(2,1)S(1)}, bf16[1,24,2304]{2,1,0:T(8,128)(2,1)S(1)}, u32[]{:S(2)}, u32[]{:S(2)}) %collective-permute-start.5) | collective-permute-done | bytes 110624 | tf_op jit(solution)/shard_map/ppermute | solution.py:843
  37.4 3.2 stack.15.scal
  41.0 1.1 collective-permute-start.4
  43.1 8.0 %collective-permute-done.3.y0 = bf16[256,768]{1,0:T(8,128)(2,1)S(1)} collective-permute-done((bf16[256,768]{1,0:T(8,128)(2,1)S(1)}, bf16[256,768]{1,0:T(8,128)(2,1)S(1)}, u32[]{:S(2)}, u32[]{:S(2)}) %collective-permute-start.3) | collective-permute-done | bytes 393248 | tf_op jit(solution)/shard_map/ppermute | solution.py:843
  51.0 8.5 %collective-permute-done.4.y2 = bf16[256,768]{1,0:T(8,128)(2,1)S(1)} collective-permute-done((bf16[256,768]{1,0:T(8,128)(2,1)S(1)}, bf16[256,768]{1,0:T(8,128)(2,1)S(1)}, u32[]{:S(2)}, u32[]{:S(2)}) %collective-permute-start.4) | collective-permute-done | bytes 393248 | tf_op jit(solution)/shard_map/ppermute | solution.py:843
  62.3 1.1 reshape.428.pos_col
  64.1 1.2 reshape.429.doc_col
  65.8 4.5 %collective-permute-done.7.cot_other = bf16[256,768]{1,0:T(8,128)(2,1)S(1)} collective-permute-done((bf16[256,768]{1,0:T(8,128)(2,1)S(1)}, bf16[256,768]{1,0:T(8,128)(2,1)S(1)}, u32[]{:S(2)}, u32[]{:S(2)}) %collective-permute-start.7) | collective-permute-done | bytes 393248 | tf_op jit(solution)/shard_map/ppermute | solution.py:843
  70.3 8.9 %all-gather.3.cloned.1.call-done = bf16[19968,128]{1,0:T(8,128)(2,1)} async-done(((bf16[1248,128]{1,0:T(8,128)(2,1)}), bf16[19968,128]{1,0:T(8,128)(2,1)}) %all-gather.3.cloned.1.call-update) | async-done | bytes 5111824 | tf_op jit(solution)/shard_map/all_gather | solution.py:1013
  79.2 0.8 slice_bitcast_fusion
  80.7 1.2 collective-permute-start.11
  82.5 8.8 %project.1 = (bf16[512,384]{1,0:T(8,128)(2,1)}, bf16[1536,384]{1,0:T(8,128)(2,1)}, bf16[1536,384]{1,0:T(8,128)(2,1)}, bf16[1536,768]{1,0:T(8,128)(2,1)}, bf16[6,...) custom-call(s32[8]{0:T(128)} %stack.15.scal, bf16[256,768]{1,0:T(8,128)(2,1)} %bitcast.169, bf16[256,768]{1,0:T(8,128)(2,1)} %copy-done.18, ...), custom_call_target="tpu_custom_call" | custom-call | flops 10350000128 | bytes 1000 | tf_op jit(solution)/shard_map/project/pallas_call | solution.py:596
  91.4 27.9 %attend.1 = (bf16[2,256,384]{2,1,0:T(8,128)(2,1)}, f32[3,8,512]{2,1,0:T(8,128)}, bf16[3,2,6,256,512]{4,3,2,1,0:T(8,128)(2,1)}, bf16[3,2,6,256,512]{4,3,2,1,0:T(8,128)(2,1)}, bf16[6,512,256]{2,1,0:T(8,128)(2,1)}) custom-call(s32[8]{0:T(128)} %stack.15.scal, s32[1536,1]{1,0:T(8,128)} %reshape.428.pos_col, s32[6,1,256]{2,1,0:T(1,128)} %reshape.398.pos_row, ...), custom_call_target="tpu_custom_call" | custom-call | flops 29899999232 | bytes 1000 | tf_op jit(solution)/shard_map/attend/pallas_call | solution.py:623
  121.9 6.9 %collective-permute-done.12.ctx_other = bf16[2,256,384]{2,1,0:T(8,128)(2,1)S(1)} collective-permute-done((bf16[2,256,384]{2,1,0:T(8,128)(2,1)}, bf16[2,256,384]{2,1,0:T(8,128)(2,1)S(1)}, u32[]{:S(2)}, u32[]{:S(2)}) %collective-permute-start.12) | collective-permute-done | bytes 393248 | tf_op jit(solution)/shard_map/ppermute | solution.py:843
  128.9 10.7 %all-gather.5.cloned.1.call-done = bf16[3840,768]{1,0:T(8,128)(2,1)} async-done(((bf16[240,768]{1,0:T(8,128)(2,1)}), bf16[3840,768]{1,0:T(8,128)(2,1)}) %all-gather.5.cloned.1.call-update) | async-done | bytes 5898256 | tf_op jit(solution)/shard_map/all_gather | solution.py:1020
  140.2 7.0 %feed_up_0.1 = (f32[256,768]{1,0:T(8,128)}, f32[256,128]{1,0:T(8,128)}, bf16[256,768]{1,0:T(8,128)(2,1)}, f32[256,768]{1,0:T(8,128)}, bf16[256,768]{1,0:T(8,128)...) custom-call(s32[8]{0:T(128)} %stack.15.scal, bf16[1536,768]{1,0:T(8,128)(2,1)} %get-tuple-element.161.x, ...), custom_call_target="tpu_custom_call" | custom-call | flops 9200000000 | bytes 1000 | tf_op jit(solution)/shard_map/feed_up_0/pallas_call | solution.py:748
  147.2 1.3 collective-permute-start.13
  149.1 7.0 %feed_up_1.1 = (f32[256,768]{1,0:T(8,128)}, f32[256,128]{1,0:T(8,128)}, bf16[256,768]{1,0:T(8,128)(2,1)}, f32[256,768]{1,0:T(8,128)}, bf16[256,768]{1,0:T(8,128)...) custom-call(s32[8]{0:T(128)} %stack.15.scal, bf16[1536,768]{1,0:T(8,128)(2,1)} %get-tuple-element.161.x, ...), custom_call_target="tpu_custom_call" | custom-call | flops 9200000000 | bytes 1000 | tf_op jit(solution)/shard_map/feed_up_1/pallas_call | solution.py:748
  156.1 1.8 collective-permute-done.13.got
  158.0 1.3 collective-permute-start.14
  159.2 7.5 %feed_back_0.1 = (bf16[256,768]{1,0:T(8,128)(2,1)}, bf16[256,768]{1,0:T(8,128)(2,1)}, bf16[2,256,768]{2,1,0:T(8,128)(2,1)}, f32[256,768]{1,0:T(8,128)}, bf16[256,768]{1,0:T(8,128)(2,1)}, /*index=5*/f32[16,768]{1,0:T(8,128)}) custom-call(s32[8]{0:T(128)} %stack.15.scal, f32[256,768]{1,0:T(8,128)} %get-tuple-element.171.base, bf16[256,768]{1,0:T(8,128)(2,1)} %copy-done.26, ...), custom_call_target="tpu_custom_call" | custom-call | flops 8049999872 | bytes 1000 | tf_op jit(solution)/shard_map/feed_back_0/pallas_call | solution.py:771
  166.7 1.0 collective-permute-done.14.got
  167.7 1.3 collective-permute-start.15
  169.0 7.7 %feed_back_1.1 = (bf16[256,768]{1,0:T(8,128)(2,1)}, bf16[256,768]{1,0:T(8,128)(2,1)}, bf16[2,256,768]{2,1,0:T(8,128)(2,1)}, f32[256,768]{1,0:T(8,128)}, bf16[256,768]{1,0:T(8,128)(2,1)}, /*index=5*/f32[16,768]{1,0:T(8,128)}) custom-call(s32[8]{0:T(128)} %stack.15.scal, f32[256,768]{1,0:T(8,128)} %get-tuple-element.191.base, bf16[256,768]{1,0:T(8,128)(2,1)} %copy-done.27, ...), custom_call_target="tpu_custom_call" | custom-call | flops 8049999872 | bytes 1000 | tf_op jit(solution)/shard_map/feed_back_1/pallas_call | solution.py:771
  176.7 1.1 collective-permute-start.16
  177.8 1.4 add.232.sums_in
  179.2 7.4 %weight_grads.1 = (bf16[8,192,768]{2,1,0:T(8,128)(2,1)}, bf16[8,192,768]{2,1,0:T(8,128)(2,1)}) custom-call(s32[8]{0:T(128)} %stack.15.scal, bf16[2,256,768]{2,1,0:T(8,128)(2,1)} %get-tuple-element.218.act0, bf16[256,768]{1,0:T(8,128)(2,1)} %get-tuple-element.219.ddown0, bf16[256,768]{1,0:T(8,128)(2,1)} %get-tuple-element.220.nlow0, ...), custom_call_target="tpu_custom_call" | custom-call | flops 8049999872 | bytes 1000 | tf_op jit(solution)/shard_map/weight_grads/pallas_call | solution.py:809
  186.7 4.0 %feed_close_0.1 = (f32[256,768]{1,0:T(8,128)}, bf16[256,768]{1,0:T(8,128)(2,1)}, bf16[256,384]{1,0:T(8,128)(2,1)}, f32[16,768]{1,0:T(8,128)}) custom-call(s32[8]{0:T(128)} %stack.15.scal, f32[256,768]{1,0:T(8,128)} %get-tuple-element.208.base, bf16[256,768]{1,0:T(8,128)(2,1)} %copy-done.25, f32[256,768]{1,0:T(8,128)} %get-tuple-element.210.unit1, ...), custom_call_target="tpu_custom_call" | custom-call | flops 4600000000 | bytes 1000 | tf_op jit(solution)/shard_map/feed_close_0/pallas_call | solution.py:791
  190.8 3.2 collective-permute-start.17
  194.0 4.2 %feed_close_1.1 = (f32[256,768]{1,0:T(8,128)}, bf16[256,768]{1,0:T(8,128)(2,1)}, bf16[256,384]{1,0:T(8,128)(2,1)}, f32[16,768]{1,0:T(8,128)}) custom-call(s32[8]{0:T(128)} %stack.15.scal, f32[256,768]{1,0:T(8,128)} %get-tuple-element.207.base, bf16[256,768]{1,0:T(8,128)(2,1)} %copy-done.23, f32[256,768]{1,0:T(8,128)} %get-tuple-element.230.unit1, ...), custom_call_target="tpu_custom_call" | custom-call | flops 4600000000 | bytes 1000 | tf_op jit(solution)/shard_map/feed_close_1/pallas_call | solution.py:791
  198.5 3.3 fusion
  202.0 27.4 %attend_back_0.1 = (bf16[512,384]{1,0:T(8,128)(2,1)}, f32[2,512,384]{2,1,0:T(8,128)}, bf16[2,512,384]{2,1,0:T(8,128)(2,1)}, bf16[2,512,384]{2,1,0:T(8,128)(2,1)}...) custom-call(s32[8]{0:T(128)} %stack.15.scal, ...), custom_call_target="tpu_custom_call" | custom-call | flops 34500001792 | bytes 1000 | tf_op jit(solution)/shard_map/attend_back_0/pallas_call | solution.py:671
  229.7 1.1 copy-done.14
  230.8 0.9 collective-permute-start.20
  231.8 2.8 collective-permute-start.21
  234.6 13.2 %collective-permute-done.21 = bf16[2,192,768]{2,1,0:T(8,128)(2,1)S(1)} collective-permute-done((bf16[2,192,768]{2,1,0:T(8,128)(2,1)S(1)}, bf16[2,192,768]{2,1,0:T(8,128)(2,1)S(1)}, u32[]{:S(2)}, u32[]{:S(2)}) %collective-permute-start.21) | collective-permute-done | bytes 589856 | tf_op jit(solution)/shard_map/ppermute | solution.py:843
  247.9 1.3 fusion.4
  249.1 0.9 fusion.9
  250.8 2.9 collective-permute-start.23
  253.7 2.8 fusion.2
  256.5 10.9 %collective-permute-done.23 = bf16[192,768]{1,0:T(8,128)(2,1)S(1)} collective-permute-done((bf16[192,768]{1,0:T(8,128)(2,1)}, bf16[192,768]{1,0:T(8,128)(2,1)S(1)}, u32[]{:S(2)}, u32[]{:S(2)}) %collective-permute-start.23) | collective-permute-done | bytes 294944 | tf_op jit(solution)/shard_map/ppermute | solution.py:843
  267.7 5.0 %collective-permute-start.25 = (bf16[2,512,384]{2,1,0:T(8,128)(2,1)}, bf16[2,512,384]{2,1,0:T(8,128)(2,1)}, u32[]{:S(2)}, u32[]{:S(2)}) collective-permute-start(bf16[2,512,384]{2,1,0:T(8,128)(2,1)} %get-tuple-element.280), channel_id=1, source_target_pairs={{0,1},{1,2},{2,3},{3,4},{4,5},{5,6},{6,7},{7,8},{8,9},{9,10},{10,1... | collective-permute-start | bytes 2359304 | tf_op jit(solution)/shard_map/ppermute | solution.py:849
  272.8 2.2 collective-permute-start.26
  276.3 2.2 add_convert_fusion.1
  278.5 3.5 %all-to-all-start = ((bf16[4,720,128]{2,1,0:T(8,128)(2,1)}), bf16[4,720,128]{2,1,0:T(8,128)(2,1)S(1)}, u32[]{:S(2)}, u32[]{:S(2)}) async-start(bf16[4,720,128]{2,1,0:T(8,128)(2,1)} %add_convert_fusion.1), calls=%async_computation | async-start | bytes 1474560 | tf_op jit(solution)/shard_map/all_to_all | solution.py:861
  282.8 9.0 %collective-permute-done.24 = bf16[4,768,128]{2,1,0:T(8,128)(2,1)S(1)} collective-permute-done((bf16[4,768,128]{2,1,0:T(8,128)(2,1)}, bf16[4,768,128]{2,1,0:T(8,128)(2,1)S(1)}, u32[]{:S(2)}, u32[]{:S(2)}) %collective-permute-start.24) | collective-permute-done | bytes 786464 | tf_op jit(solution)/shard_map/ppermute | solution.py:843
  291.8 10.5 %collective-permute-done.25.refs_2_ = bf16[2,512,384]{2,1,0:T(8,128)(2,1)} collective-permute-done((bf16[2,512,384]{2,1,0:T(8,128)(2,1)}, bf16[2,512,384]{2,1,0:T(8,128)(2,1)}, u32[]{:S(2)}, u32[]{:S(2)}) %collective-permute-start.25) | collective-permute-done | bytes 786464 | tf_op jit(solution)/shard_map/ppermute | solution.py:849
  302.2 1.1 add_convert_fusion
  303.4 6.3 %project_back.1 = (f32[256,768]{1,0:T(8,128)}, bf16[256,768]{1,0:T(8,128)(2,1)}) custom-call(s32[8]{0:T(128)} %stack.15.scal, bf16[512,384]{1,0:T(8,128)(2,1)} %get-tuple-element.263.refs_0_, f32[2,512,384]{2,1,0:T(8,128)} %get-tuple-element.264.refs_1_, bf16[2,512,384]{2,1,0:T(8,128)(2,1)} %collective-permute-done.25.refs_2_, ...), custom_call_target="tpu_custom_call" | custom-call | flops 6899999744 | bytes 1000 | tf_op jit(solution)/shard_map/project_back/pallas_call | solution.py:825
  310.0 4.3 %all-to-all-start.1 = ((bf16[4,768,128]{2,1,0:T(8,128)(2,1)}), bf16[4,768,128]{2,1,0:T(8,128)(2,1)S(1)}, u32[]{:S(2)}, u32[]{:S(2)}) async-start(bf16[4,768,128]{2,1,0:T(8,128)(2,1)} %add_convert_fusion), calls=%async_computation.1 | async-start | bytes 1572864 | tf_op jit(solution)/shard_map/all_to_all | solution.py:861
  314.6 1.2 collective-permute-start.28
  318.7 0.9 reshape.421
  319.6 0.9 add_bitcast_fusion
  320.5 9.0 %all-to-all-done.1 = bf16[4,768,128]{2,1,0:T(8,128)(2,1)S(1)} async-done(((bf16[4,768,128]{2,1,0:T(8,128)(2,1)}), bf16[4,768,128]{2,1,0:T(8,128)(2,1)S(1)}, u32[]{:S(2)}, u32[]{:S(2)}) %all-to-all-start.1) | async-done | bytes 786464 | tf_op jit(solution)/shard_map/all_to_all | solution.py:861
  330.2 0.9 multiply_divide_fusion
  (197 shorter events, 22.8 us)
Async XLA Ops:
  7.2 11.4 %copy-start.12 = (bf16[6,24]{1,0:T(8,128)(2,1)S(1)}, bf16[6,24]{1,0:T(8,128)(2,1)}, u32[]{:S(2)}) copy-start(bf16[6,24]{1,0:T(8,128)(2,1)} %param.19) | copy-start | bytes 868
  7.2 11.5 %copy-start.28 = (bf16[2,24]{1,0:T(2,128)(2,1)S(1)}, bf16[2,24]{1,0:T(2,128)(2,1)}, u32[]{:S(2)}) copy-start(bf16[2,24]{1,0:T(2,128)(2,1)} %param.20) | copy-start | bytes 292
  7.2 11.5 %copy-start.29 = (bf16[96]{0:T(256)(128)(2,1)S(1)}, bf16[96]{0:T(256)(128)(2,1)}, u32[]{:S(2)}) copy-start(bf16[96]{0:T(256)(128)(2,1)} %param.21) | copy-start | bytes 580
  7.2 72.0 %all-gather.3.cloned.1.call-start = ((), (), s32[]{:S(2)}) async-start(), calls=%async_computation.2 | async-start | bytes 5431296 | tf_op jit(solution)/shard_map/all_gather | solution.py:1013
  8.9 9.8 %collective-permute-start.8 = (bf16[24,1152]{1,0:T(8,128)(2,1)S(1)}, bf16[24,1152]{1,0:T(8,128)(2,1)S(1)}, u32[]{:S(2)}, u32[]{:S(2)}) collective-permute-start(bf16[24,1152]{1,0:T(8,128)(2,1)S(1)} %bitcast.154), channel_id=1, source_target_pairs={{0,16},{2,18},{4,20},{6,22},{8,24},{10,26},{12,28},{14,30},{17,1},... | collective-permute-start | bytes 165896 | tf_op jit(solution)/shard_map/ppermute | solution.py:913
  10.2 8.5 %collective-permute-start.10 = (bf16[24,1152]{1,0:T(8,128)(2,1)S(1)}, bf16[24,1152]{1,0:T(8,128)(2,1)S(1)}, u32[]{:S(2)}, u32[]{:S(2)}) collective-permute-start(bf16[24,1152]{1,0:T(8,128)(2,1)S(1)} %bitcast.155), channel_id=1, source_target_pairs={{1,16},{3,18},{5,20},{7,22},{9,24},{11,26},{13,28},{15,30},{16,1},... | collective-permute-start | bytes 165896 | tf_op jit(solution)/shard_map/ppermute | solution.py:914
  14.8 4.0 %collective-permute-start.9 = (bf16[24,1152]{1,0:T(8,128)(2,1)S(1)}, bf16[24,1152]{1,0:T(8,128)(2,1)S(1)}, u32[]{:S(2)}, u32[]{:S(2)}) collective-permute-start(bf16[24,1152]{1,0:T(8,128)(2,1)S(1)} %bitcast.147), channel_id=1, source_target_pairs={{1,0},{3,2},{5,4},{7,6},{9,8},{11,10},{13,12},{15,14},{16,17},{18,... | collective-permute-start | bytes 165896 | tf_op jit(solution)/shard_map/ppermute | solution.py:914
  18.5 3.7 %copy-start.15 = (bf16[1,256,768]{2,1,0:T(8,128)(2,1)S(1)}, bf16[1,256,768]{2,1,0:T(8,128)(2,1)}, u32[]{:S(2)}) copy-start(bf16[1,256,768]{2,1,0:T(8,128)(2,1)} %param.14) | copy-start | bytes 1179652
  18.5 8.8 %copy-start.7 = (bf16[24,3072]{1,0:T(8,128)(2,1)S(1)}, bf16[24,3072]{1,0:T(8,128)(2,1)}, u32[]{:S(2)}) copy-start(bf16[24,3072]{1,0:T(8,128)(2,1)} %param.17) | copy-start | bytes 442372
  18.7 9.1 %copy-start.8 = (bf16[24,768]{1,0:T(8,128)(2,1)S(1)}, bf16[24,768]{1,0:T(8,128)(2,1)}, u32[]{:S(2)}) copy-start(bf16[24,768]{1,0:T(8,128)(2,1)} %param.16) | copy-start | bytes 110596
  18.8 10.2 %copy-start.13 = (s32[32]{0:T(128)S(1)}, s32[32]{0:T(128)}, u32[]{:S(2)}) copy-start(s32[32]{0:T(128)} %param.25) | copy-start | bytes 388
  18.8 10.5 %copy-start.30 = (s32[4]{0:T(128)S(1)}, s32[4]{0:T(128)}, u32[]{:S(2)}) copy-start(s32[4]{0:T(128)} %constant.175.clone) | copy-start | bytes 52
  22.2 117.4 %all-gather.5.cloned.1.call-start = ((), (), s32[]{:S(2)}) async-start(), calls=%async_computation.3 | async-start | bytes 6266880 | tf_op jit(solution)/shard_map/all_gather | solution.py:1020
  22.3 18.3 %collective-permute-start = (bf16[256,768]{1,0:T(8,128)(2,1)S(1)}, bf16[256,768]{1,0:T(8,128)(2,1)S(1)}, u32[]{:S(2)}, u32[]{:S(2)}) collective-permute-start(bf16[256,768]{1,0:T(8,128)(2,1)S(1)} %bitcast.170), channel_id=1, source_target_pairs={{0,16},{16,0},{1,17},{17,1},{2,18},{18,2},{3,19},{19,3},{4,20},{20... | collective-permute-start | bytes 1179656 | tf_op jit(solution)/shard_map/ppermute | solution.py:843
  22.3 18.3 %collective-permute-start.1 = (bf16[256,768]{1,0:T(8,128)(2,1)S(1)}, bf16[256,768]{1,0:T(8,128)(2,1)S(1)}, u32[]{:S(2)}, u32[]{:S(2)}) collective-permute-start(bf16[256,768]{1,0:T(8,128)(2,1)S(1)} %bitcast.171), channel_id=1, source_target_pairs={{0,1},{1,2},{2,3},{3,4},{4,5},{5,6},{6,7},{7,8},{8,9},{9,10},{10,1... | collective-permute-start | bytes 1179656 | tf_op jit(solution)/shard_map/ppermute | solution.py:849
  25.4 15.2 %collective-permute-start.2 = (bf16[256,768]{1,0:T(8,128)(2,1)S(1)}, bf16[256,768]{1,0:T(8,128)(2,1)S(1)}, u32[]{:S(2)}, u32[]{:S(2)}) collective-permute-start(bf16[256,768]{1,0:T(8,128)(2,1)S(1)} %bitcast.172), channel_id=1, source_target_pairs={{1,0},{2,1},{3,2},{4,3},{5,4},{6,5},{7,6},{8,7},{9,8},{10,9},{11,1... | collective-permute-start | bytes 1179656 | tf_op jit(solution)/shard_map/ppermute | solution.py:849
  27.8 7.9 %collective-permute-start.5 = (bf16[1,24,2304]{2,1,0:T(8,128)(2,1)S(1)}, bf16[1,24,2304]{2,1,0:T(8,128)(2,1)S(1)}, u32[]{:S(2)}, u32[]{:S(2)}) collective-permute-start(bf16[1,24,2304]{2,1,0:T(8,128)(2,1)S(1)} %fusion.13), channel_id=1, source_target_pairs={{0,16},{16,0},{1,17},{17,1},{2,18},{18,2},{3,19},{19,3},{4,20},{20... | collective-permute-start | bytes 331784 | tf_op jit(solution)/shard_map/ppermute | solution.py:843
  35.9 6.4 %copy-start.9 = (bf16[96,768]{1,0:T(8,128)(2,1)S(1)}, bf16[96,768]{1,0:T(8,128)(2,1)}, u32[]{:S(2)}) copy-start(bf16[96,768]{1,0:T(8,128)(2,1)} %param.18) | copy-start | bytes 442372
  36.6 24.2 %copy-start.16 = (bf16[1,256,768]{2,1,0:T(8,128)(2,1)S(1)}, bf16[1,256,768]{2,1,0:T(8,128)(2,1)}, u32[]{:S(2)}) copy-start(bf16[1,256,768]{2,1,0:T(8,128)(2,1)} %param.26) | copy-start | bytes 1179652
  36.6 5.5 %collective-permute-start.6 = (bf16[2,24,1152]{2,1,0:T(8,128)(2,1)S(1)}, bf16[2,24,1152]{2,1,0:T(8,128)(2,1)S(1)}, u32[]{:S(2)}, u32[]{:S(2)}) collective-permute-start(bf16[2,24,1152]{2,1,0:T(8,128)(2,1)S(1)} %bitcast.150), channel_id=1, source_target_pairs={{0,1},{1,0},{2,3},{3,2},{4,5},{5,4},{6,7},{7,6},{8,9},{9,8},{10,11... | collective-permute-start | bytes 331784 | tf_op jit(solution)/shard_map/ppermute | solution.py:843
  40.6 22.8 %copy-start.17 = (bf16[256,768]{1,0:T(8,128)(2,1)}, bf16[256,768]{1,0:T(8,128)(2,1)S(1)}, u32[]{:S(2)}) copy-start(bf16[256,768]{1,0:T(8,128)(2,1)S(1)} %collective-permute-done.y1) | copy-start | bytes 1179652
  40.6 22.8 %copy-start.18 = (bf16[256,768]{1,0:T(8,128)(2,1)}, bf16[256,768]{1,0:T(8,128)(2,1)S(1)}, u32[]{:S(2)}) copy-start(bf16[256,768]{1,0:T(8,128)(2,1)S(1)} %collective-permute-done.1.x0) | copy-start | bytes 1179652
  40.6 22.8 %copy-start.19 = (bf16[256,768]{1,0:T(8,128)(2,1)}, bf16[256,768]{1,0:T(8,128)(2,1)S(1)}, u32[]{:S(2)}) copy-start(bf16[256,768]{1,0:T(8,128)(2,1)S(1)} %collective-permute-done.2.x2) | copy-start | bytes 1179652
  40.6 10.4 %collective-permute-start.3 = (bf16[256,768]{1,0:T(8,128)(2,1)S(1)}, bf16[256,768]{1,0:T(8,128)(2,1)S(1)}, u32[]{:S(2)}, u32[]{:S(2)}) collective-permute-start(bf16[256,768]{1,0:T(8,128)(2,1)S(1)} %collective-permute-done.1.x0), channel_id=1, source_target_pairs={{0,16},{16,0},{1,17},{17,1},{2,18},{18,2},{3,19},{19,3},{4,20},{20... | collective-permute-start | bytes 1179656 | tf_op jit(solution)/shard_map/ppermute | solution.py:843
  41.0 18.5 %collective-permute-start.4 = (bf16[256,768]{1,0:T(8,128)(2,1)S(1)}, bf16[256,768]{1,0:T(8,128)(2,1)S(1)}, u32[]{:S(2)}, u32[]{:S(2)}) collective-permute-start(bf16[256,768]{1,0:T(8,128)(2,1)S(1)} %collective-permute-done.2.x2), channel_id=1, source_target_pairs={{0,16},{16,0},{1,17},{17,1},{2,18},{18,2},{3,19},{19,3},{4,20},{20... | collective-permute-start | bytes 1179656 | tf_op jit(solution)/shard_map/ppermute | solution.py:843
  51.0 31.5 %copy-start.21 = (bf16[256,768]{1,0:T(8,128)(2,1)}, bf16[256,768]{1,0:T(8,128)(2,1)S(1)}, u32[]{:S(2)}) copy-start(bf16[256,768]{1,0:T(8,128)(2,1)S(1)} %collective-permute-done.3.y0) | copy-start | bytes 1179652
  59.6 23.0 %copy-start.22 = (bf16[256,768]{1,0:T(8,128)(2,1)}, bf16[256,768]{1,0:T(8,128)(2,1)S(1)}, u32[]{:S(2)}) copy-start(bf16[256,768]{1,0:T(8,128)(2,1)S(1)} %collective-permute-done.4.y2) | copy-start | bytes 1179652
  60.8 9.5 %collective-permute-start.7 = (bf16[256,768]{1,0:T(8,128)(2,1)S(1)}, bf16[256,768]{1,0:T(8,128)(2,1)S(1)}, u32[]{:S(2)}, u32[]{:S(2)}) collective-permute-start(bf16[256,768]{1,0:T(8,128)(2,1)S(1)} %bitcast.175), channel_id=1, source_target_pairs={{0,16},{16,0},{1,17},{17,1},{2,18},{18,2},{3,19},{19,3},{4,20},{20... | collective-permute-start | bytes 1179656 | tf_op jit(solution)/shard_map/ppermute | solution.py:843
  70.3 21.0 %copy-start.20 = (bf16[256,768]{1,0:T(8,128)(2,1)}, bf16[256,768]{1,0:T(8,128)(2,1)S(1)}, u32[]{:S(2)}) copy-start(bf16[256,768]{1,0:T(8,128)(2,1)S(1)} %collective-permute-done.7.cot_other) | copy-start | bytes 1179652
  80.7 10.7 %collective-permute-start.11 = (bf16[16,16,128]{2,0,1:T(8,128)(2,1)S(1)}, bf16[16,16,128]{2,0,1:T(8,128)(2,1)S(1)}, u32[]{:S(2)}, u32[]{:S(2)}) collective-permute-start(bf16[16,16,128]{2,0,1:T(8,128)(2,1)S(1)} %slice_bitcast_fusion), channel_id=1, source_target_pairs={{0,16},{16,0},{1,17},{17,1},{2,18},{18,2},{3,19},{19,3},{4,20},{20... | collective-permute-start | bytes 196616 | tf_op jit(solution)/shard_map/ppermute | solution.py:843
  119.4 9.5 %collective-permute-start.12 = (bf16[2,256,384]{2,1,0:T(8,128)(2,1)}, bf16[2,256,384]{2,1,0:T(8,128)(2,1)S(1)}, u32[]{:S(2)}, u32[]{:S(2)}) collective-permute-start(bf16[2,256,384]{2,1,0:T(8,128)(2,1)} %get-tuple-element.168.ctx_mine.ctx.ctx_all), channel_id=1, source_target_pairs={{0,16},{16,0},{1,17},{17,1},{2,18},{18,2},{3,19},{19,3},{4,20},{20... | collective-permute-start | bytes 1179656 | tf_op jit(solution)/shard_map/ppermute | solution.py:843
  128.9 11.3 %copy-start.24 = (bf16[2,256,384]{2,1,0:T(8,128)(2,1)}, bf16[2,256,384]{2,1,0:T(8,128)(2,1)S(1)}, u32[]{:S(2)}) copy-start(bf16[2,256,384]{2,1,0:T(8,128)(2,1)S(1)} %collective-permute-done.12.ctx_other) | copy-start | bytes 1179652
  147.2 10.7 %collective-permute-start.13 = (bf16[256,768]{1,0:T(8,128)(2,1)}, bf16[256,768]{1,0:T(8,128)(2,1)S(1)}, u32[]{:S(2)}, u32[]{:S(2)}) collective-permute-start(bf16[256,768]{1,0:T(8,128)(2,1)} %get-tuple-element.179), channel_id=1, source_target_pairs={{0,16},{16,0},{1,17},{17,1},{2,18},{18,2},{3,19},{19,3},{4,20},{20... | collective-permute-start | bytes 1179656 | tf_op jit(solution)/shard_map/ppermute | solution.py:843
  158.0 9.8 %collective-permute-start.14 = (bf16[256,768]{1,0:T(8,128)(2,1)}, bf16[256,768]{1,0:T(8,128)(2,1)S(1)}, u32[]{:S(2)}, u32[]{:S(2)}) collective-permute-start(bf16[256,768]{1,0:T(8,128)(2,1)} %get-tuple-element.189), channel_id=1, source_target_pairs={{0,16},{16,0},{1,17},{17,1},{2,18},{18,2},{3,19},{19,3},{4,20},{20... | collective-permute-start | bytes 1179656 | tf_op jit(solution)/shard_map/ppermute | solution.py:843
  167.7 1.3 copy-start.27
  167.7 10.1 %copy-start.10 = (f32[16,768]{1,0:T(8,128)S(1)}, f32[16,768]{1,0:T(8,128)}, u32[]{:S(2)}) copy-start(f32[16,768]{1,0:T(8,128)} %get-tuple-element.212) | copy-start | bytes 147460
  167.7 8.9 %collective-permute-start.15 = (bf16[256,768]{1,0:T(8,128)(2,1)}, bf16[256,768]{1,0:T(8,128)(2,1)S(1)}, u32[]{:S(2)}, u32[]{:S(2)}) collective-permute-start(bf16[256,768]{1,0:T(8,128)(2,1)} %get-tuple-element.200), channel_id=1, source_target_pairs={{0,16},{16,0},{1,17},{17,1},{2,18},{18,2},{3,19},{19,3},{4,20},{20... | collective-permute-start | bytes 1179656 | tf_op jit(solution)/shard_map/ppermute | solution.py:843
  176.7 10.0 %copy-start.25 = (bf16[256,768]{1,0:T(8,128)(2,1)}, bf16[256,768]{1,0:T(8,128)(2,1)S(1)}, u32[]{:S(2)}) copy-start(bf16[256,768]{1,0:T(8,128)(2,1)S(1)} %collective-permute-done.15.got) | copy-start | bytes 1179652
  176.7 14.0 %collective-permute-start.16 = (bf16[256,768]{1,0:T(8,128)(2,1)}, bf16[256,768]{1,0:T(8,128)(2,1)S(1)}, u32[]{:S(2)}, u32[]{:S(2)}) collective-permute-start(bf16[256,768]{1,0:T(8,128)(2,1)} %get-tuple-element.228), channel_id=1, source_target_pairs={{0,16},{16,0},{1,17},{17,1},{2,18},{18,2},{3,19},{19,3},{4,20},{20... | collective-permute-start | bytes 1179656 | tf_op jit(solution)/shard_map/ppermute | solution.py:843
  190.7 3.2 copy-start.23
  190.8 7.7 %collective-permute-start.17 = (bf16[2,4,192,768]{3,2,1,0:T(8,128)(2,1)}, bf16[2,4,192,768]{3,2,1,0:T(8,128)(2,1)}, u32[]{:S(2)}, u32[]{:S(2)}) collective-permute-start(bf16[2,4,192,768]{3,2,1,0:T(8,128)(2,1)} %bitcast.22), channel_id=1, source_target_pairs={{0,1},{1,0},{2,3},{3,2},{4,5},{5,4},{6,7},{7,6},{8,9},{9,8},{10,11... | collective-permute-start | bytes 7077896 | tf_op jit(solution)/shard_map/ppermute | solution.py:843
  194.0 4.5 %copy-start = (bf16[8,192,768]{2,1,0:T(8,128)(2,1)S(1)}, bf16[8,192,768]{2,1,0:T(8,128)(2,1)}, u32[]{:S(2)}) copy-start(bf16[8,192,768]{2,1,0:T(8,128)(2,1)} %get-tuple-element.252) | copy-start | bytes 7077892
  201.8 27.7 %collective-permute-start.18 = (bf16[4,192,768]{2,1,0:T(8,128)(2,1)}, bf16[4,192,768]{2,1,0:T(8,128)(2,1)S(1)}, u32[]{:S(2)}, u32[]{:S(2)}) collective-permute-start(bf16[4,192,768]{2,1,0:T(8,128)(2,1)} %get-tuple-element.305), channel_id=1, source_target_pairs={{0,2},{1,3},{2,0},{3,1},{4,6},{5,7},{6,4},{7,5},{8,10},{9,11},{10,... | collective-permute-start | bytes 3538952 | tf_op jit(solution)/shard_map/ppermute | solution.py:843
  229.4 1.4 copy-start.14
  229.4 18.4 %copy-start.3 = (bf16[8,720,128]{2,1,0:T(8,128)(2,1)S(1)}, bf16[8,720,128]{2,1,0:T(8,128)(2,1)}, u32[]{:S(2)}) copy-start(bf16[8,720,128]{2,1,0:T(8,128)(2,1)} %get-tuple-element.265) | copy-start | bytes 4423684
  230.8 17.0 %collective-permute-start.20 = (bf16[2,4,768,128]{3,2,1,0:T(8,128)(2,1)S(1)}, bf16[2,4,768,128]{3,2,1,0:T(8,128)(2,1)}, u32[]{:S(2)}, u32[]{:S(2)}) collective-permute-start(bf16[2,4,768,128]{3,2,1,0:T(8,128)(2,1)S(1)} %bitcast.167), channel_id=1, source_target_pairs={{0,1},{1,0},{2,3},{3,2},{4,5},{5,4},{6,7},{7,6},{8,9},{9,8},{10,11... | collective-permute-start | bytes 4718600 | tf_op jit(solution)/shard_map/ppermute | solution.py:843
  231.8 16.1 %collective-permute-start.19 = (bf16[2,4,720,128]{3,2,1,0:T(8,128)(2,1)}, bf16[2,4,720,128]{3,2,1,0:T(8,128)(2,1)S(1)}, u32[]{:S(2)}, u32[]{:S(2)}) collective-permute-start(bf16[2,4,720,128]{3,2,1,0:T(8,128)(2,1)} %bitcast.168), channel_id=1, source_target_pairs={{0,1},{1,0},{2,3},{3,2},{4,5},{5,4},{6,7},{7,6},{8,9},{9,8},{10,11... | collective-permute-start | bytes 4423688 | tf_op jit(solution)/shard_map/ppermute | solution.py:843
  231.8 16.1 %collective-permute-start.21 = (bf16[2,192,768]{2,1,0:T(8,128)(2,1)S(1)}, bf16[2,192,768]{2,1,0:T(8,128)(2,1)S(1)}, u32[]{:S(2)}, u32[]{:S(2)}) collective-permute-start(bf16[2,192,768]{2,1,0:T(8,128)(2,1)S(1)} %get-tuple-element.268), channel_id=1, source_target_pairs={{0,4},{1,5},{2,6},{3,7},{4,0},{5,1},{6,2},{7,3},{8,12},{9,13},{10,... | collective-permute-start | bytes 1769480 | tf_op jit(solution)/shard_map/ppermute | solution.py:843
  247.9 2.1 copy-start.5
  247.9 2.1 copy-start.6
  249.1 4.6 %copy-start.1 = (bf16[8,768,128]{2,1,0:T(8,128)(2,1)S(1)}, bf16[8,768,128]{2,1,0:T(8,128)(2,1)}, u32[]{:S(2)}) copy-start(bf16[8,768,128]{2,1,0:T(8,128)(2,1)} %get-tuple-element.274) | copy-start | bytes 4718596
  250.0 17.4 %collective-permute-start.22 = (bf16[4,720,128]{2,1,0:T(8,128)(2,1)}, bf16[4,720,128]{2,1,0:T(8,128)(2,1)}, u32[]{:S(2)}, u32[]{:S(2)}) collective-permute-start(bf16[4,720,128]{2,1,0:T(8,128)(2,1)} %get-tuple-element.272), channel_id=1, source_target_pairs={{0,2},{1,3},{2,0},{3,1},{4,6},{5,7},{6,4},{7,5},{8,10},{9,11},{10,... | collective-permute-start | bytes 2211848 | tf_op jit(solution)/shard_map/ppermute | solution.py:843
  250.8 16.6 %collective-permute-start.23 = (bf16[192,768]{1,0:T(8,128)(2,1)}, bf16[192,768]{1,0:T(8,128)(2,1)S(1)}, u32[]{:S(2)}, u32[]{:S(2)}) collective-permute-start(bf16[192,768]{1,0:T(8,128)(2,1)} %get-tuple-element.273), channel_id=1, source_target_pairs={{0,8},{1,9},{2,10},{3,11},{4,12},{5,13},{6,14},{7,15},{8,0},{9,1},... | collective-permute-start | bytes 884744 | tf_op jit(solution)/shard_map/ppermute | solution.py:843
  267.4 24.4 %collective-permute-start.24 = (bf16[4,768,128]{2,1,0:T(8,128)(2,1)}, bf16[4,768,128]{2,1,0:T(8,128)(2,1)S(1)}, u32[]{:S(2)}, u32[]{:S(2)}) collective-permute-start(bf16[4,768,128]{2,1,0:T(8,128)(2,1)} %get-tuple-element.279), channel_id=1, source_target_pairs={{0,2},{1,3},{2,0},{3,1},{4,6},{5,7},{6,4},{7,5},{8,10},{9,11},{10,... | collective-permute-start | bytes 2359304 | tf_op jit(solution)/shard_map/ppermute | solution.py:843
  267.7 34.5 %collective-permute-start.25 = (bf16[2,512,384]{2,1,0:T(8,128)(2,1)}, bf16[2,512,384]{2,1,0:T(8,128)(2,1)}, u32[]{:S(2)}, u32[]{:S(2)}) collective-permute-start(bf16[2,512,384]{2,1,0:T(8,128)(2,1)} %get-tuple-element.280), channel_id=1, source_target_pairs={{0,1},{1,2},{2,3},{3,4},{4,5},{5,6},{6,7},{7,8},{8,9},{9,10},{10,1... | collective-permute-start | bytes 2359304 | tf_op jit(solution)/shard_map/ppermute | solution.py:849
  272.8 29.5 %collective-permute-start.26 = (bf16[2,512,384]{2,1,0:T(8,128)(2,1)}, bf16[2,512,384]{2,1,0:T(8,128)(2,1)}, u32[]{:S(2)}, u32[]{:S(2)}) collective-permute-start(bf16[2,512,384]{2,1,0:T(8,128)(2,1)} %get-tuple-element.281), channel_id=1, source_target_pairs={{1,0},{2,1},{3,2},{4,3},{5,4},{6,5},{7,6},{8,7},{9,8},{10,9},{11,1... | collective-permute-start | bytes 2359304 | tf_op jit(solution)/shard_map/ppermute | solution.py:849
  276.0 6.0 %collective-permute-start.29 = (bf16[24,1536]{1,0:T(8,128)(2,1)S(1)}, bf16[24,1536]{1,0:T(8,128)(2,1)S(1)}, u32[]{:S(2)}, u32[]{:S(2)}) collective-permute-start(bf16[24,1536]{1,0:T(8,128)(2,1)S(1)} %dynamic-slice_bitcast_fusion), channel_id=1, source_target_pairs={{0,16},{16,0},{1,17},{17,1},{2,18},{18,2},{3,19},{19,3},{4,20},{20... | collective-permute-start | bytes 221192 | tf_op jit(solution)/shard_map/ppermute | solution.py:843
  278.5 31.5 %all-to-all-start = ((bf16[4,720,128]{2,1,0:T(8,128)(2,1)}), bf16[4,720,128]{2,1,0:T(8,128)(2,1)S(1)}, u32[]{:S(2)}, u32[]{:S(2)}) async-start(bf16[4,720,128]{2,1,0:T(8,128)(2,1)} %add_convert_fusion.1), calls=%async_computation | async-start | bytes 1474560 | tf_op jit(solution)/shard_map/all_to_all | solution.py:861
  309.7 9.9 %collective-permute-start.27 = (bf16[256,768]{1,0:T(8,128)(2,1)}, bf16[256,768]{1,0:T(8,128)(2,1)S(1)}, u32[]{:S(2)}, u32[]{:S(2)}) collective-permute-start(bf16[256,768]{1,0:T(8,128)(2,1)} %get-tuple-element.290), channel_id=1, source_target_pairs={{0,16},{16,0},{1,17},{17,1},{2,18},{18,2},{3,19},{19,3},{4,20},{20... | collective-permute-start | bytes 1179656 | tf_op jit(solution)/shard_map/ppermute | solution.py:843
  310.0 19.5 %all-to-all-start.1 = ((bf16[4,768,128]{2,1,0:T(8,128)(2,1)}), bf16[4,768,128]{2,1,0:T(8,128)(2,1)S(1)}, u32[]{:S(2)}, u32[]{:S(2)}) async-start(bf16[4,768,128]{2,1,0:T(8,128)(2,1)} %add_convert_fusion), calls=%async_computation.1 | async-start | bytes 1572864 | tf_op jit(solution)/shard_map/all_to_all | solution.py:861
  314.5 5.1 %copy-start.4 = (f32[256,768]{1,0:T(8,128)S(1)}, f32[256,768]{1,0:T(8,128)}, u32[]{:S(2)}) copy-start(f32[256,768]{1,0:T(8,128)} %get-tuple-element.289) | copy-start | bytes 2359300
  314.6 3.8 %collective-permute-start.28 = (bf16[216,128]{1,0:T(8,128)(2,1)S(1)}, bf16[216,128]{1,0:T(8,128)(2,1)S(1)}, u32[]{:S(2)}, u32[]{:S(2)}) collective-permute-start(bf16[216,128]{1,0:T(8,128)(2,1)S(1)} %bitcast.153), channel_id=1, source_target_pairs={{0,16},{16,0},{1,17},{17,1},{2,18},{18,2},{3,19},{19,3},{4,20},{20... | collective-permute-start | bytes 165896 | tf_op jit(solution)/shard_map/ppermute | solution.py:843
  320.5 9.6 %copy-start.2 = (f32[6,32,512]{2,1,0:T(8,128)S(1)}, f32[6,32,512]{2,1,0:T(8,128)}, u32[]{:S(2)}) copy-start(f32[6,32,512]{2,1,0:T(8,128)} %get-tuple-element.303) | copy-start | bytes 1179652
  320.5 9.6 %copy-start.11 = (f32[6]{0:T(128)S(1)}, f32[6]{0:T(128)}, u32[]{:S(2)}) copy-start(f32[6]{0:T(128)} %param.24) | copy-start | bytes 76
  (1 other events, 1.3 us)
Sparse Core Ops, SparseCore 0:
  22.3 56.8 all-gather.2
  81.5 58.0 all-gather.4
where the time goes:
time: 339 us; the launch traced here: 338 us
  Pallas kernels  115 us (34%)
  waiting for transfers between devices  109 us (32%)
  starting transfers between devices  50.1 us (15%)
  other arithmetic  25.3 us (7%)
  local copies, waits for them, and re-layouts  23.3 us (7%)
  between operations  15 us (4%)
    ppermute x23, waiting for transfers between devices, swap(): return lax.ppermute(value, axis, [(i, i ^ bit) for i in range(count)])  69.7 us
    pallas_call x1, Pallas kernels, attend(): pl.pallas_call(attend_kernel, name='attend', grid=(3,), out_shape=(shape(...  27.9 us
    pallas_call x1, Pallas kernels, attend_back(): pl.pallas_call(partial(attend_back_kernel, len(before)), name=f'attend_ba...  27.4 us
    ppermute x23, starting transfers between devices, swap(): return lax.ppermute(value, axis, [(i, i ^ bit) for i in range(count)])  22.5 us
    pallas_call x2, Pallas kernels, feed_back(): pl.pallas_call(partial(feed_back_kernel, index), name=f'feed_back_{index}...  15.1 us
    pallas_call x2, Pallas kernels, feed_up(): pl.pallas_call(feed_up_kernel, name=f'feed_up_{index}', grid=(1,), out_sh...  14 us
    ppermute x4, starting transfers between devices, shifted(): lax.ppermute(value, axis, [(source, source + steps) for source in range(l...  12.2 us
    convert_element_type x8, other arithmetic, add(): return (mine.astype(F32) + got.astype(F32)).astype(mine.dtype)  11.8 us
  transfers between devices with their start and end apart: 34, of which 15 were waited for; matrix products, arithmetic and copies ran while one was open for 10% of the time, Pallas kernels for 32%

commit v1 on v0

--- a/solution.py
+++ b/solution.py
@@ -22,10 +22,10 @@
 BF = jnp.bfloat16
 F32 = jnp.float32
 HIGH = lax.Precision.HIGHEST
-PART_TOTALS = 144
-PART_SUMS = 160
-PART_OUT = 192
-PART = 240
+PART_SUMS = 144
+PART_TOTALS = PART_SUMS + 6
+PART_OUT = 176
+PART = 224
 PART_TABLE = 256
 
 
@@ -306,10 +306,10 @@
     gout[...] = tn(ctx_all[0], dattn0[...]) + tn(ctx_all[1], dattn1[...])
     totals = jnp.concatenate(
         [
+            sums[0:6, 0:128],
             column_sum(query_grad.astype(F32)),
             column_sum(pair_grad[:, 128:].astype(F32)),
-            jnp.zeros((14, 128), F32),
-            sums[:, 0:128],
+            sums[8:16, 0:128],
             sums[:, 128:256],
         ],
         axis=0,
@@ -324,7 +324,7 @@
             both = jnp.concatenate(rows, axis=0).astype(BF)
             for i in range(3):
                 out[t, i * 48 : i * 48 + 48, :] = both[:, i * 128 : (i + 1) * 128]
-            out[t, PART_TOTALS:PART_OUT, :] = totals
+            out[t, PART_SUMS:PART_OUT, :] = totals
             rows = gout[pl.ds(pl.multiple_of(place * 24, 8), 24), :]
             out[t, PART_OUT:PART, :] = jnp.concatenate(
                 [rows[:, 0:128], rows[:, 128:256]], axis=0
@@ -1105,11 +1105,11 @@
         feed_got = swap(feed[1], "fsdp", 4)
         part_got = swap(by_core(parts[1]), *CORE)
         table_got = swap(by_core(parts[3]), *CORE)
-        part_got, table_got, feed_got = tie(part_got, table_got, feed_got)
+        part_got, table_got = tie(part_got, table_got)
+        part, table_part = sum_core(parts[0], part_got), sum_core(parts[2], table_got)
+        part_got = swap(part[1], *ALONG_Y)
         feed = add(feed[0][0], feed_got[0]), add(feed[0][1], feed_got[1])
-        part, table_part = sum_core(parts[0], part_got), sum_core(parts[2], table_got)
-        part, feed = tie(part, feed)
-        part_got, feed_got = swap(part[1], *ALONG_Y), swap(feed[1], "fsdp", 8)
+        feed_got = swap(feed[1], "fsdp", 8)
         part_got, feed_got, table_part, low, high = tie(
             part_got, feed_got, table_part, low, high
         )
@@ -1127,7 +1127,7 @@
         table_total = table_total.reshape(3, 2, 4, 32, 128).transpose(0, 1, 3, 2, 4)
         table_total = table_total.reshape(6, 32, MPOS).astype(F32)
         blocks = part.reshape(3, PART, 128)
-        weight = blocks[:, :PART_TOTALS].reshape(3, 3, 2, rows, 128).transpose(1, 0, 2, 3, 4)
+        weight = blocks[:, :PART_SUMS].reshape(3, 3, 2, rows, 128).transpose(1, 0, 2, 3, 4)
         mine = lax.dynamic_index_in_dim(weight, side, 2, False)
         sent = lax.dynamic_index_in_dim(weight, 1 - side, 2, False)
         sums = blocks[:, PART_SUMS:PART_OUT].reshape(6, 16, 128)
@@ -1162,7 +1162,7 @@
         table_total = lax.psum_scatter(
             table_grad.reshape(6, MPOS, MPOS), "fsdp", scatter_dimension=1, tiled=True
         ).astype(F32)
-        head_rows = blocks[:, :, :, :PART_TOTALS].reshape(8, 2, 3, 3, 2, 24, 128)
+        head_rows = blocks[:, :, :, :PART_SUMS].reshape(8, 2, 3, 3, 2, 24, 128)
         head_rows = head_rows.transpose(4, 0, 1, 5, 3, 2, 6).reshape(D, 3, 1, OWN)
         blank = jnp.zeros_like(head_rows)
         both = jnp.concatenate(

time: 339 us -> 334 us (0.985)
  waiting for transfers between devices: 109 us -> 104 us
    ppermute x23, waiting for transfers between devices: 69.7 us -> 65.2 us  [swap(): return lax.ppermute(value, axis, [(i, i ^ bit) for i in range(count)])]
  transfers between devices with their start and end apart: 34 -> 34, of which waited for: 15 -> 16; matrix products, arithmetic and copies ran while one was open for 10% -> 11% of each run, Pallas kernels for 32% -> 32%
where the time goes in v1:
time: 334 us; the launch traced here: 333 us
  Pallas kernels  115 us (34%)
  waiting for transfers between devices  104 us (31%)
  starting transfers between devices  50.6 us (15%)
  other arithmetic  24.5 us (7%)
  local copies, waits for them, and re-layouts  23.5 us (7%)
  between operations  15 us (4%)
    ppermute x23, waiting for transfers between devices, swap(): return lax.ppermute(value, axis, [(i, i ^ bit) for i in range(count)])  65.2 us
    pallas_call x1, Pallas kernels, attend(): pl.pallas_call(attend_kernel, name='attend', grid=(3,), out_shape=(shape(...  27.9 us
    pallas_call x1, Pallas kernels, attend_back(): pl.pallas_call(partial(attend_back_kernel, len(before)), name=f'attend_ba...  27.3 us
    ppermute x23, starting transfers between devices, swap(): return lax.ppermute(value, axis, [(i, i ^ bit) for i in range(count)])  25.5 us
    pallas_call x2, Pallas kernels, feed_back(): pl.pallas_call(partial(feed_back_kernel, index), name=f'feed_back_{index}...  15.1 us
    pallas_call x2, Pallas kernels, feed_up(): pl.pallas_call(feed_up_kernel, name=f'feed_up_{index}', grid=(1,), out_sh...  14.2 us
    all_gather x1, waiting for transfers between devices, per_device(): wg = lax.all_gather(shard, 'fsdp', axis=0, tiled=True).reshape(8, 2, 240, D)  13.1 us
    ppermute x4, starting transfers between devices, shifted(): lax.ppermute(value, axis, [(source, source + steps) for source in range(l...  10.5 us
  transfers between devices with their start and end apart: 34, of which 16 were waited for; matrix products, arithmetic and copies ran while one was open for 11% of the time, Pallas kernels for 32%

profile of v1, /device:TPU:1, one launch (start us, length us, event | category | flops | bytes accessed | tf_op | source)
XLA Modules:
  0.0 333.2 jit_solution(16089741239996514344)
XLA Ops:
  7.3 0.9 reshape.392
  8.9 1.3 collective-permute-start.8
  10.2 4.5 %collective-permute-start.10 = (bf16[24,1152]{1,0:T(8,128)(2,1)S(1)}, bf16[24,1152]{1,0:T(8,128)(2,1)S(1)}, u32[]{:S(2)}, u32[]{:S(2)}) collective-permute-start(bf16[24,1152]{1,0:T(8,128)(2,1)S(1)} %bitcast.158), channel_id=1, source_target_pairs={{1,16},{3,18},{5,20},{7,22},{9,24},{11,26},{13,28},{15,30},{16,1},... | collective-permute-start | bytes 165896 | tf_op jit(solution)/shard_map/ppermute | solution.py:914
  14.8 1.7 collective-permute-start.9
  16.4 2.1 fusion.29
  18.9 3.2 concatenate.46
  22.3 3.1 collective-permute-start.1
  25.4 1.9 collective-permute-start.2
  27.8 1.1 collective-permute-start.5
  30.2 5.5 %collective-permute-done.5 = bf16[1,24,2304]{2,1,0:T(8,128)(2,1)S(1)} collective-permute-done((bf16[1,24,2304]{2,1,0:T(8,128)(2,1)S(1)}, bf16[1,24,2304]{2,1,0:T(8,128)(2,1)S(1)}, u32[]{:S(2)}, u32[]{:S(2)}) %collective-permute-start.5) | collective-permute-done | bytes 110624 | tf_op jit(solution)/shard_map/ppermute | solution.py:843
  37.4 3.2 stack.15.scal
  41.0 1.1 collective-permute-start.4
  43.0 8.0 %collective-permute-done.3.y0 = bf16[256,768]{1,0:T(8,128)(2,1)S(1)} collective-permute-done((bf16[256,768]{1,0:T(8,128)(2,1)S(1)}, bf16[256,768]{1,0:T(8,128)(2,1)S(1)}, u32[]{:S(2)}, u32[]{:S(2)}) %collective-permute-start.3) | collective-permute-done | bytes 393248 | tf_op jit(solution)/shard_map/ppermute | solution.py:843
  51.0 8.5 %collective-permute-done.4.y2 = bf16[256,768]{1,0:T(8,128)(2,1)S(1)} collective-permute-done((bf16[256,768]{1,0:T(8,128)(2,1)S(1)}, bf16[256,768]{1,0:T(8,128)(2,1)S(1)}, u32[]{:S(2)}, u32[]{:S(2)}) %collective-permute-start.4) | collective-permute-done | bytes 393248 | tf_op jit(solution)/shard_map/ppermute | solution.py:843
  62.3 1.1 reshape.431.pos_col
  64.0 1.1 reshape.432.doc_col
  65.8 4.6 %collective-permute-done.7.cot_other = bf16[256,768]{1,0:T(8,128)(2,1)S(1)} collective-permute-done((bf16[256,768]{1,0:T(8,128)(2,1)S(1)}, bf16[256,768]{1,0:T(8,128)(2,1)S(1)}, u32[]{:S(2)}, u32[]{:S(2)}) %collective-permute-start.7) | collective-permute-done | bytes 393248 | tf_op jit(solution)/shard_map/ppermute | solution.py:843
  70.3 8.9 %all-gather.3.cloned.1.call-done = bf16[19968,128]{1,0:T(8,128)(2,1)} async-done(((bf16[1248,128]{1,0:T(8,128)(2,1)}), bf16[19968,128]{1,0:T(8,128)(2,1)}) %all-gather.3.cloned.1.call-update) | async-done | bytes 5111824 | tf_op jit(solution)/shard_map/all_gather | solution.py:1013
  80.7 1.2 collective-permute-start.11
  82.5 8.9 %project.1 = (bf16[512,384]{1,0:T(8,128)(2,1)}, bf16[1536,384]{1,0:T(8,128)(2,1)}, bf16[1536,384]{1,0:T(8,128)(2,1)}, bf16[1536,768]{1,0:T(8,128)(2,1)}, bf16[6,...) custom-call(s32[8]{0:T(128)} %stack.15.scal, bf16[256,768]{1,0:T(8,128)(2,1)} %bitcast.170, bf16[256,768]{1,0:T(8,128)(2,1)} %copy-done.20, ...), custom_call_target="tpu_custom_call" | custom-call | flops 10350000128 | bytes 1000 | tf_op jit(solution)/shard_map/project/pallas_call | solution.py:596
  91.4 27.9 %attend.1 = (bf16[2,256,384]{2,1,0:T(8,128)(2,1)}, f32[3,8,512]{2,1,0:T(8,128)}, bf16[3,2,6,256,512]{4,3,2,1,0:T(8,128)(2,1)}, bf16[3,2,6,256,512]{4,3,2,1,0:T(8,128)(2,1)}, bf16[6,512,256]{2,1,0:T(8,128)(2,1)}) custom-call(s32[8]{0:T(128)} %stack.15.scal, s32[1536,1]{1,0:T(8,128)} %reshape.431.pos_col, s32[6,1,256]{2,1,0:T(1,128)} %reshape.400.pos_row, ...), custom_call_target="tpu_custom_call" | custom-call | flops 29899999232 | bytes 1000 | tf_op jit(solution)/shard_map/attend/pallas_call | solution.py:623
  121.9 4.8 %collective-permute-done.12.ctx_other = bf16[2,256,384]{2,1,0:T(8,128)(2,1)S(1)} collective-permute-done((bf16[2,256,384]{2,1,0:T(8,128)(2,1)}, bf16[2,256,384]{2,1,0:T(8,128)(2,1)S(1)}, u32[]{:S(2)}, u32[]{:S(2)}) %collective-permute-start.12) | collective-permute-done | bytes 393248 | tf_op jit(solution)/shard_map/ppermute | solution.py:843
  126.7 13.1 %all-gather.5.cloned.1.call-done = bf16[3840,768]{1,0:T(8,128)(2,1)} async-done(((bf16[240,768]{1,0:T(8,128)(2,1)}), bf16[3840,768]{1,0:T(8,128)(2,1)}) %all-gather.5.cloned.1.call-update) | async-done | bytes 5898256 | tf_op jit(solution)/shard_map/all_gather | solution.py:1020
  140.4 7.1 %feed_up_0.1 = (f32[256,768]{1,0:T(8,128)}, f32[256,128]{1,0:T(8,128)}, bf16[256,768]{1,0:T(8,128)(2,1)}, f32[256,768]{1,0:T(8,128)}, bf16[256,768]{1,0:T(8,128)...) custom-call(s32[8]{0:T(128)} %stack.15.scal, bf16[1536,768]{1,0:T(8,128)(2,1)} %get-tuple-element.156.x, ...), custom_call_target="tpu_custom_call" | custom-call | flops 9200000000 | bytes 1000 | tf_op jit(solution)/shard_map/feed_up_0/pallas_call | solution.py:748
  147.5 1.3 collective-permute-start.13
  149.3 7.1 %feed_up_1.1 = (f32[256,768]{1,0:T(8,128)}, f32[256,128]{1,0:T(8,128)}, bf16[256,768]{1,0:T(8,128)(2,1)}, f32[256,768]{1,0:T(8,128)}, bf16[256,768]{1,0:T(8,128)...) custom-call(s32[8]{0:T(128)} %stack.15.scal, bf16[1536,768]{1,0:T(8,128)(2,1)} %get-tuple-element.156.x, ...), custom_call_target="tpu_custom_call" | custom-call | flops 9200000000 | bytes 1000 | tf_op jit(solution)/shard_map/feed_up_1/pallas_call | solution.py:748
  156.5 1.8 collective-permute-done.13.got
  158.2 1.2 collective-permute-start.14
  159.4 7.4 %feed_back_0.1 = (bf16[256,768]{1,0:T(8,128)(2,1)}, bf16[256,768]{1,0:T(8,128)(2,1)}, bf16[2,256,768]{2,1,0:T(8,128)(2,1)}, f32[256,768]{1,0:T(8,128)}, bf16[256,768]{1,0:T(8,128)(2,1)}, /*index=5*/f32[16,768]{1,0:T(8,128)}) custom-call(s32[8]{0:T(128)} %stack.15.scal, f32[256,768]{1,0:T(8,128)} %get-tuple-element.166.base, bf16[256,768]{1,0:T(8,128)(2,1)} %copy-done.28, ...), custom_call_target="tpu_custom_call" | custom-call | flops 8049999872 | bytes 1000 | tf_op jit(solution)/shard_map/feed_back_0/pallas_call | solution.py:771
  166.9 1.1 collective-permute-done.14.got
  168.0 1.2 collective-permute-start.15
  169.2 7.7 %feed_back_1.1 = (bf16[256,768]{1,0:T(8,128)(2,1)}, bf16[256,768]{1,0:T(8,128)(2,1)}, bf16[2,256,768]{2,1,0:T(8,128)(2,1)}, f32[256,768]{1,0:T(8,128)}, bf16[256,768]{1,0:T(8,128)(2,1)}, /*index=5*/f32[16,768]{1,0:T(8,128)}) custom-call(s32[8]{0:T(128)} %stack.15.scal, f32[256,768]{1,0:T(8,128)} %get-tuple-element.186.base, bf16[256,768]{1,0:T(8,128)(2,1)} %copy-done.29, ...), custom_call_target="tpu_custom_call" | custom-call | flops 8049999872 | bytes 1000 | tf_op jit(solution)/shard_map/feed_back_1/pallas_call | solution.py:771
  176.9 1.1 collective-permute-start.16
  178.0 1.4 add.232.sums_in
  179.5 7.3 %weight_grads.1 = (bf16[8,192,768]{2,1,0:T(8,128)(2,1)}, bf16[8,192,768]{2,1,0:T(8,128)(2,1)}) custom-call(s32[8]{0:T(128)} %stack.15.scal, bf16[2,256,768]{2,1,0:T(8,128)(2,1)} %get-tuple-element.213.act0, bf16[256,768]{1,0:T(8,128)(2,1)} %get-tuple-element.214.ddown0, bf16[256,768]{1,0:T(8,128)(2,1)} %get-tuple-element.215.nlow0, ...), custom_call_target="tpu_custom_call" | custom-call | flops 8049999872 | bytes 1000 | tf_op jit(solution)/shard_map/weight_grads/pallas_call | solution.py:809
  186.8 4.0 %feed_close_0.1 = (f32[256,768]{1,0:T(8,128)}, bf16[256,768]{1,0:T(8,128)(2,1)}, bf16[256,384]{1,0:T(8,128)(2,1)}, f32[16,768]{1,0:T(8,128)}) custom-call(s32[8]{0:T(128)} %stack.15.scal, f32[256,768]{1,0:T(8,128)} %get-tuple-element.203.base, bf16[256,768]{1,0:T(8,128)(2,1)} %copy-done.27, f32[256,768]{1,0:T(8,128)} %get-tuple-element.205.unit1, ...), custom_call_target="tpu_custom_call" | custom-call | flops 4600000000 | bytes 1000 | tf_op jit(solution)/shard_map/feed_close_0/pallas_call | solution.py:791
  190.9 3.2 collective-permute-start.17
  194.1 4.2 %feed_close_1.1 = (f32[256,768]{1,0:T(8,128)}, bf16[256,768]{1,0:T(8,128)(2,1)}, bf16[256,384]{1,0:T(8,128)(2,1)}, f32[16,768]{1,0:T(8,128)}) custom-call(s32[8]{0:T(128)} %stack.15.scal, f32[256,768]{1,0:T(8,128)} %get-tuple-element.202.base, bf16[256,768]{1,0:T(8,128)(2,1)} %copy-done.25, f32[256,768]{1,0:T(8,128)} %get-tuple-element.225.unit1, ...), custom_call_target="tpu_custom_call" | custom-call | flops 4600000000 | bytes 1000 | tf_op jit(solution)/shard_map/feed_close_1/pallas_call | solution.py:791
  198.6 3.2 fusion
  202.1 27.3 %attend_back_0.1 = (bf16[512,384]{1,0:T(8,128)(2,1)}, f32[2,512,384]{2,1,0:T(8,128)}, bf16[2,512,384]{2,1,0:T(8,128)(2,1)}, bf16[2,512,384]{2,1,0:T(8,128)(2,1)}...) custom-call(s32[8]{0:T(128)} %stack.15.scal, ...), custom_call_target="tpu_custom_call" | custom-call | flops 34500001792 | bytes 1000 | tf_op jit(solution)/shard_map/attend_back_0/pallas_call | solution.py:671
  229.7 1.0 collective-permute-start.20
  230.9 2.6 collective-permute-start.22
  233.4 2.7 collective-permute-done.19
  236.1 1.5 fusion.5
  237.6 2.8 collective-permute-start.21
  241.2 5.8 %collective-permute-done.22 = bf16[2,192,768]{2,1,0:T(8,128)(2,1)S(1)} collective-permute-done((bf16[2,192,768]{2,1,0:T(8,128)(2,1)S(1)}, bf16[2,192,768]{2,1,0:T(8,128)(2,1)S(1)}, u32[]{:S(2)}, u32[]{:S(2)}) %collective-permute-start.22) | collective-permute-done | bytes 589856 | tf_op jit(solution)/shard_map/ppermute | solution.py:843
  247.9 1.7 collective-permute-start.23
  249.6 1.3 fusion.2
  250.9 12.1 %collective-permute-done.23 = bf16[192,768]{1,0:T(8,128)(2,1)S(1)} collective-permute-done((bf16[192,768]{1,0:T(8,128)(2,1)S(1)}, bf16[192,768]{1,0:T(8,128)(2,1)S(1)}, u32[]{:S(2)}, u32[]{:S(2)}) %collective-permute-start.23) | collective-permute-done | bytes 294944 | tf_op jit(solution)/shard_map/ppermute | solution.py:843
  263.0 2.0 collective-permute-start.24
  265.0 3.0 collective-permute-start.25
  268.0 2.4 collective-permute-start.26
  272.5 2.4 add_convert_fusion.1
  275.0 3.5 %all-to-all-start = ((bf16[4,672,128]{2,1,0:T(8,128)(2,1)}), bf16[4,672,128]{2,1,0:T(8,128)(2,1)S(1)}, u32[]{:S(2)}, u32[]{:S(2)}) async-start(bf16[4,672,128]{2,1,0:T(8,128)(2,1)} %add_convert_fusion.1), calls=%async_computation | async-start | bytes 1376256 | tf_op jit(solution)/shard_map/all_to_all | solution.py:861
  278.5 0.9 bitcast_select_fusion.3
  280.1 10.0 %collective-permute-done.24 = bf16[4,768,128]{2,1,0:T(8,128)(2,1)S(1)} collective-permute-done((bf16[4,768,128]{2,1,0:T(8,128)(2,1)}, bf16[4,768,128]{2,1,0:T(8,128)(2,1)S(1)}, u32[]{:S(2)}, u32[]{:S(2)}) %collective-permute-start.24) | collective-permute-done | bytes 786464 | tf_op jit(solution)/shard_map/ppermute | solution.py:843
  290.1 9.4 %collective-permute-done.25.refs_2_ = bf16[2,512,384]{2,1,0:T(8,128)(2,1)} collective-permute-done((bf16[2,512,384]{2,1,0:T(8,128)(2,1)}, bf16[2,512,384]{2,1,0:T(8,128)(2,1)}, u32[]{:S(2)}, u32[]{:S(2)}) %collective-permute-start.25) | collective-permute-done | bytes 786464 | tf_op jit(solution)/shard_map/ppermute | solution.py:849
  299.5 1.1 add_convert_fusion
  300.6 6.3 %project_back.1 = (f32[256,768]{1,0:T(8,128)}, bf16[256,768]{1,0:T(8,128)(2,1)}) custom-call(s32[8]{0:T(128)} %stack.15.scal, bf16[512,384]{1,0:T(8,128)(2,1)} %get-tuple-element.258.refs_0_, f32[2,512,384]{2,1,0:T(8,128)} %get-tuple-element.259.refs_1_, bf16[2,512,384]{2,1,0:T(8,128)(2,1)} %collective-permute-done.25.refs_2_, ...), custom_call_target="tpu_custom_call" | custom-call | flops 6899999744 | bytes 1000 | tf_op jit(solution)/shard_map/project_back/pallas_call | solution.py:825
  307.3 3.5 %all-to-all-start.1 = ((bf16[4,768,128]{2,1,0:T(8,128)(2,1)}), bf16[4,768,128]{2,1,0:T(8,128)(2,1)S(1)}, u32[]{:S(2)}, u32[]{:S(2)}) async-start(bf16[4,768,128]{2,1,0:T(8,128)(2,1)} %add_convert_fusion), calls=%async_computation.1 | async-start | bytes 1572864 | tf_op jit(solution)/shard_map/all_to_all | solution.py:861
  311.0 1.3 collective-permute-start.28
  315.3 0.9 reshape.423
  316.1 1.0 add_bitcast_fusion
  317.1 7.8 %all-to-all-done.1 = bf16[4,768,128]{2,1,0:T(8,128)(2,1)S(1)} async-done(((bf16[4,768,128]{2,1,0:T(8,128)(2,1)}), bf16[4,768,128]{2,1,0:T(8,128)(2,1)S(1)}, u32[]{:S(2)}, u32[]{:S(2)}) %all-to-all-start.1) | async-done | bytes 786464 | tf_op jit(solution)/shard_map/all_to_all | solution.py:861
  (201 shorter events, 25.7 us)
Async XLA Ops:
  7.2 11.5 %copy-start.15 = (bf16[6,24]{1,0:T(8,128)(2,1)S(1)}, bf16[6,24]{1,0:T(8,128)(2,1)}, u32[]{:S(2)}) copy-start(bf16[6,24]{1,0:T(8,128)(2,1)} %param.19) | copy-start | bytes 868
  7.2 11.5 %copy-start.30 = (bf16[2,24]{1,0:T(2,128)(2,1)S(1)}, bf16[2,24]{1,0:T(2,128)(2,1)}, u32[]{:S(2)}) copy-start(bf16[2,24]{1,0:T(2,128)(2,1)} %param.20) | copy-start | bytes 292
  7.2 11.5 %copy-start.31 = (bf16[96]{0:T(256)(128)(2,1)S(1)}, bf16[96]{0:T(256)(128)(2,1)}, u32[]{:S(2)}) copy-start(bf16[96]{0:T(256)(128)(2,1)} %param.21) | copy-start | bytes 580
  7.2 72.0 %all-gather.3.cloned.1.call-start = ((), (), s32[]{:S(2)}) async-start(), calls=%async_computation.2 | async-start | bytes 5431296 | tf_op jit(solution)/shard_map/all_gather | solution.py:1013
  8.9 9.8 %collective-permute-start.8 = (bf16[24,1152]{1,0:T(8,128)(2,1)S(1)}, bf16[24,1152]{1,0:T(8,128)(2,1)S(1)}, u32[]{:S(2)}, u32[]{:S(2)}) collective-permute-start(bf16[24,1152]{1,0:T(8,128)(2,1)S(1)} %bitcast.157), channel_id=1, source_target_pairs={{0,16},{2,18},{4,20},{6,22},{8,24},{10,26},{12,28},{14,30},{17,1},... | collective-permute-start | bytes 165896 | tf_op jit(solution)/shard_map/ppermute | solution.py:913
  10.2 8.5 %collective-permute-start.10 = (bf16[24,1152]{1,0:T(8,128)(2,1)S(1)}, bf16[24,1152]{1,0:T(8,128)(2,1)S(1)}, u32[]{:S(2)}, u32[]{:S(2)}) collective-permute-start(bf16[24,1152]{1,0:T(8,128)(2,1)S(1)} %bitcast.158), channel_id=1, source_target_pairs={{1,16},{3,18},{5,20},{7,22},{9,24},{11,26},{13,28},{15,30},{16,1},... | collective-permute-start | bytes 165896 | tf_op jit(solution)/shard_map/ppermute | solution.py:914
  14.8 4.0 %collective-permute-start.9 = (bf16[24,1152]{1,0:T(8,128)(2,1)S(1)}, bf16[24,1152]{1,0:T(8,128)(2,1)S(1)}, u32[]{:S(2)}, u32[]{:S(2)}) collective-permute-start(bf16[24,1152]{1,0:T(8,128)(2,1)S(1)} %bitcast.150), channel_id=1, source_target_pairs={{1,0},{3,2},{5,4},{7,6},{9,8},{11,10},{13,12},{15,14},{16,17},{18,... | collective-permute-start | bytes 165896 | tf_op jit(solution)/shard_map/ppermute | solution.py:914
  18.5 3.7 %copy-start.17 = (bf16[1,256,768]{2,1,0:T(8,128)(2,1)S(1)}, bf16[1,256,768]{2,1,0:T(8,128)(2,1)}, u32[]{:S(2)}) copy-start(bf16[1,256,768]{2,1,0:T(8,128)(2,1)} %param.14) | copy-start | bytes 1179652
  18.5 8.8 %copy-start.10 = (bf16[24,3072]{1,0:T(8,128)(2,1)S(1)}, bf16[24,3072]{1,0:T(8,128)(2,1)}, u32[]{:S(2)}) copy-start(bf16[24,3072]{1,0:T(8,128)(2,1)} %param.17) | copy-start | bytes 442372
  18.7 9.1 %copy-start.11 = (bf16[24,768]{1,0:T(8,128)(2,1)S(1)}, bf16[24,768]{1,0:T(8,128)(2,1)}, u32[]{:S(2)}) copy-start(bf16[24,768]{1,0:T(8,128)(2,1)} %param.16) | copy-start | bytes 110596
  18.8 10.1 %copy-start.16 = (s32[32]{0:T(128)S(1)}, s32[32]{0:T(128)}, u32[]{:S(2)}) copy-start(s32[32]{0:T(128)} %param.25) | copy-start | bytes 388
  18.8 10.4 %copy-start.32 = (s32[4]{0:T(128)S(1)}, s32[4]{0:T(128)}, u32[]{:S(2)}) copy-start(s32[4]{0:T(128)} %constant.175.clone) | copy-start | bytes 52
  22.2 117.7 %all-gather.5.cloned.1.call-start = ((), (), s32[]{:S(2)}) async-start(), calls=%async_computation.3 | async-start | bytes 6266880 | tf_op jit(solution)/shard_map/all_gather | solution.py:1020
  22.2 18.4 %collective-permute-start = (bf16[256,768]{1,0:T(8,128)(2,1)S(1)}, bf16[256,768]{1,0:T(8,128)(2,1)S(1)}, u32[]{:S(2)}, u32[]{:S(2)}) collective-permute-start(bf16[256,768]{1,0:T(8,128)(2,1)S(1)} %bitcast.171), channel_id=1, source_target_pairs={{0,16},{16,0},{1,17},{17,1},{2,18},{18,2},{3,19},{19,3},{4,20},{20... | collective-permute-start | bytes 1179656 | tf_op jit(solution)/shard_map/ppermute | solution.py:843
  22.3 18.3 %collective-permute-start.1 = (bf16[256,768]{1,0:T(8,128)(2,1)S(1)}, bf16[256,768]{1,0:T(8,128)(2,1)S(1)}, u32[]{:S(2)}, u32[]{:S(2)}) collective-permute-start(bf16[256,768]{1,0:T(8,128)(2,1)S(1)} %bitcast.172), channel_id=1, source_target_pairs={{0,1},{1,2},{2,3},{3,4},{4,5},{5,6},{6,7},{7,8},{8,9},{9,10},{10,1... | collective-permute-start | bytes 1179656 | tf_op jit(solution)/shard_map/ppermute | solution.py:849
  25.4 15.2 %collective-permute-start.2 = (bf16[256,768]{1,0:T(8,128)(2,1)S(1)}, bf16[256,768]{1,0:T(8,128)(2,1)S(1)}, u32[]{:S(2)}, u32[]{:S(2)}) collective-permute-start(bf16[256,768]{1,0:T(8,128)(2,1)S(1)} %bitcast.173), channel_id=1, source_target_pairs={{1,0},{2,1},{3,2},{4,3},{5,4},{6,5},{7,6},{8,7},{9,8},{10,9},{11,1... | collective-permute-start | bytes 1179656 | tf_op jit(solution)/shard_map/ppermute | solution.py:849
  27.8 7.9 %collective-permute-start.5 = (bf16[1,24,2304]{2,1,0:T(8,128)(2,1)S(1)}, bf16[1,24,2304]{2,1,0:T(8,128)(2,1)S(1)}, u32[]{:S(2)}, u32[]{:S(2)}) collective-permute-start(bf16[1,24,2304]{2,1,0:T(8,128)(2,1)S(1)} %fusion.14), channel_id=1, source_target_pairs={{0,16},{16,0},{1,17},{17,1},{2,18},{18,2},{3,19},{19,3},{4,20},{20... | collective-permute-start | bytes 331784 | tf_op jit(solution)/shard_map/ppermute | solution.py:843
  35.9 6.4 %copy-start.12 = (bf16[96,768]{1,0:T(8,128)(2,1)S(1)}, bf16[96,768]{1,0:T(8,128)(2,1)}, u32[]{:S(2)}) copy-start(bf16[96,768]{1,0:T(8,128)(2,1)} %param.18) | copy-start | bytes 442372
  36.6 24.3 %copy-start.18 = (bf16[1,256,768]{2,1,0:T(8,128)(2,1)S(1)}, bf16[1,256,768]{2,1,0:T(8,128)(2,1)}, u32[]{:S(2)}) copy-start(bf16[1,256,768]{2,1,0:T(8,128)(2,1)} %param.26) | copy-start | bytes 1179652
  36.6 5.6 %collective-permute-start.6 = (bf16[2,24,1152]{2,1,0:T(8,128)(2,1)S(1)}, bf16[2,24,1152]{2,1,0:T(8,128)(2,1)S(1)}, u32[]{:S(2)}, u32[]{:S(2)}) collective-permute-start(bf16[2,24,1152]{2,1,0:T(8,128)(2,1)S(1)} %bitcast.153), channel_id=1, source_target_pairs={{0,1},{1,0},{2,3},{3,2},{4,5},{5,4},{6,7},{7,6},{8,9},{9,8},{10,11... | collective-permute-start | bytes 331784 | tf_op jit(solution)/shard_map/ppermute | solution.py:843
  40.6 22.8 %copy-start.19 = (bf16[256,768]{1,0:T(8,128)(2,1)}, bf16[256,768]{1,0:T(8,128)(2,1)S(1)}, u32[]{:S(2)}) copy-start(bf16[256,768]{1,0:T(8,128)(2,1)S(1)} %collective-permute-done.y1) | copy-start | bytes 1179652
  40.6 22.8 %copy-start.20 = (bf16[256,768]{1,0:T(8,128)(2,1)}, bf16[256,768]{1,0:T(8,128)(2,1)S(1)}, u32[]{:S(2)}) copy-start(bf16[256,768]{1,0:T(8,128)(2,1)S(1)} %collective-permute-done.1.x0) | copy-start | bytes 1179652
  40.6 22.8 %copy-start.21 = (bf16[256,768]{1,0:T(8,128)(2,1)}, bf16[256,768]{1,0:T(8,128)(2,1)S(1)}, u32[]{:S(2)}) copy-start(bf16[256,768]{1,0:T(8,128)(2,1)S(1)} %collective-permute-done.2.x2) | copy-start | bytes 1179652
  40.6 10.4 %collective-permute-start.3 = (bf16[256,768]{1,0:T(8,128)(2,1)S(1)}, bf16[256,768]{1,0:T(8,128)(2,1)S(1)}, u32[]{:S(2)}, u32[]{:S(2)}) collective-permute-start(bf16[256,768]{1,0:T(8,128)(2,1)S(1)} %collective-permute-done.1.x0), channel_id=1, source_target_pairs={{0,16},{16,0},{1,17},{17,1},{2,18},{18,2},{3,19},{19,3},{4,20},{20... | collective-permute-start | bytes 1179656 | tf_op jit(solution)/shard_map/ppermute | solution.py:843
  41.0 18.5 %collective-permute-start.4 = (bf16[256,768]{1,0:T(8,128)(2,1)S(1)}, bf16[256,768]{1,0:T(8,128)(2,1)S(1)}, u32[]{:S(2)}, u32[]{:S(2)}) collective-permute-start(bf16[256,768]{1,0:T(8,128)(2,1)S(1)} %collective-permute-done.2.x2), channel_id=1, source_target_pairs={{0,16},{16,0},{1,17},{17,1},{2,18},{18,2},{3,19},{19,3},{4,20},{20... | collective-permute-start | bytes 1179656 | tf_op jit(solution)/shard_map/ppermute | solution.py:843
  51.0 31.5 %copy-start.23 = (bf16[256,768]{1,0:T(8,128)(2,1)}, bf16[256,768]{1,0:T(8,128)(2,1)S(1)}, u32[]{:S(2)}) copy-start(bf16[256,768]{1,0:T(8,128)(2,1)S(1)} %collective-permute-done.3.y0) | copy-start | bytes 1179652
  59.5 23.0 %copy-start.24 = (bf16[256,768]{1,0:T(8,128)(2,1)}, bf16[256,768]{1,0:T(8,128)(2,1)S(1)}, u32[]{:S(2)}) copy-start(bf16[256,768]{1,0:T(8,128)(2,1)S(1)} %collective-permute-done.4.y2) | copy-start | bytes 1179652
  60.8 9.5 %collective-permute-start.7 = (bf16[256,768]{1,0:T(8,128)(2,1)S(1)}, bf16[256,768]{1,0:T(8,128)(2,1)S(1)}, u32[]{:S(2)}, u32[]{:S(2)}) collective-permute-start(bf16[256,768]{1,0:T(8,128)(2,1)S(1)} %bitcast.176), channel_id=1, source_target_pairs={{0,16},{16,0},{1,17},{17,1},{2,18},{18,2},{3,19},{19,3},{4,20},{20... | collective-permute-start | bytes 1179656 | tf_op jit(solution)/shard_map/ppermute | solution.py:843
  70.3 21.1 %copy-start.22 = (bf16[256,768]{1,0:T(8,128)(2,1)}, bf16[256,768]{1,0:T(8,128)(2,1)S(1)}, u32[]{:S(2)}) copy-start(bf16[256,768]{1,0:T(8,128)(2,1)S(1)} %collective-permute-done.7.cot_other) | copy-start | bytes 1179652
  80.7 10.7 %collective-permute-start.11 = (bf16[16,16,128]{2,0,1:T(8,128)(2,1)S(1)}, bf16[16,16,128]{2,0,1:T(8,128)(2,1)S(1)}, u32[]{:S(2)}, u32[]{:S(2)}) collective-permute-start(bf16[16,16,128]{2,0,1:T(8,128)(2,1)S(1)} %slice_bitcast_fusion), channel_id=1, source_target_pairs={{0,16},{16,0},{1,17},{17,1},{2,18},{18,2},{3,19},{19,3},{4,20},{20... | collective-permute-start | bytes 196616 | tf_op jit(solution)/shard_map/ppermute | solution.py:843
  119.4 7.3 %collective-permute-start.12 = (bf16[2,256,384]{2,1,0:T(8,128)(2,1)}, bf16[2,256,384]{2,1,0:T(8,128)(2,1)S(1)}, u32[]{:S(2)}, u32[]{:S(2)}) collective-permute-start(bf16[2,256,384]{2,1,0:T(8,128)(2,1)} %get-tuple-element.163.ctx_mine.ctx.ctx_all), channel_id=1, source_target_pairs={{0,16},{16,0},{1,17},{17,1},{2,18},{18,2},{3,19},{19,3},{4,20},{20... | collective-permute-start | bytes 1179656 | tf_op jit(solution)/shard_map/ppermute | solution.py:843
  126.7 13.7 %copy-start.26 = (bf16[2,256,384]{2,1,0:T(8,128)(2,1)}, bf16[2,256,384]{2,1,0:T(8,128)(2,1)S(1)}, u32[]{:S(2)}) copy-start(bf16[2,256,384]{2,1,0:T(8,128)(2,1)S(1)} %collective-permute-done.12.ctx_other) | copy-start | bytes 1179652
  147.5 10.7 %collective-permute-start.13 = (bf16[256,768]{1,0:T(8,128)(2,1)}, bf16[256,768]{1,0:T(8,128)(2,1)S(1)}, u32[]{:S(2)}, u32[]{:S(2)}) collective-permute-start(bf16[256,768]{1,0:T(8,128)(2,1)} %get-tuple-element.174), channel_id=1, source_target_pairs={{0,16},{16,0},{1,17},{17,1},{2,18},{18,2},{3,19},{19,3},{4,20},{20... | collective-permute-start | bytes 1179656 | tf_op jit(solution)/shard_map/ppermute | solution.py:843
  158.2 9.8 %collective-permute-start.14 = (bf16[256,768]{1,0:T(8,128)(2,1)}, bf16[256,768]{1,0:T(8,128)(2,1)S(1)}, u32[]{:S(2)}, u32[]{:S(2)}) collective-permute-start(bf16[256,768]{1,0:T(8,128)(2,1)} %get-tuple-element.184), channel_id=1, source_target_pairs={{0,16},{16,0},{1,17},{17,1},{2,18},{18,2},{3,19},{19,3},{4,20},{20... | collective-permute-start | bytes 1179656 | tf_op jit(solution)/shard_map/ppermute | solution.py:843
  168.0 10.0 %copy-start.13 = (f32[16,768]{1,0:T(8,128)S(1)}, f32[16,768]{1,0:T(8,128)}, u32[]{:S(2)}) copy-start(f32[16,768]{1,0:T(8,128)} %get-tuple-element.207) | copy-start | bytes 147460
  168.0 8.9 %collective-permute-start.15 = (bf16[256,768]{1,0:T(8,128)(2,1)}, bf16[256,768]{1,0:T(8,128)(2,1)S(1)}, u32[]{:S(2)}, u32[]{:S(2)}) collective-permute-start(bf16[256,768]{1,0:T(8,128)(2,1)} %get-tuple-element.195), channel_id=1, source_target_pairs={{0,16},{16,0},{1,17},{17,1},{2,18},{18,2},{3,19},{19,3},{4,20},{20... | collective-permute-start | bytes 1179656 | tf_op jit(solution)/shard_map/ppermute | solution.py:843
  176.9 9.9 %copy-start.27 = (bf16[256,768]{1,0:T(8,128)(2,1)}, bf16[256,768]{1,0:T(8,128)(2,1)S(1)}, u32[]{:S(2)}) copy-start(bf16[256,768]{1,0:T(8,128)(2,1)S(1)} %collective-permute-done.15.got) | copy-start | bytes 1179652
  176.9 14.0 %collective-permute-start.16 = (bf16[256,768]{1,0:T(8,128)(2,1)}, bf16[256,768]{1,0:T(8,128)(2,1)S(1)}, u32[]{:S(2)}, u32[]{:S(2)}) collective-permute-start(bf16[256,768]{1,0:T(8,128)(2,1)} %get-tuple-element.223), channel_id=1, source_target_pairs={{0,16},{16,0},{1,17},{17,1},{2,18},{18,2},{3,19},{19,3},{4,20},{20... | collective-permute-start | bytes 1179656 | tf_op jit(solution)/shard_map/ppermute | solution.py:843
  190.9 3.2 copy-start.25
  190.9 7.7 %collective-permute-start.17 = (bf16[2,4,192,768]{3,2,1,0:T(8,128)(2,1)}, bf16[2,4,192,768]{3,2,1,0:T(8,128)(2,1)}, u32[]{:S(2)}, u32[]{:S(2)}) collective-permute-start(bf16[2,4,192,768]{3,2,1,0:T(8,128)(2,1)} %bitcast.22), channel_id=1, source_target_pairs={{0,1},{1,0},{2,3},{3,2},{4,5},{5,4},{6,7},{7,6},{8,9},{9,8},{10,11... | collective-permute-start | bytes 7077896 | tf_op jit(solution)/shard_map/ppermute | solution.py:843
  194.1 4.5 %copy-start = (bf16[8,192,768]{2,1,0:T(8,128)(2,1)S(1)}, bf16[8,192,768]{2,1,0:T(8,128)(2,1)}, u32[]{:S(2)}) copy-start(bf16[8,192,768]{2,1,0:T(8,128)(2,1)} %get-tuple-element.247) | copy-start | bytes 7077892
  201.8 27.6 %collective-permute-start.18 = (bf16[4,192,768]{2,1,0:T(8,128)(2,1)}, bf16[4,192,768]{2,1,0:T(8,128)(2,1)S(1)}, u32[]{:S(2)}, u32[]{:S(2)}) collective-permute-start(bf16[4,192,768]{2,1,0:T(8,128)(2,1)} %get-tuple-element.295), channel_id=1, source_target_pairs={{0,2},{1,3},{2,0},{3,1},{4,6},{5,7},{6,4},{7,5},{8,10},{9,11},{10,... | collective-permute-start | bytes 3538952 | tf_op jit(solution)/shard_map/ppermute | solution.py:843
  229.7 6.4 %collective-permute-start.20 = (bf16[2,4,768,128]{3,2,1,0:T(8,128)(2,1)}, bf16[2,4,768,128]{3,2,1,0:T(8,128)(2,1)S(1)}, u32[]{:S(2)}, u32[]{:S(2)}) collective-permute-start(bf16[2,4,768,128]{3,2,1,0:T(8,128)(2,1)} %bitcast.26), channel_id=1, source_target_pairs={{0,1},{1,0},{2,3},{3,2},{4,5},{5,4},{6,7},{7,6},{8,9},{9,8},{10,11... | collective-permute-start | bytes 4718600 | tf_op jit(solution)/shard_map/ppermute | solution.py:843
  230.8 5.3 %collective-permute-start.19 = (bf16[2,4,672,128]{3,2,1,0:T(8,128)(2,1)}, bf16[2,4,672,128]{3,2,1,0:T(8,128)(2,1)}, u32[]{:S(2)}, u32[]{:S(2)}) collective-permute-start(bf16[2,4,672,128]{3,2,1,0:T(8,128)(2,1)} %bitcast.25), channel_id=1, source_target_pairs={{0,1},{1,0},{2,3},{3,2},{4,5},{5,4},{6,7},{7,6},{8,9},{9,8},{10,11... | collective-permute-start | bytes 4128776 | tf_op jit(solution)/shard_map/ppermute | solution.py:843
  230.9 16.2 %collective-permute-start.22 = (bf16[2,192,768]{2,1,0:T(8,128)(2,1)S(1)}, bf16[2,192,768]{2,1,0:T(8,128)(2,1)S(1)}, u32[]{:S(2)}, u32[]{:S(2)}) collective-permute-start(bf16[2,192,768]{2,1,0:T(8,128)(2,1)S(1)} %get-tuple-element.265), channel_id=1, source_target_pairs={{0,4},{1,5},{2,6},{3,7},{4,0},{5,1},{6,2},{7,3},{8,12},{9,13},{10,... | collective-permute-start | bytes 1769480 | tf_op jit(solution)/shard_map/ppermute | solution.py:843
  233.4 7.0 %copy-start.9 = (bf16[256,768]{1,0:T(8,128)(2,1)S(1)}, bf16[256,768]{1,0:T(8,128)(2,1)}, u32[]{:S(2)}) copy-start(bf16[256,768]{1,0:T(8,128)(2,1)} %get-tuple-element.185) | copy-start | bytes 1179652
  233.4 16.1 %copy-start.1 = (bf16[8,768,128]{2,1,0:T(8,128)(2,1)S(1)}, bf16[8,768,128]{2,1,0:T(8,128)(2,1)}, u32[]{:S(2)}) copy-start(bf16[8,768,128]{2,1,0:T(8,128)(2,1)} %get-tuple-element.266) | copy-start | bytes 4718596
  237.6 25.4 %collective-permute-start.21 = (bf16[4,672,128]{2,1,0:T(8,128)(2,1)S(1)}, bf16[4,672,128]{2,1,0:T(8,128)(2,1)S(1)}, u32[]{:S(2)}, u32[]{:S(2)}) collective-permute-start(bf16[4,672,128]{2,1,0:T(8,128)(2,1)S(1)} %fusion.5), channel_id=1, source_target_pairs={{0,2},{1,3},{2,0},{3,1},{4,6},{5,7},{6,4},{7,5},{8,10},{9,11},{10,... | collective-permute-start | bytes 2064392 | tf_op jit(solution)/shard_map/ppermute | solution.py:843
  247.9 15.1 %collective-permute-start.23 = (bf16[192,768]{1,0:T(8,128)(2,1)S(1)}, bf16[192,768]{1,0:T(8,128)(2,1)S(1)}, u32[]{:S(2)}, u32[]{:S(2)}) collective-permute-start(bf16[192,768]{1,0:T(8,128)(2,1)S(1)} %fusion.9), channel_id=1, source_target_pairs={{0,8},{1,9},{2,10},{3,11},{4,12},{5,13},{6,14},{7,15},{8,0},{9,1},... | collective-permute-start | bytes 884744 | tf_op jit(solution)/shard_map/ppermute | solution.py:843
  249.6 20.9 %copy-start.7 = (bf16[2,192,768]{2,1,0:T(8,128)(2,1)S(1)}, bf16[2,192,768]{2,1,0:T(8,128)(2,1)}, u32[]{:S(2)}) copy-start(bf16[2,192,768]{2,1,0:T(8,128)(2,1)} %copy-done.6) | copy-start | bytes 1769476
  250.9 21.7 %copy-start.3 = (bf16[8,672,128]{2,1,0:T(8,128)(2,1)S(1)}, bf16[8,672,128]{2,1,0:T(8,128)(2,1)}, u32[]{:S(2)}) copy-start(bf16[8,672,128]{2,1,0:T(8,128)(2,1)} %get-tuple-element.260) | copy-start | bytes 4128772
  263.0 8.4 %copy-start.5 = (bf16[4,672,128]{2,1,0:T(8,128)(2,1)}, bf16[4,672,128]{2,1,0:T(8,128)(2,1)S(1)}, u32[]{:S(2)}) copy-start(bf16[4,672,128]{2,1,0:T(8,128)(2,1)S(1)} %collective-permute-done.21) | copy-start | bytes 2064388
  263.0 27.1 %collective-permute-start.24 = (bf16[4,768,128]{2,1,0:T(8,128)(2,1)}, bf16[4,768,128]{2,1,0:T(8,128)(2,1)S(1)}, u32[]{:S(2)}, u32[]{:S(2)}) collective-permute-start(bf16[4,768,128]{2,1,0:T(8,128)(2,1)} %get-tuple-element.271), channel_id=1, source_target_pairs={{0,2},{1,3},{2,0},{3,1},{4,6},{5,7},{6,4},{7,5},{8,10},{9,11},{10,... | collective-permute-start | bytes 2359304 | tf_op jit(solution)/shard_map/ppermute | solution.py:843
  265.0 34.5 %collective-permute-start.25 = (bf16[2,512,384]{2,1,0:T(8,128)(2,1)}, bf16[2,512,384]{2,1,0:T(8,128)(2,1)}, u32[]{:S(2)}, u32[]{:S(2)}) collective-permute-start(bf16[2,512,384]{2,1,0:T(8,128)(2,1)} %get-tuple-element.272), channel_id=1, source_target_pairs={{0,1},{1,2},{2,3},{3,4},{4,5},{5,6},{6,7},{7,8},{8,9},{9,10},{10,1... | collective-permute-start | bytes 2359304 | tf_op jit(solution)/shard_map/ppermute | solution.py:849
  268.0 31.5 %collective-permute-start.26 = (bf16[2,512,384]{2,1,0:T(8,128)(2,1)}, bf16[2,512,384]{2,1,0:T(8,128)(2,1)}, u32[]{:S(2)}, u32[]{:S(2)}) collective-permute-start(bf16[2,512,384]{2,1,0:T(8,128)(2,1)} %get-tuple-element.273), channel_id=1, source_target_pairs={{1,0},{2,1},{3,2},{4,3},{5,4},{6,5},{7,6},{8,7},{9,8},{10,9},{11,1... | collective-permute-start | bytes 2359304 | tf_op jit(solution)/shard_map/ppermute | solution.py:849
  271.6 3.4 %copy-start.8 = (bf16[2,24,1536]{2,1,0:T(8,128)(2,1)}, bf16[2,24,1536]{2,1,0:T(8,128)(2,1)S(1)}, u32[]{:S(2)}) copy-start(bf16[2,24,1536]{2,1,0:T(8,128)(2,1)S(1)} %reshape.415) | copy-start | bytes 442372
  272.3 6.2 %collective-permute-start.29 = (bf16[24,1536]{1,0:T(8,128)(2,1)}, bf16[24,1536]{1,0:T(8,128)(2,1)}, u32[]{:S(2)}, u32[]{:S(2)}) collective-permute-start(bf16[24,1536]{1,0:T(8,128)(2,1)} %dynamic-slice_bitcast_fusion), channel_id=1, source_target_pairs={{0,16},{16,0},{1,17},{17,1},{2,18},{18,2},{3,19},{19,3},{4,20},{20... | collective-permute-start | bytes 221192 | tf_op jit(solution)/shard_map/ppermute | solution.py:843
  275.0 32.3 %all-to-all-start = ((bf16[4,672,128]{2,1,0:T(8,128)(2,1)}), bf16[4,672,128]{2,1,0:T(8,128)(2,1)S(1)}, u32[]{:S(2)}, u32[]{:S(2)}) async-start(bf16[4,672,128]{2,1,0:T(8,128)(2,1)} %add_convert_fusion.1), calls=%async_computation | async-start | bytes 1376256 | tf_op jit(solution)/shard_map/all_to_all | solution.py:861
  307.0 9.2 %collective-permute-start.27 = (bf16[256,768]{1,0:T(8,128)(2,1)}, bf16[256,768]{1,0:T(8,128)(2,1)S(1)}, u32[]{:S(2)}, u32[]{:S(2)}) collective-permute-start(bf16[256,768]{1,0:T(8,128)(2,1)} %get-tuple-element.282), channel_id=1, source_target_pairs={{0,16},{16,0},{1,17},{17,1},{2,18},{18,2},{3,19},{19,3},{4,20},{20... | collective-permute-start | bytes 1179656 | tf_op jit(solution)/shard_map/ppermute | solution.py:843
  307.3 17.6 %all-to-all-start.1 = ((bf16[4,768,128]{2,1,0:T(8,128)(2,1)}), bf16[4,768,128]{2,1,0:T(8,128)(2,1)S(1)}, u32[]{:S(2)}, u32[]{:S(2)}) async-start(bf16[4,768,128]{2,1,0:T(8,128)(2,1)} %add_convert_fusion), calls=%async_computation.1 | async-start | bytes 1572864 | tf_op jit(solution)/shard_map/all_to_all | solution.py:861
  310.9 5.2 %copy-start.4 = (f32[256,768]{1,0:T(8,128)S(1)}, f32[256,768]{1,0:T(8,128)}, u32[]{:S(2)}) copy-start(f32[256,768]{1,0:T(8,128)} %get-tuple-element.281) | copy-start | bytes 2359300
  311.0 3.9 %collective-permute-start.28 = (bf16[216,128]{1,0:T(8,128)(2,1)S(1)}, bf16[216,128]{1,0:T(8,128)(2,1)S(1)}, u32[]{:S(2)}, u32[]{:S(2)}) collective-permute-start(bf16[216,128]{1,0:T(8,128)(2,1)S(1)} %bitcast.156), channel_id=1, source_target_pairs={{0,16},{16,0},{1,17},{17,1},{2,18},{18,2},{3,19},{19,3},{4,20},{20... | collective-permute-start | bytes 165896 | tf_op jit(solution)/shard_map/ppermute | solution.py:843
  317.1 8.4 %copy-start.2 = (f32[6,32,512]{2,1,0:T(8,128)S(1)}, f32[6,32,512]{2,1,0:T(8,128)}, u32[]{:S(2)}) copy-start(f32[6,32,512]{2,1,0:T(8,128)} %get-tuple-element.293) | copy-start | bytes 1179652
  317.1 8.4 %copy-start.14 = (f32[6]{0:T(128)S(1)}, f32[6]{0:T(128)}, u32[]{:S(2)}) copy-start(f32[6]{0:T(128)} %param.24) | copy-start | bytes 76
  (3 other events, 3.2 us)
Sparse Core Ops, SparseCore 0:
  22.3 56.8 all-gather.2
  81.5 58.2 all-gather.4

commit v2 on v1

--- a/solution.py
+++ b/solution.py
@@ -508,6 +508,7 @@
     unit1,
     rstd1,
     sums_in,
+    sums_more,
     smalls,
     owner,
     spread,
@@ -522,7 +523,7 @@
 ):
     copies = load_feed(wg, sem, wm)
     gain1 = spread_out(smalls[6], spread[...], owner[...], group[...])
-    sums[...] = sums_in[...]
+    sums[...] = sums_in[...] + sums_more[...]
     grad = base[...] + got[...].astype(F32)
     unit = unit1[...]
     sums[2:3, :] += column_sum(grad)
@@ -787,7 +788,7 @@
     )(scal, base, got, cot, cot_other, slope, smalls, owner, spread, group, wg)
 
 
-def feed_close(index, scal, base, got, unit1, rstd1, sums, smalls, owner, spread, group, wg):
+def feed_close(index, scal, base, got, unit1, rstd1, sums, more, smalls, owner, spread, group, wg):
     return pl.pallas_call(
         feed_close_kernel,
         name=f"feed_close_{index}",
@@ -797,12 +798,12 @@
             shape((HALF, OWN), BF),
             shape((16, D), F32),
         ),
-        in_specs=[SMEM] + [VM] * 9 + [HBM],
+        in_specs=[SMEM] + [VM] * 10 + [HBM],
         out_specs=[VM] * 4,
         scratch_shapes=[MERGE, pltpu.SemaphoreType.DMA((4,))],
         compiler_params=params(),
         cost_estimate=cost(4),
-    )(scal, base, got, unit1, rstd1, sums, smalls, owner, spread, group, wg)
+    )(scal, base, got, unit1, rstd1, sums, more, smalls, owner, spread, group, wg)
 
 
 def weight_grads(scal, *halves):
@@ -1064,8 +1065,8 @@
     down = lambda i, base, got, slope: feed_back(
         i, scal, base, got, cot, cot_other, slope, *params_of
     )
-    close = lambda i, base, got, unit, rstd, sums: feed_close(
-        i, scal, base, got, unit, rstd, sums, *params_of
+    close = lambda i, base, got, unit, rstd, sums, more: feed_close(
+        i, scal, base, got, unit, rstd, sums, more, *params_of
     )
     up0 = up(0)
     got0 = swap(up0[4], *SIDE)
@@ -1075,14 +1076,14 @@
     got0 = swap(down0[4], *SIDE)
     down1, got0 = tie(down(1, up1[3], got1, up1[6]), got0)
     got1 = swap(down1[4], *SIDE)
-    closed0 = close(0, down0[3], got0, up0[0], up0[1], down0[5] + down1[5])
+    closed0 = close(0, down0[3], got0, up0[0], up0[1], down0[5], down1[5])
     feed = weight_grads(
         scal, up0[5], down0[1], up0[2], down0[2], up1[5], down1[1], up1[2], down1[2]
     )
     closed0, feed, got1 = tie(closed0, feed, got1)
     if fast:
         feed_got = swap(by_core(feed[1]), *CORE)
-    closed1 = close(1, down1[3], got1, up1[0], up1[1], closed0[3])
+    closed1 = close(1, down1[3], got1, up1[0], up1[1], closed0[3], jnp.zeros((16, D), F32))
     if fast:
         closed1, feed_got = tie(closed1, feed_got)
         feed = sum_core(feed[0], feed_got)

time: 334 us -> 333 us (level)
  waiting for transfers between devices: 104 us -> 113 us
  Pallas kernels: 115 us -> 107 us
    ppermute x23, waiting for transfers between devices: 65.2 us -> 71.2 us  [swap(): return lax.ppermute(value, axis, [(i, i ^ bit) for i in range(count)])]
    pallas_call x1, Pallas kernels: 27.9 us -> 22.7 us  [attend(): pl.pallas_call(attend_kernel, name='attend', grid=(3,), out_shape=(shape(...]
    pallas_call x1, Pallas kernels: 27.3 us -> 23.8 us  [attend_back(): pl.pallas_call(partial(attend_back_kernel, len(before)), name=f'attend_ba...]
  transfers between devices with their start and end apart: 34 -> 34, of which waited for: 16 -> 16; matrix products, arithmetic and copies ran while one was open for 11% -> 11% of each run, Pallas kernels for 32% -> 30%
where the time goes in v2:
time: 333 us; the launch traced here: 332 us
  waiting for transfers between devices  113 us (34%)
  Pallas kernels  107 us (32%)
  starting transfers between devices  50.7 us (15%)
  local copies, waits for them, and re-layouts  24.2 us (7%)
  other arithmetic  23.1 us (7%)
  between operations  15 us (5%)
    ppermute x23, waiting for transfers between devices, swap(): return lax.ppermute(value, axis, [(i, i ^ bit) for i in range(count)])  71.2 us
    ppermute x23, starting transfers between devices, swap(): return lax.ppermute(value, axis, [(i, i ^ bit) for i in range(count)])  25.6 us
    pallas_call x1, Pallas kernels, attend_back(): pl.pallas_call(partial(attend_back_kernel, len(before)), name=f'attend_ba...  23.8 us
    pallas_call x1, Pallas kernels, attend(): pl.pallas_call(attend_kernel, name='attend', grid=(3,), out_shape=(shape(...  22.7 us
    all_gather x1, waiting for transfers between devices, per_device(): wg = lax.all_gather(shard, 'fsdp', axis=0, tiled=True).reshape(8, 2, 240, D)  15.8 us
    pallas_call x2, Pallas kernels, feed_back(): pl.pallas_call(partial(feed_back_kernel, index), name=f'feed_back_{index}...  15.1 us
    pallas_call x2, Pallas kernels, feed_up(): pl.pallas_call(feed_up_kernel, name=f'feed_up_{index}', grid=(1,), out_sh...  14.1 us
    ppermute x4, starting transfers between devices, shifted(): lax.ppermute(value, axis, [(source, source + steps) for source in range(l...  10.5 us
  transfers between devices with their start and end apart: 34, of which 16 were waited for; matrix products, arithmetic and copies ran while one was open for 11% of the time, Pallas kernels for 30%

profile of v2, /device:TPU:1, one launch (start us, length us, event | category | flops | bytes accessed | tf_op | source)
XLA Modules:
  0.0 332.4 jit_solution(3455191819222003726)
XLA Ops:
  7.3 0.9 reshape.392
  8.9 1.3 collective-permute-start.8
  10.2 4.5 %collective-permute-start.10 = (bf16[24,1152]{1,0:T(8,128)(2,1)S(1)}, bf16[24,1152]{1,0:T(8,128)(2,1)S(1)}, u32[]{:S(2)}, u32[]{:S(2)}) collective-permute-start(bf16[24,1152]{1,0:T(8,128)(2,1)S(1)} %bitcast.158), channel_id=1, source_target_pairs={{1,16},{3,18},{5,20},{7,22},{9,24},{11,26},{13,28},{15,30},{16,1},... | collective-permute-start | bytes 165896 | tf_op jit(solution)/shard_map/ppermute | solution.py:915
  14.8 1.7 collective-permute-start.9
  16.4 2.1 fusion.29
  18.9 3.2 concatenate.46
  22.3 3.1 collective-permute-start.1
  25.4 1.9 collective-permute-start.2
  27.8 1.1 collective-permute-start.5
  30.2 5.5 %collective-permute-done.5 = bf16[1,24,2304]{2,1,0:T(8,128)(2,1)S(1)} collective-permute-done((bf16[1,24,2304]{2,1,0:T(8,128)(2,1)S(1)}, bf16[1,24,2304]{2,1,0:T(8,128)(2,1)S(1)}, u32[]{:S(2)}, u32[]{:S(2)}) %collective-permute-start.5) | collective-permute-done | bytes 110624 | tf_op jit(solution)/shard_map/ppermute | solution.py:844
  37.4 3.3 stack.15.scal
  41.1 1.1 collective-permute-start.4
  43.1 8.0 %collective-permute-done.3.y0 = bf16[256,768]{1,0:T(8,128)(2,1)S(1)} collective-permute-done((bf16[256,768]{1,0:T(8,128)(2,1)S(1)}, bf16[256,768]{1,0:T(8,128)(2,1)S(1)}, u32[]{:S(2)}, u32[]{:S(2)}) %collective-permute-start.3) | collective-permute-done | bytes 393248 | tf_op jit(solution)/shard_map/ppermute | solution.py:844
  51.1 8.5 %collective-permute-done.4.y2 = bf16[256,768]{1,0:T(8,128)(2,1)S(1)} collective-permute-done((bf16[256,768]{1,0:T(8,128)(2,1)S(1)}, bf16[256,768]{1,0:T(8,128)(2,1)S(1)}, u32[]{:S(2)}, u32[]{:S(2)}) %collective-permute-start.4) | collective-permute-done | bytes 393248 | tf_op jit(solution)/shard_map/ppermute | solution.py:844
  62.4 1.1 reshape.431.pos_col
  64.1 1.1 reshape.432.doc_col
  65.9 4.5 %collective-permute-done.7.cot_other = bf16[256,768]{1,0:T(8,128)(2,1)S(1)} collective-permute-done((bf16[256,768]{1,0:T(8,128)(2,1)S(1)}, bf16[256,768]{1,0:T(8,128)(2,1)S(1)}, u32[]{:S(2)}, u32[]{:S(2)}) %collective-permute-start.7) | collective-permute-done | bytes 393248 | tf_op jit(solution)/shard_map/ppermute | solution.py:844
  70.4 8.8 %all-gather.3.cloned.1.call-done = bf16[19968,128]{1,0:T(8,128)(2,1)} async-done(((bf16[1248,128]{1,0:T(8,128)(2,1)}), bf16[19968,128]{1,0:T(8,128)(2,1)}) %all-gather.3.cloned.1.call-update) | async-done | bytes 5111824 | tf_op jit(solution)/shard_map/all_gather | solution.py:1014
  80.7 1.2 collective-permute-start.11
  82.5 8.9 %project.1 = (bf16[512,384]{1,0:T(8,128)(2,1)}, bf16[1536,384]{1,0:T(8,128)(2,1)}, bf16[1536,384]{1,0:T(8,128)(2,1)}, bf16[1536,768]{1,0:T(8,128)(2,1)}, bf16[6,...) custom-call(s32[8]{0:T(128)} %stack.15.scal, bf16[256,768]{1,0:T(8,128)(2,1)} %bitcast.170, bf16[256,768]{1,0:T(8,128)(2,1)} %copy-done.19, ...), custom_call_target="tpu_custom_call" | custom-call | flops 10350000128 | bytes 1000 | tf_op jit(solution)/shard_map/project/pallas_call | solution.py:597
  91.4 22.7 %attend.1 = (bf16[2,256,384]{2,1,0:T(8,128)(2,1)}, f32[3,8,512]{2,1,0:T(8,128)}, bf16[3,2,6,256,512]{4,3,2,1,0:T(8,128)(2,1)}, bf16[3,2,6,256,512]{4,3,2,1,0:T(8,128)(2,1)}, bf16[6,512,256]{2,1,0:T(8,128)(2,1)}) custom-call(s32[8]{0:T(128)} %stack.15.scal, s32[1536,1]{1,0:T(8,128)} %reshape.431.pos_col, s32[6,1,256]{2,1,0:T(1,128)} %reshape.400.pos_row, ...), custom_call_target="tpu_custom_call" | custom-call | flops 29899999232 | bytes 1000 | tf_op jit(solution)/shard_map/attend/pallas_call | solution.py:624
  116.7 7.4 %collective-permute-done.12.ctx_other = bf16[2,256,384]{2,1,0:T(8,128)(2,1)S(1)} collective-permute-done((bf16[2,256,384]{2,1,0:T(8,128)(2,1)}, bf16[2,256,384]{2,1,0:T(8,128)(2,1)S(1)}, u32[]{:S(2)}, u32[]{:S(2)}) %collective-permute-start.12) | collective-permute-done | bytes 393248 | tf_op jit(solution)/shard_map/ppermute | solution.py:844
  124.1 15.8 %all-gather.5.cloned.1.call-done = bf16[3840,768]{1,0:T(8,128)(2,1)} async-done(((bf16[240,768]{1,0:T(8,128)(2,1)}), bf16[3840,768]{1,0:T(8,128)(2,1)}) %all-gather.5.cloned.1.call-update) | async-done | bytes 5898256 | tf_op jit(solution)/shard_map/all_gather | solution.py:1021
  140.4 7.0 %feed_up_0.1 = (f32[256,768]{1,0:T(8,128)}, f32[256,128]{1,0:T(8,128)}, bf16[256,768]{1,0:T(8,128)(2,1)}, f32[256,768]{1,0:T(8,128)}, bf16[256,768]{1,0:T(8,128)...) custom-call(s32[8]{0:T(128)} %stack.15.scal, bf16[1536,768]{1,0:T(8,128)(2,1)} %get-tuple-element.156.x, ...), custom_call_target="tpu_custom_call" | custom-call | flops 9200000000 | bytes 1000 | tf_op jit(solution)/shard_map/feed_up_0/pallas_call | solution.py:749
  147.5 1.2 collective-permute-start.13
  149.3 7.1 %feed_up_1.1 = (f32[256,768]{1,0:T(8,128)}, f32[256,128]{1,0:T(8,128)}, bf16[256,768]{1,0:T(8,128)(2,1)}, f32[256,768]{1,0:T(8,128)}, bf16[256,768]{1,0:T(8,128)...) custom-call(s32[8]{0:T(128)} %stack.15.scal, bf16[1536,768]{1,0:T(8,128)(2,1)} %get-tuple-element.156.x, ...), custom_call_target="tpu_custom_call" | custom-call | flops 9200000000 | bytes 1000 | tf_op jit(solution)/shard_map/feed_up_1/pallas_call | solution.py:749
  156.4 1.8 collective-permute-done.13.got
  158.2 1.2 collective-permute-start.14
  159.4 7.5 %feed_back_0.1 = (bf16[256,768]{1,0:T(8,128)(2,1)}, bf16[256,768]{1,0:T(8,128)(2,1)}, bf16[2,256,768]{2,1,0:T(8,128)(2,1)}, f32[256,768]{1,0:T(8,128)}, bf16[256,768]{1,0:T(8,128)(2,1)}, /*index=5*/f32[16,768]{1,0:T(8,128)}) custom-call(s32[8]{0:T(128)} %stack.15.scal, f32[256,768]{1,0:T(8,128)} %get-tuple-element.166.base, bf16[256,768]{1,0:T(8,128)(2,1)} %copy-done.27, ...), custom_call_target="tpu_custom_call" | custom-call | flops 8049999872 | bytes 1000 | tf_op jit(solution)/shard_map/feed_back_0/pallas_call | solution.py:772
  166.9 1.1 collective-permute-done.14.got
  168.0 1.2 collective-permute-start.15
  169.2 7.7 %feed_back_1.1 = (bf16[256,768]{1,0:T(8,128)(2,1)}, bf16[256,768]{1,0:T(8,128)(2,1)}, bf16[2,256,768]{2,1,0:T(8,128)(2,1)}, f32[256,768]{1,0:T(8,128)}, bf16[256,768]{1,0:T(8,128)(2,1)}, /*index=5*/f32[16,768]{1,0:T(8,128)}) custom-call(s32[8]{0:T(128)} %stack.15.scal, f32[256,768]{1,0:T(8,128)} %get-tuple-element.186.base, bf16[256,768]{1,0:T(8,128)(2,1)} %copy-done.28, ...), custom_call_target="tpu_custom_call" | custom-call | flops 8049999872 | bytes 1000 | tf_op jit(solution)/shard_map/feed_back_1/pallas_call | solution.py:772
  176.9 1.1 collective-permute-start.16
  178.0 7.3 %weight_grads.1 = (bf16[8,192,768]{2,1,0:T(8,128)(2,1)}, bf16[8,192,768]{2,1,0:T(8,128)(2,1)}) custom-call(s32[8]{0:T(128)} %stack.15.scal, bf16[2,256,768]{2,1,0:T(8,128)(2,1)} %get-tuple-element.213.act0, bf16[256,768]{1,0:T(8,128)(2,1)} %get-tuple-element.214.ddown0, bf16[256,768]{1,0:T(8,128)(2,1)} %get-tuple-element.215.nlow0, ...), custom_call_target="tpu_custom_call" | custom-call | flops 8049999872 | bytes 1000 | tf_op jit(solution)/shard_map/weight_grads/pallas_call | solution.py:810
  185.3 4.0 %feed_close_0.1 = (f32[256,768]{1,0:T(8,128)}, bf16[256,768]{1,0:T(8,128)(2,1)}, bf16[256,384]{1,0:T(8,128)(2,1)}, f32[16,768]{1,0:T(8,128)}) custom-call(s32[8]{0:T(128)} %stack.15.scal, f32[256,768]{1,0:T(8,128)} %get-tuple-element.203.base, bf16[256,768]{1,0:T(8,128)(2,1)} %copy-done.26, f32[256,768]{1,0:T(8,128)} %get-tuple-element.205.unit1, ...), custom_call_target="tpu_custom_call" | custom-call | flops 4600000000 | bytes 1000 | tf_op jit(solution)/shard_map/feed_close_0/pallas_call | solution.py:792
  189.4 3.2 collective-permute-start.17
  193.3 4.2 %feed_close_1.1 = (f32[256,768]{1,0:T(8,128)}, bf16[256,768]{1,0:T(8,128)(2,1)}, bf16[256,384]{1,0:T(8,128)(2,1)}, f32[16,768]{1,0:T(8,128)}) custom-call(s32[8]{0:T(128)} %stack.15.scal, f32[256,768]{1,0:T(8,128)} %get-tuple-element.202.base, bf16[256,768]{1,0:T(8,128)(2,1)} %copy-done.24, f32[256,768]{1,0:T(8,128)} %get-tuple-element.225.unit1, ...), custom_call_target="tpu_custom_call" | custom-call | flops 4600000000 | bytes 1000 | tf_op jit(solution)/shard_map/feed_close_1/pallas_call | solution.py:792
  197.5 3.3 fusion
  201.1 23.8 %attend_back_0.1 = (bf16[512,384]{1,0:T(8,128)(2,1)}, f32[2,512,384]{2,1,0:T(8,128)}, bf16[2,512,384]{2,1,0:T(8,128)(2,1)}, bf16[2,512,384]{2,1,0:T(8,128)(2,1)}...) custom-call(s32[8]{0:T(128)} %stack.15.scal, ...), custom_call_target="tpu_custom_call" | custom-call | flops 34500001792 | bytes 1000 | tf_op jit(solution)/shard_map/attend_back_0/pallas_call | solution.py:672
  224.8 3.7 %collective-permute-done.18 = bf16[4,192,768]{2,1,0:T(8,128)(2,1)S(1)} collective-permute-done((bf16[4,192,768]{2,1,0:T(8,128)(2,1)}, bf16[4,192,768]{2,1,0:T(8,128)(2,1)S(1)}, u32[]{:S(2)}, u32[]{:S(2)}) %collective-permute-start.18) | collective-permute-done | bytes 1179680 | tf_op jit(solution)/shard_map/ppermute | solution.py:844
  228.8 0.9 collective-permute-start.20
  229.8 1.2 collective-permute-start.22
  231.0 4.0 %collective-permute-done.19 = bf16[2,4,672,128]{3,2,1,0:T(8,128)(2,1)} collective-permute-done((bf16[2,4,672,128]{3,2,1,0:T(8,128)(2,1)}, bf16[2,4,672,128]{3,2,1,0:T(8,128)(2,1)}, u32[]{:S(2)}, u32[]{:S(2)}) %collective-permute-start.19) | collective-permute-done | bytes 1376288 | tf_op jit(solution)/shard_map/ppermute | solution.py:844
  235.1 1.5 fusion.5
  236.5 2.6 collective-permute-start.21
  240.0 4.3 %collective-permute-done.22 = bf16[2,192,768]{2,1,0:T(8,128)(2,1)S(1)} collective-permute-done((bf16[2,192,768]{2,1,0:T(8,128)(2,1)S(1)}, bf16[2,192,768]{2,1,0:T(8,128)(2,1)S(1)}, u32[]{:S(2)}, u32[]{:S(2)}) %collective-permute-start.22) | collective-permute-done | bytes 589856 | tf_op jit(solution)/shard_map/ppermute | solution.py:844
  245.1 3.2 collective-permute-start.23
  248.3 1.3 fusion.2
  249.6 12.4 %collective-permute-done.23 = bf16[192,768]{1,0:T(8,128)(2,1)S(1)} collective-permute-done((bf16[192,768]{1,0:T(8,128)(2,1)S(1)}, bf16[192,768]{1,0:T(8,128)(2,1)S(1)}, u32[]{:S(2)}, u32[]{:S(2)}) %collective-permute-start.23) | collective-permute-done | bytes 294944 | tf_op jit(solution)/shard_map/ppermute | solution.py:844
  262.0 2.2 collective-permute-start.24
  264.2 2.3 collective-permute-start.25
  266.5 3.2 collective-permute-start.26
  271.8 2.4 add_convert_fusion.1
  274.2 3.5 %all-to-all-start = ((bf16[4,672,128]{2,1,0:T(8,128)(2,1)}), bf16[4,672,128]{2,1,0:T(8,128)(2,1)S(1)}, u32[]{:S(2)}, u32[]{:S(2)}) async-start(bf16[4,672,128]{2,1,0:T(8,128)(2,1)} %add_convert_fusion.1), calls=%async_computation | async-start | bytes 1376256 | tf_op jit(solution)/shard_map/all_to_all | solution.py:862
  277.7 0.9 bitcast_select_fusion.3
  279.4 10.0 %collective-permute-done.24 = bf16[4,768,128]{2,1,0:T(8,128)(2,1)S(1)} collective-permute-done((bf16[4,768,128]{2,1,0:T(8,128)(2,1)}, bf16[4,768,128]{2,1,0:T(8,128)(2,1)S(1)}, u32[]{:S(2)}, u32[]{:S(2)}) %collective-permute-start.24) | collective-permute-done | bytes 786464 | tf_op jit(solution)/shard_map/ppermute | solution.py:844
  289.3 9.4 %collective-permute-done.25.refs_2_ = bf16[2,512,384]{2,1,0:T(8,128)(2,1)} collective-permute-done((bf16[2,512,384]{2,1,0:T(8,128)(2,1)}, bf16[2,512,384]{2,1,0:T(8,128)(2,1)}, u32[]{:S(2)}, u32[]{:S(2)}) %collective-permute-start.25) | collective-permute-done | bytes 786464 | tf_op jit(solution)/shard_map/ppermute | solution.py:850
  298.7 1.1 add_convert_fusion
  299.8 6.3 %project_back.1 = (f32[256,768]{1,0:T(8,128)}, bf16[256,768]{1,0:T(8,128)(2,1)}) custom-call(s32[8]{0:T(128)} %stack.15.scal, bf16[512,384]{1,0:T(8,128)(2,1)} %get-tuple-element.258.refs_0_, f32[2,512,384]{2,1,0:T(8,128)} %get-tuple-element.259.refs_1_, bf16[2,512,384]{2,1,0:T(8,128)(2,1)} %collective-permute-done.25.refs_2_, ...), custom_call_target="tpu_custom_call" | custom-call | flops 6899999744 | bytes 1000 | tf_op jit(solution)/shard_map/project_back/pallas_call | solution.py:826
  306.5 3.5 %all-to-all-start.1 = ((bf16[4,768,128]{2,1,0:T(8,128)(2,1)}), bf16[4,768,128]{2,1,0:T(8,128)(2,1)S(1)}, u32[]{:S(2)}, u32[]{:S(2)}) async-start(bf16[4,768,128]{2,1,0:T(8,128)(2,1)} %add_convert_fusion), calls=%async_computation.1 | async-start | bytes 1572864 | tf_op jit(solution)/shard_map/all_to_all | solution.py:862
  310.2 1.2 collective-permute-start.28
  314.4 0.9 reshape.423
  315.3 1.0 add_bitcast_fusion
  316.3 7.8 %all-to-all-done.1 = bf16[4,768,128]{2,1,0:T(8,128)(2,1)S(1)} async-done(((bf16[4,768,128]{2,1,0:T(8,128)(2,1)}), bf16[4,768,128]{2,1,0:T(8,128)(2,1)S(1)}, u32[]{:S(2)}, u32[]{:S(2)}) %all-to-all-start.1) | async-done | bytes 786464 | tf_op jit(solution)/shard_map/all_to_all | solution.py:862
  (199 shorter events, 26.1 us)
Async XLA Ops:
  7.2 11.4 %copy-start.14 = (bf16[6,24]{1,0:T(8,128)(2,1)S(1)}, bf16[6,24]{1,0:T(8,128)(2,1)}, u32[]{:S(2)}) copy-start(bf16[6,24]{1,0:T(8,128)(2,1)} %param.19) | copy-start | bytes 868
  7.2 11.5 %copy-start.29 = (bf16[2,24]{1,0:T(2,128)(2,1)S(1)}, bf16[2,24]{1,0:T(2,128)(2,1)}, u32[]{:S(2)}) copy-start(bf16[2,24]{1,0:T(2,128)(2,1)} %param.20) | copy-start | bytes 292
  7.2 11.5 %copy-start.30 = (bf16[96]{0:T(256)(128)(2,1)S(1)}, bf16[96]{0:T(256)(128)(2,1)}, u32[]{:S(2)}) copy-start(bf16[96]{0:T(256)(128)(2,1)} %param.21) | copy-start | bytes 580
  7.2 72.0 %all-gather.3.cloned.1.call-start = ((), (), s32[]{:S(2)}) async-start(), calls=%async_computation.2 | async-start | bytes 5431296 | tf_op jit(solution)/shard_map/all_gather | solution.py:1014
  8.9 9.8 %collective-permute-start.8 = (bf16[24,1152]{1,0:T(8,128)(2,1)S(1)}, bf16[24,1152]{1,0:T(8,128)(2,1)S(1)}, u32[]{:S(2)}, u32[]{:S(2)}) collective-permute-start(bf16[24,1152]{1,0:T(8,128)(2,1)S(1)} %bitcast.157), channel_id=1, source_target_pairs={{0,16},{2,18},{4,20},{6,22},{8,24},{10,26},{12,28},{14,30},{17,1},... | collective-permute-start | bytes 165896 | tf_op jit(solution)/shard_map/ppermute | solution.py:914
  10.2 8.5 %collective-permute-start.10 = (bf16[24,1152]{1,0:T(8,128)(2,1)S(1)}, bf16[24,1152]{1,0:T(8,128)(2,1)S(1)}, u32[]{:S(2)}, u32[]{:S(2)}) collective-permute-start(bf16[24,1152]{1,0:T(8,128)(2,1)S(1)} %bitcast.158), channel_id=1, source_target_pairs={{1,16},{3,18},{5,20},{7,22},{9,24},{11,26},{13,28},{15,30},{16,1},... | collective-permute-start | bytes 165896 | tf_op jit(solution)/shard_map/ppermute | solution.py:915
  14.8 4.0 %collective-permute-start.9 = (bf16[24,1152]{1,0:T(8,128)(2,1)S(1)}, bf16[24,1152]{1,0:T(8,128)(2,1)S(1)}, u32[]{:S(2)}, u32[]{:S(2)}) collective-permute-start(bf16[24,1152]{1,0:T(8,128)(2,1)S(1)} %bitcast.150), channel_id=1, source_target_pairs={{1,0},{3,2},{5,4},{7,6},{9,8},{11,10},{13,12},{15,14},{16,17},{18,... | collective-permute-start | bytes 165896 | tf_op jit(solution)/shard_map/ppermute | solution.py:915
  18.5 3.7 %copy-start.16 = (bf16[1,256,768]{2,1,0:T(8,128)(2,1)S(1)}, bf16[1,256,768]{2,1,0:T(8,128)(2,1)}, u32[]{:S(2)}) copy-start(bf16[1,256,768]{2,1,0:T(8,128)(2,1)} %param.14) | copy-start | bytes 1179652
  18.5 8.8 %copy-start.10 = (bf16[24,3072]{1,0:T(8,128)(2,1)S(1)}, bf16[24,3072]{1,0:T(8,128)(2,1)}, u32[]{:S(2)}) copy-start(bf16[24,3072]{1,0:T(8,128)(2,1)} %param.17) | copy-start | bytes 442372
  18.7 9.1 %copy-start.11 = (bf16[24,768]{1,0:T(8,128)(2,1)S(1)}, bf16[24,768]{1,0:T(8,128)(2,1)}, u32[]{:S(2)}) copy-start(bf16[24,768]{1,0:T(8,128)(2,1)} %param.16) | copy-start | bytes 110596
  18.8 10.2 %copy-start.15 = (s32[32]{0:T(128)S(1)}, s32[32]{0:T(128)}, u32[]{:S(2)}) copy-start(s32[32]{0:T(128)} %param.25) | copy-start | bytes 388
  18.8 10.5 %copy-start.31 = (s32[4]{0:T(128)S(1)}, s32[4]{0:T(128)}, u32[]{:S(2)}) copy-start(s32[4]{0:T(128)} %constant.177.clone) | copy-start | bytes 52
  22.2 117.7 %all-gather.5.cloned.1.call-start = ((), (), s32[]{:S(2)}) async-start(), calls=%async_computation.3 | async-start | bytes 6266880 | tf_op jit(solution)/shard_map/all_gather | solution.py:1021
  22.2 18.4 %collective-permute-start = (bf16[256,768]{1,0:T(8,128)(2,1)S(1)}, bf16[256,768]{1,0:T(8,128)(2,1)S(1)}, u32[]{:S(2)}, u32[]{:S(2)}) collective-permute-start(bf16[256,768]{1,0:T(8,128)(2,1)S(1)} %bitcast.171), channel_id=1, source_target_pairs={{0,16},{16,0},{1,17},{17,1},{2,18},{18,2},{3,19},{19,3},{4,20},{20... | collective-permute-start | bytes 1179656 | tf_op jit(solution)/shard_map/ppermute | solution.py:844
  22.3 18.4 %collective-permute-start.1 = (bf16[256,768]{1,0:T(8,128)(2,1)S(1)}, bf16[256,768]{1,0:T(8,128)(2,1)S(1)}, u32[]{:S(2)}, u32[]{:S(2)}) collective-permute-start(bf16[256,768]{1,0:T(8,128)(2,1)S(1)} %bitcast.172), channel_id=1, source_target_pairs={{0,1},{1,2},{2,3},{3,4},{4,5},{5,6},{6,7},{7,8},{8,9},{9,10},{10,1... | collective-permute-start | bytes 1179656 | tf_op jit(solution)/shard_map/ppermute | solution.py:850
  25.4 15.3 %collective-permute-start.2 = (bf16[256,768]{1,0:T(8,128)(2,1)S(1)}, bf16[256,768]{1,0:T(8,128)(2,1)S(1)}, u32[]{:S(2)}, u32[]{:S(2)}) collective-permute-start(bf16[256,768]{1,0:T(8,128)(2,1)S(1)} %bitcast.173), channel_id=1, source_target_pairs={{1,0},{2,1},{3,2},{4,3},{5,4},{6,5},{7,6},{8,7},{9,8},{10,9},{11,1... | collective-permute-start | bytes 1179656 | tf_op jit(solution)/shard_map/ppermute | solution.py:850
  27.8 7.9 %collective-permute-start.5 = (bf16[1,24,2304]{2,1,0:T(8,128)(2,1)S(1)}, bf16[1,24,2304]{2,1,0:T(8,128)(2,1)S(1)}, u32[]{:S(2)}, u32[]{:S(2)}) collective-permute-start(bf16[1,24,2304]{2,1,0:T(8,128)(2,1)S(1)} %fusion.14), channel_id=1, source_target_pairs={{0,16},{16,0},{1,17},{17,1},{2,18},{18,2},{3,19},{19,3},{4,20},{20... | collective-permute-start | bytes 331784 | tf_op jit(solution)/shard_map/ppermute | solution.py:844
  35.9 6.5 %copy-start.12 = (bf16[96,768]{1,0:T(8,128)(2,1)S(1)}, bf16[96,768]{1,0:T(8,128)(2,1)}, u32[]{:S(2)}) copy-start(bf16[96,768]{1,0:T(8,128)(2,1)} %param.18) | copy-start | bytes 442372
  36.6 24.3 %copy-start.17 = (bf16[1,256,768]{2,1,0:T(8,128)(2,1)S(1)}, bf16[1,256,768]{2,1,0:T(8,128)(2,1)}, u32[]{:S(2)}) copy-start(bf16[1,256,768]{2,1,0:T(8,128)(2,1)} %param.26) | copy-start | bytes 1179652
  36.6 5.6 %collective-permute-start.6 = (bf16[2,24,1152]{2,1,0:T(8,128)(2,1)S(1)}, bf16[2,24,1152]{2,1,0:T(8,128)(2,1)S(1)}, u32[]{:S(2)}, u32[]{:S(2)}) collective-permute-start(bf16[2,24,1152]{2,1,0:T(8,128)(2,1)S(1)} %bitcast.153), channel_id=1, source_target_pairs={{0,1},{1,0},{2,3},{3,2},{4,5},{5,4},{6,7},{7,6},{8,9},{9,8},{10,11... | collective-permute-start | bytes 331784 | tf_op jit(solution)/shard_map/ppermute | solution.py:844
  40.7 22.9 %copy-start.18 = (bf16[256,768]{1,0:T(8,128)(2,1)}, bf16[256,768]{1,0:T(8,128)(2,1)S(1)}, u32[]{:S(2)}) copy-start(bf16[256,768]{1,0:T(8,128)(2,1)S(1)} %collective-permute-done.y1) | copy-start | bytes 1179652
  40.7 22.9 %copy-start.19 = (bf16[256,768]{1,0:T(8,128)(2,1)}, bf16[256,768]{1,0:T(8,128)(2,1)S(1)}, u32[]{:S(2)}) copy-start(bf16[256,768]{1,0:T(8,128)(2,1)S(1)} %collective-permute-done.1.x0) | copy-start | bytes 1179652
  40.7 22.8 %copy-start.20 = (bf16[256,768]{1,0:T(8,128)(2,1)}, bf16[256,768]{1,0:T(8,128)(2,1)S(1)}, u32[]{:S(2)}) copy-start(bf16[256,768]{1,0:T(8,128)(2,1)S(1)} %collective-permute-done.2.x2) | copy-start | bytes 1179652
  40.7 10.4 %collective-permute-start.3 = (bf16[256,768]{1,0:T(8,128)(2,1)S(1)}, bf16[256,768]{1,0:T(8,128)(2,1)S(1)}, u32[]{:S(2)}, u32[]{:S(2)}) collective-permute-start(bf16[256,768]{1,0:T(8,128)(2,1)S(1)} %collective-permute-done.1.x0), channel_id=1, source_target_pairs={{0,16},{16,0},{1,17},{17,1},{2,18},{18,2},{3,19},{19,3},{4,20},{20... | collective-permute-start | bytes 1179656 | tf_op jit(solution)/shard_map/ppermute | solution.py:844
  41.1 18.5 %collective-permute-start.4 = (bf16[256,768]{1,0:T(8,128)(2,1)S(1)}, bf16[256,768]{1,0:T(8,128)(2,1)S(1)}, u32[]{:S(2)}, u32[]{:S(2)}) collective-permute-start(bf16[256,768]{1,0:T(8,128)(2,1)S(1)} %collective-permute-done.2.x2), channel_id=1, source_target_pairs={{0,16},{16,0},{1,17},{17,1},{2,18},{18,2},{3,19},{19,3},{4,20},{20... | collective-permute-start | bytes 1179656 | tf_op jit(solution)/shard_map/ppermute | solution.py:844
  51.1 31.4 %copy-start.22 = (bf16[256,768]{1,0:T(8,128)(2,1)}, bf16[256,768]{1,0:T(8,128)(2,1)S(1)}, u32[]{:S(2)}) copy-start(bf16[256,768]{1,0:T(8,128)(2,1)S(1)} %collective-permute-done.3.y0) | copy-start | bytes 1179652
  59.6 22.9 %copy-start.23 = (bf16[256,768]{1,0:T(8,128)(2,1)}, bf16[256,768]{1,0:T(8,128)(2,1)S(1)}, u32[]{:S(2)}) copy-start(bf16[256,768]{1,0:T(8,128)(2,1)S(1)} %collective-permute-done.4.y2) | copy-start | bytes 1179652
  60.9 9.5 %collective-permute-start.7 = (bf16[256,768]{1,0:T(8,128)(2,1)S(1)}, bf16[256,768]{1,0:T(8,128)(2,1)S(1)}, u32[]{:S(2)}, u32[]{:S(2)}) collective-permute-start(bf16[256,768]{1,0:T(8,128)(2,1)S(1)} %bitcast.176), channel_id=1, source_target_pairs={{0,16},{16,0},{1,17},{17,1},{2,18},{18,2},{3,19},{19,3},{4,20},{20... | collective-permute-start | bytes 1179656 | tf_op jit(solution)/shard_map/ppermute | solution.py:844
  70.4 21.0 %copy-start.21 = (bf16[256,768]{1,0:T(8,128)(2,1)}, bf16[256,768]{1,0:T(8,128)(2,1)S(1)}, u32[]{:S(2)}) copy-start(bf16[256,768]{1,0:T(8,128)(2,1)S(1)} %collective-permute-done.7.cot_other) | copy-start | bytes 1179652
  80.7 10.7 %collective-permute-start.11 = (bf16[16,16,128]{2,0,1:T(8,128)(2,1)S(1)}, bf16[16,16,128]{2,0,1:T(8,128)(2,1)S(1)}, u32[]{:S(2)}, u32[]{:S(2)}) collective-permute-start(bf16[16,16,128]{2,0,1:T(8,128)(2,1)S(1)} %slice_bitcast_fusion), channel_id=1, source_target_pairs={{0,16},{16,0},{1,17},{17,1},{2,18},{18,2},{3,19},{19,3},{4,20},{20... | collective-permute-start | bytes 196616 | tf_op jit(solution)/shard_map/ppermute | solution.py:844
  114.2 9.9 %collective-permute-start.12 = (bf16[2,256,384]{2,1,0:T(8,128)(2,1)}, bf16[2,256,384]{2,1,0:T(8,128)(2,1)S(1)}, u32[]{:S(2)}, u32[]{:S(2)}) collective-permute-start(bf16[2,256,384]{2,1,0:T(8,128)(2,1)} %get-tuple-element.163.ctx_mine.ctx.ctx_all), channel_id=1, source_target_pairs={{0,16},{16,0},{1,17},{17,1},{2,18},{18,2},{3,19},{19,3},{4,20},{20... | collective-permute-start | bytes 1179656 | tf_op jit(solution)/shard_map/ppermute | solution.py:844
  124.1 16.4 %copy-start.25 = (bf16[2,256,384]{2,1,0:T(8,128)(2,1)}, bf16[2,256,384]{2,1,0:T(8,128)(2,1)S(1)}, u32[]{:S(2)}) copy-start(bf16[2,256,384]{2,1,0:T(8,128)(2,1)S(1)} %collective-permute-done.12.ctx_other) | copy-start | bytes 1179652
  147.5 10.7 %collective-permute-start.13 = (bf16[256,768]{1,0:T(8,128)(2,1)}, bf16[256,768]{1,0:T(8,128)(2,1)S(1)}, u32[]{:S(2)}, u32[]{:S(2)}) collective-permute-start(bf16[256,768]{1,0:T(8,128)(2,1)} %get-tuple-element.174), channel_id=1, source_target_pairs={{0,16},{16,0},{1,17},{17,1},{2,18},{18,2},{3,19},{19,3},{4,20},{20... | collective-permute-start | bytes 1179656 | tf_op jit(solution)/shard_map/ppermute | solution.py:844
  158.2 1.2 copy-start.27
  158.2 9.8 %collective-permute-start.14 = (bf16[256,768]{1,0:T(8,128)(2,1)}, bf16[256,768]{1,0:T(8,128)(2,1)S(1)}, u32[]{:S(2)}, u32[]{:S(2)}) collective-permute-start(bf16[256,768]{1,0:T(8,128)(2,1)} %get-tuple-element.184), channel_id=1, source_target_pairs={{0,16},{16,0},{1,17},{17,1},{2,18},{18,2},{3,19},{19,3},{4,20},{20... | collective-permute-start | bytes 1179656 | tf_op jit(solution)/shard_map/ppermute | solution.py:844
  168.0 8.9 %collective-permute-start.15 = (bf16[256,768]{1,0:T(8,128)(2,1)}, bf16[256,768]{1,0:T(8,128)(2,1)S(1)}, u32[]{:S(2)}, u32[]{:S(2)}) collective-permute-start(bf16[256,768]{1,0:T(8,128)(2,1)} %get-tuple-element.195), channel_id=1, source_target_pairs={{0,16},{16,0},{1,17},{17,1},{2,18},{18,2},{3,19},{19,3},{4,20},{20... | collective-permute-start | bytes 1179656 | tf_op jit(solution)/shard_map/ppermute | solution.py:844
  176.9 8.5 %copy-start.26 = (bf16[256,768]{1,0:T(8,128)(2,1)}, bf16[256,768]{1,0:T(8,128)(2,1)S(1)}, u32[]{:S(2)}) copy-start(bf16[256,768]{1,0:T(8,128)(2,1)S(1)} %collective-permute-done.15.got) | copy-start | bytes 1179652
  176.9 12.5 %collective-permute-start.16 = (bf16[256,768]{1,0:T(8,128)(2,1)}, bf16[256,768]{1,0:T(8,128)(2,1)S(1)}, u32[]{:S(2)}, u32[]{:S(2)}) collective-permute-start(bf16[256,768]{1,0:T(8,128)(2,1)} %get-tuple-element.223), channel_id=1, source_target_pairs={{0,16},{16,0},{1,17},{17,1},{2,18},{18,2},{3,19},{19,3},{4,20},{20... | collective-permute-start | bytes 1179656 | tf_op jit(solution)/shard_map/ppermute | solution.py:844
  189.4 3.9 %copy-start.24 = (bf16[256,768]{1,0:T(8,128)(2,1)}, bf16[256,768]{1,0:T(8,128)(2,1)S(1)}, u32[]{:S(2)}) copy-start(bf16[256,768]{1,0:T(8,128)(2,1)S(1)} %collective-permute-done.16.got) | copy-start | bytes 1179652
  189.4 8.1 %collective-permute-start.17 = (bf16[2,4,192,768]{3,2,1,0:T(8,128)(2,1)}, bf16[2,4,192,768]{3,2,1,0:T(8,128)(2,1)}, u32[]{:S(2)}, u32[]{:S(2)}) collective-permute-start(bf16[2,4,192,768]{3,2,1,0:T(8,128)(2,1)} %bitcast.22), channel_id=1, source_target_pairs={{0,1},{1,0},{2,3},{3,2},{4,5},{5,4},{6,7},{7,6},{8,9},{9,8},{10,11... | collective-permute-start | bytes 7077896 | tf_op jit(solution)/shard_map/ppermute | solution.py:844
  193.3 4.2 %copy-start = (bf16[8,192,768]{2,1,0:T(8,128)(2,1)S(1)}, bf16[8,192,768]{2,1,0:T(8,128)(2,1)}, u32[]{:S(2)}) copy-start(bf16[8,192,768]{2,1,0:T(8,128)(2,1)} %get-tuple-element.247) | copy-start | bytes 7077892
  200.8 27.8 %collective-permute-start.18 = (bf16[4,192,768]{2,1,0:T(8,128)(2,1)}, bf16[4,192,768]{2,1,0:T(8,128)(2,1)S(1)}, u32[]{:S(2)}, u32[]{:S(2)}) collective-permute-start(bf16[4,192,768]{2,1,0:T(8,128)(2,1)} %get-tuple-element.295), channel_id=1, source_target_pairs={{0,2},{1,3},{2,0},{3,1},{4,6},{5,7},{6,4},{7,5},{8,10},{9,11},{10,... | collective-permute-start | bytes 3538952 | tf_op jit(solution)/shard_map/ppermute | solution.py:844
  228.8 6.3 %collective-permute-start.20 = (bf16[2,4,768,128]{3,2,1,0:T(8,128)(2,1)}, bf16[2,4,768,128]{3,2,1,0:T(8,128)(2,1)S(1)}, u32[]{:S(2)}, u32[]{:S(2)}) collective-permute-start(bf16[2,4,768,128]{3,2,1,0:T(8,128)(2,1)} %bitcast.26), channel_id=1, source_target_pairs={{0,1},{1,0},{2,3},{3,2},{4,5},{5,4},{6,7},{7,6},{8,9},{9,8},{10,11... | collective-permute-start | bytes 4718600 | tf_op jit(solution)/shard_map/ppermute | solution.py:844
  229.7 5.3 %collective-permute-start.19 = (bf16[2,4,672,128]{3,2,1,0:T(8,128)(2,1)}, bf16[2,4,672,128]{3,2,1,0:T(8,128)(2,1)}, u32[]{:S(2)}, u32[]{:S(2)}) collective-permute-start(bf16[2,4,672,128]{3,2,1,0:T(8,128)(2,1)} %bitcast.25), channel_id=1, source_target_pairs={{0,1},{1,0},{2,3},{3,2},{4,5},{5,4},{6,7},{7,6},{8,9},{9,8},{10,11... | collective-permute-start | bytes 4128776 | tf_op jit(solution)/shard_map/ppermute | solution.py:844
  229.8 14.5 %collective-permute-start.22 = (bf16[2,192,768]{2,1,0:T(8,128)(2,1)S(1)}, bf16[2,192,768]{2,1,0:T(8,128)(2,1)S(1)}, u32[]{:S(2)}, u32[]{:S(2)}) collective-permute-start(bf16[2,192,768]{2,1,0:T(8,128)(2,1)S(1)} %get-tuple-element.265), channel_id=1, source_target_pairs={{0,4},{1,5},{2,6},{3,7},{4,0},{5,1},{6,2},{7,3},{8,12},{9,13},{10,... | collective-permute-start | bytes 1769480 | tf_op jit(solution)/shard_map/ppermute | solution.py:844
  231.0 8.1 %copy-start.9 = (bf16[256,768]{1,0:T(8,128)(2,1)S(1)}, bf16[256,768]{1,0:T(8,128)(2,1)}, u32[]{:S(2)}) copy-start(bf16[256,768]{1,0:T(8,128)(2,1)} %get-tuple-element.185) | copy-start | bytes 1179652
  231.0 17.3 %copy-start.1 = (bf16[8,768,128]{2,1,0:T(8,128)(2,1)S(1)}, bf16[8,768,128]{2,1,0:T(8,128)(2,1)}, u32[]{:S(2)}) copy-start(bf16[8,768,128]{2,1,0:T(8,128)(2,1)} %get-tuple-element.266) | copy-start | bytes 4718596
  236.5 25.4 %collective-permute-start.21 = (bf16[4,672,128]{2,1,0:T(8,128)(2,1)S(1)}, bf16[4,672,128]{2,1,0:T(8,128)(2,1)S(1)}, u32[]{:S(2)}, u32[]{:S(2)}) collective-permute-start(bf16[4,672,128]{2,1,0:T(8,128)(2,1)S(1)} %fusion.5), channel_id=1, source_target_pairs={{0,2},{1,3},{2,0},{3,1},{4,6},{5,7},{6,4},{7,5},{8,10},{9,11},{10,... | collective-permute-start | bytes 2064392 | tf_op jit(solution)/shard_map/ppermute | solution.py:844
  245.1 16.9 %collective-permute-start.23 = (bf16[192,768]{1,0:T(8,128)(2,1)S(1)}, bf16[192,768]{1,0:T(8,128)(2,1)S(1)}, u32[]{:S(2)}, u32[]{:S(2)}) collective-permute-start(bf16[192,768]{1,0:T(8,128)(2,1)S(1)} %fusion.9), channel_id=1, source_target_pairs={{0,8},{1,9},{2,10},{3,11},{4,12},{5,13},{6,14},{7,15},{8,0},{9,1},... | collective-permute-start | bytes 884744 | tf_op jit(solution)/shard_map/ppermute | solution.py:844
  248.3 21.4 %copy-start.7 = (bf16[2,192,768]{2,1,0:T(8,128)(2,1)S(1)}, bf16[2,192,768]{2,1,0:T(8,128)(2,1)}, u32[]{:S(2)}) copy-start(bf16[2,192,768]{2,1,0:T(8,128)(2,1)} %copy-done.6) | copy-start | bytes 1769476
  249.6 22.2 %copy-start.3 = (bf16[8,672,128]{2,1,0:T(8,128)(2,1)S(1)}, bf16[8,672,128]{2,1,0:T(8,128)(2,1)}, u32[]{:S(2)}) copy-start(bf16[8,672,128]{2,1,0:T(8,128)(2,1)} %get-tuple-element.260) | copy-start | bytes 4128772
  262.0 8.6 %copy-start.5 = (bf16[4,672,128]{2,1,0:T(8,128)(2,1)}, bf16[4,672,128]{2,1,0:T(8,128)(2,1)S(1)}, u32[]{:S(2)}) copy-start(bf16[4,672,128]{2,1,0:T(8,128)(2,1)S(1)} %collective-permute-done.21) | copy-start | bytes 2064388
  262.0 27.4 %collective-permute-start.24 = (bf16[4,768,128]{2,1,0:T(8,128)(2,1)}, bf16[4,768,128]{2,1,0:T(8,128)(2,1)S(1)}, u32[]{:S(2)}, u32[]{:S(2)}) collective-permute-start(bf16[4,768,128]{2,1,0:T(8,128)(2,1)} %get-tuple-element.271), channel_id=1, source_target_pairs={{0,2},{1,3},{2,0},{3,1},{4,6},{5,7},{6,4},{7,5},{8,10},{9,11},{10,... | collective-permute-start | bytes 2359304 | tf_op jit(solution)/shard_map/ppermute | solution.py:844
  264.2 34.5 %collective-permute-start.25 = (bf16[2,512,384]{2,1,0:T(8,128)(2,1)}, bf16[2,512,384]{2,1,0:T(8,128)(2,1)}, u32[]{:S(2)}, u32[]{:S(2)}) collective-permute-start(bf16[2,512,384]{2,1,0:T(8,128)(2,1)} %get-tuple-element.272), channel_id=1, source_target_pairs={{0,1},{1,2},{2,3},{3,4},{4,5},{5,6},{6,7},{7,8},{8,9},{9,10},{10,1... | collective-permute-start | bytes 2359304 | tf_op jit(solution)/shard_map/ppermute | solution.py:850
  266.5 32.2 %collective-permute-start.26 = (bf16[2,512,384]{2,1,0:T(8,128)(2,1)}, bf16[2,512,384]{2,1,0:T(8,128)(2,1)}, u32[]{:S(2)}, u32[]{:S(2)}) collective-permute-start(bf16[2,512,384]{2,1,0:T(8,128)(2,1)} %get-tuple-element.273), channel_id=1, source_target_pairs={{1,0},{2,1},{3,2},{4,3},{5,4},{6,5},{7,6},{8,7},{9,8},{10,9},{11,1... | collective-permute-start | bytes 2359304 | tf_op jit(solution)/shard_map/ppermute | solution.py:850
  270.8 3.4 %copy-start.8 = (bf16[2,24,1536]{2,1,0:T(8,128)(2,1)}, bf16[2,24,1536]{2,1,0:T(8,128)(2,1)S(1)}, u32[]{:S(2)}) copy-start(bf16[2,24,1536]{2,1,0:T(8,128)(2,1)S(1)} %reshape.415) | copy-start | bytes 442372
  271.5 6.2 %collective-permute-start.29 = (bf16[24,1536]{1,0:T(8,128)(2,1)}, bf16[24,1536]{1,0:T(8,128)(2,1)}, u32[]{:S(2)}, u32[]{:S(2)}) collective-permute-start(bf16[24,1536]{1,0:T(8,128)(2,1)} %dynamic-slice_bitcast_fusion), channel_id=1, source_target_pairs={{0,16},{16,0},{1,17},{17,1},{2,18},{18,2},{3,19},{19,3},{4,20},{20... | collective-permute-start | bytes 221192 | tf_op jit(solution)/shard_map/ppermute | solution.py:844
  274.2 32.3 %all-to-all-start = ((bf16[4,672,128]{2,1,0:T(8,128)(2,1)}), bf16[4,672,128]{2,1,0:T(8,128)(2,1)S(1)}, u32[]{:S(2)}, u32[]{:S(2)}) async-start(bf16[4,672,128]{2,1,0:T(8,128)(2,1)} %add_convert_fusion.1), calls=%async_computation | async-start | bytes 1376256 | tf_op jit(solution)/shard_map/all_to_all | solution.py:862
  306.1 9.2 %collective-permute-start.27 = (bf16[256,768]{1,0:T(8,128)(2,1)}, bf16[256,768]{1,0:T(8,128)(2,1)S(1)}, u32[]{:S(2)}, u32[]{:S(2)}) collective-permute-start(bf16[256,768]{1,0:T(8,128)(2,1)} %get-tuple-element.282), channel_id=1, source_target_pairs={{0,16},{16,0},{1,17},{17,1},{2,18},{18,2},{3,19},{19,3},{4,20},{20... | collective-permute-start | bytes 1179656 | tf_op jit(solution)/shard_map/ppermute | solution.py:844
  306.5 17.5 %all-to-all-start.1 = ((bf16[4,768,128]{2,1,0:T(8,128)(2,1)}), bf16[4,768,128]{2,1,0:T(8,128)(2,1)S(1)}, u32[]{:S(2)}, u32[]{:S(2)}) async-start(bf16[4,768,128]{2,1,0:T(8,128)(2,1)} %add_convert_fusion), calls=%async_computation.1 | async-start | bytes 1572864 | tf_op jit(solution)/shard_map/all_to_all | solution.py:862
  310.1 5.2 %copy-start.4 = (f32[256,768]{1,0:T(8,128)S(1)}, f32[256,768]{1,0:T(8,128)}, u32[]{:S(2)}) copy-start(f32[256,768]{1,0:T(8,128)} %get-tuple-element.281) | copy-start | bytes 2359300
  310.2 3.8 %collective-permute-start.28 = (bf16[216,128]{1,0:T(8,128)(2,1)S(1)}, bf16[216,128]{1,0:T(8,128)(2,1)S(1)}, u32[]{:S(2)}, u32[]{:S(2)}) collective-permute-start(bf16[216,128]{1,0:T(8,128)(2,1)S(1)} %bitcast.156), channel_id=1, source_target_pairs={{0,16},{16,0},{1,17},{17,1},{2,18},{18,2},{3,19},{19,3},{4,20},{20... | collective-permute-start | bytes 165896 | tf_op jit(solution)/shard_map/ppermute | solution.py:844
  316.3 8.4 %copy-start.2 = (f32[6,32,512]{2,1,0:T(8,128)S(1)}, f32[6,32,512]{2,1,0:T(8,128)}, u32[]{:S(2)}) copy-start(f32[6,32,512]{2,1,0:T(8,128)} %get-tuple-element.293) | copy-start | bytes 1179652
  316.3 8.4 %copy-start.13 = (f32[6]{0:T(128)S(1)}, f32[6]{0:T(128)}, u32[]{:S(2)}) copy-start(f32[6]{0:T(128)} %param.24) | copy-start | bytes 76
  (2 other events, 2.0 us)
Sparse Core Ops, SparseCore 0:
  22.3 56.8 all-gather.2
  81.5 58.2 all-gather.4

commit v3 on v2

--- a/solution.py
+++ b/solution.py
@@ -487,7 +487,7 @@
     ddown[...] = grad.astype(BF)
     sums[1:2, :] = column_sum(ddown[...].astype(F32))
     base2[...] = grad
-    wait_for(copies)
+    wait_for(copies[4:])
 
     def back(n, carry):
         low = (nt(ddown[...], shrink_rows(wd, n)) * slope[n]).astype(BF)
@@ -496,6 +496,7 @@
         return carry
 
     lax.fori_loop(0, 2, back, 0)
+    wait_for(copies[:4])
     part = nt(dup[0], wu[0].reshape(D, D)) + nt(dup[1], wu[1].reshape(D, D))
     base2[...] += part
     send[...] = part.astype(BF)

time: 333 us -> 333 us (level)
  Pallas kernels: 107 us -> 111 us
  waiting for transfers between devices: 113 us -> 109 us
  transfers between devices with their start and end apart: 34 -> 34, of which waited for: 16 -> 16; matrix products, arithmetic and copies ran while one was open for 11% -> 11% of each run, Pallas kernels for 30% -> 31%
where the time goes in v3:
time: 333 us
  Pallas kernels  111 us (33%)
  waiting for transfers between devices  109 us (33%)
  starting transfers between devices  50.4 us (15%)
  local copies, waits for them, and re-layouts  24.2 us (7%)
  other arithmetic  23.1 us (7%)
  between operations  15 us (5%)
    ppermute x23, waiting for transfers between devices, swap(): return lax.ppermute(value, axis, [(i, i ^ bit) for i in range(count)])  68.4 us
    pallas_call x1, Pallas kernels, attend_back(): pl.pallas_call(partial(attend_back_kernel, len(before)), name=f'attend_ba...  25.6 us
    pallas_call x1, Pallas kernels, attend(): pl.pallas_call(attend_kernel, name='attend', grid=(3,), out_shape=(shape(...  25.3 us
    ppermute x23, starting transfers between devices, swap(): return lax.ppermute(value, axis, [(i, i ^ bit) for i in range(count)])  24.5 us
    pallas_call x2, Pallas kernels, feed_back(): pl.pallas_call(partial(feed_back_kernel, index), name=f'feed_back_{index}...  15.2 us
    pallas_call x2, Pallas kernels, feed_up(): pl.pallas_call(feed_up_kernel, name=f'feed_up_{index}', grid=(1,), out_sh...  14.1 us
    all_gather x1, waiting for transfers between devices, per_device(): wg = lax.all_gather(shard, 'fsdp', axis=0, tiled=True).reshape(8, 2, 240, D)  12.5 us
    ppermute x4, starting transfers between devices, shifted(): lax.ppermute(value, axis, [(source, source + steps) for source in range(l...  11.2 us
  transfers between devices with their start and end apart: 34, of which 16 were waited for; matrix products, arithmetic and copies ran while one was open for 11% of the time, Pallas kernels for 31%

profile of v3, /device:TPU:1, one launch (start us, length us, event | category | flops | bytes accessed | tf_op | source)
XLA Modules:
  0.0 332.5 jit_solution(12278290604188454028)
XLA Ops:
  7.3 0.9 reshape.392
  8.9 1.3 collective-permute-start.8
  10.2 4.5 %collective-permute-start.10 = (bf16[24,1152]{1,0:T(8,128)(2,1)S(1)}, bf16[24,1152]{1,0:T(8,128)(2,1)S(1)}, u32[]{:S(2)}, u32[]{:S(2)}) collective-permute-start(bf16[24,1152]{1,0:T(8,128)(2,1)S(1)} %bitcast.158), channel_id=1, source_target_pairs={{1,16},{3,18},{5,20},{7,22},{9,24},{11,26},{13,28},{15,30},{16,1},... | collective-permute-start | bytes 165896 | tf_op jit(solution)/shard_map/ppermute | solution.py:916
  14.8 1.7 collective-permute-start.9
  16.4 2.1 fusion.29
  18.9 3.2 concatenate.46
  22.3 3.1 collective-permute-start.1
  25.4 1.9 collective-permute-start.2
  27.8 1.1 collective-permute-start.5
  30.2 5.5 %collective-permute-done.5 = bf16[1,24,2304]{2,1,0:T(8,128)(2,1)S(1)} collective-permute-done((bf16[1,24,2304]{2,1,0:T(8,128)(2,1)S(1)}, bf16[1,24,2304]{2,1,0:T(8,128)(2,1)S(1)}, u32[]{:S(2)}, u32[]{:S(2)}) %collective-permute-start.5) | collective-permute-done | bytes 110624 | tf_op jit(solution)/shard_map/ppermute | solution.py:845
  37.4 3.3 stack.15.scal
  41.1 1.1 collective-permute-start.4
  43.1 8.0 %collective-permute-done.3.y0 = bf16[256,768]{1,0:T(8,128)(2,1)S(1)} collective-permute-done((bf16[256,768]{1,0:T(8,128)(2,1)S(1)}, bf16[256,768]{1,0:T(8,128)(2,1)S(1)}, u32[]{:S(2)}, u32[]{:S(2)}) %collective-permute-start.3) | collective-permute-done | bytes 393248 | tf_op jit(solution)/shard_map/ppermute | solution.py:845
  51.1 8.5 %collective-permute-done.4.y2 = bf16[256,768]{1,0:T(8,128)(2,1)S(1)} collective-permute-done((bf16[256,768]{1,0:T(8,128)(2,1)S(1)}, bf16[256,768]{1,0:T(8,128)(2,1)S(1)}, u32[]{:S(2)}, u32[]{:S(2)}) %collective-permute-start.4) | collective-permute-done | bytes 393248 | tf_op jit(solution)/shard_map/ppermute | solution.py:845
  62.4 1.1 reshape.431.pos_col
  64.1 1.1 reshape.432.doc_col
  65.9 4.5 %collective-permute-done.7.cot_other = bf16[256,768]{1,0:T(8,128)(2,1)S(1)} collective-permute-done((bf16[256,768]{1,0:T(8,128)(2,1)S(1)}, bf16[256,768]{1,0:T(8,128)(2,1)S(1)}, u32[]{:S(2)}, u32[]{:S(2)}) %collective-permute-start.7) | collective-permute-done | bytes 393248 | tf_op jit(solution)/shard_map/ppermute | solution.py:845
  70.4 8.8 %all-gather.3.cloned.1.call-done = bf16[19968,128]{1,0:T(8,128)(2,1)} async-done(((bf16[1248,128]{1,0:T(8,128)(2,1)}), bf16[19968,128]{1,0:T(8,128)(2,1)}) %all-gather.3.cloned.1.call-update) | async-done | bytes 5111824 | tf_op jit(solution)/shard_map/all_gather | solution.py:1015
  80.7 1.2 collective-permute-start.11
  82.5 8.9 %project.1 = (bf16[512,384]{1,0:T(8,128)(2,1)}, bf16[1536,384]{1,0:T(8,128)(2,1)}, bf16[1536,384]{1,0:T(8,128)(2,1)}, bf16[1536,768]{1,0:T(8,128)(2,1)}, bf16[6,...) custom-call(s32[8]{0:T(128)} %stack.15.scal, bf16[256,768]{1,0:T(8,128)(2,1)} %bitcast.170, bf16[256,768]{1,0:T(8,128)(2,1)} %copy-done.19, ...), custom_call_target="tpu_custom_call" | custom-call | flops 10350000128 | bytes 1000 | tf_op jit(solution)/shard_map/project/pallas_call | solution.py:598
  91.4 25.3 %attend.1 = (bf16[2,256,384]{2,1,0:T(8,128)(2,1)}, f32[3,8,512]{2,1,0:T(8,128)}, bf16[3,2,6,256,512]{4,3,2,1,0:T(8,128)(2,1)}, bf16[3,2,6,256,512]{4,3,2,1,0:T(8,128)(2,1)}, bf16[6,512,256]{2,1,0:T(8,128)(2,1)}) custom-call(s32[8]{0:T(128)} %stack.15.scal, s32[1536,1]{1,0:T(8,128)} %reshape.431.pos_col, s32[6,1,256]{2,1,0:T(1,128)} %reshape.400.pos_row, ...), custom_call_target="tpu_custom_call" | custom-call | flops 29899999232 | bytes 1000 | tf_op jit(solution)/shard_map/attend/pallas_call | solution.py:625
  119.3 8.0 %collective-permute-done.12.ctx_other = bf16[2,256,384]{2,1,0:T(8,128)(2,1)S(1)} collective-permute-done((bf16[2,256,384]{2,1,0:T(8,128)(2,1)}, bf16[2,256,384]{2,1,0:T(8,128)(2,1)S(1)}, u32[]{:S(2)}, u32[]{:S(2)}) %collective-permute-start.12) | collective-permute-done | bytes 393248 | tf_op jit(solution)/shard_map/ppermute | solution.py:845
  127.3 12.5 %all-gather.5.cloned.1.call-done = bf16[3840,768]{1,0:T(8,128)(2,1)} async-done(((bf16[240,768]{1,0:T(8,128)(2,1)}), bf16[3840,768]{1,0:T(8,128)(2,1)}) %all-gather.5.cloned.1.call-update) | async-done | bytes 5898256 | tf_op jit(solution)/shard_map/all_gather | solution.py:1022
  140.4 7.0 %feed_up_0.1 = (f32[256,768]{1,0:T(8,128)}, f32[256,128]{1,0:T(8,128)}, bf16[256,768]{1,0:T(8,128)(2,1)}, f32[256,768]{1,0:T(8,128)}, bf16[256,768]{1,0:T(8,128)...) custom-call(s32[8]{0:T(128)} %stack.15.scal, bf16[1536,768]{1,0:T(8,128)(2,1)} %get-tuple-element.156.x, ...), custom_call_target="tpu_custom_call" | custom-call | flops 9200000000 | bytes 1000 | tf_op jit(solution)/shard_map/feed_up_0/pallas_call | solution.py:750
  147.5 1.3 collective-permute-start.13
  149.3 7.1 %feed_up_1.1 = (f32[256,768]{1,0:T(8,128)}, f32[256,128]{1,0:T(8,128)}, bf16[256,768]{1,0:T(8,128)(2,1)}, f32[256,768]{1,0:T(8,128)}, bf16[256,768]{1,0:T(8,128)...) custom-call(s32[8]{0:T(128)} %stack.15.scal, bf16[1536,768]{1,0:T(8,128)(2,1)} %get-tuple-element.156.x, ...), custom_call_target="tpu_custom_call" | custom-call | flops 9200000000 | bytes 1000 | tf_op jit(solution)/shard_map/feed_up_1/pallas_call | solution.py:750
  156.4 1.8 collective-permute-done.13.got
  158.2 1.2 collective-permute-start.14
  159.4 7.5 %feed_back_0.1 = (bf16[256,768]{1,0:T(8,128)(2,1)}, bf16[256,768]{1,0:T(8,128)(2,1)}, bf16[2,256,768]{2,1,0:T(8,128)(2,1)}, f32[256,768]{1,0:T(8,128)}, bf16[256,768]{1,0:T(8,128)(2,1)}, /*index=5*/f32[16,768]{1,0:T(8,128)}) custom-call(s32[8]{0:T(128)} %stack.15.scal, f32[256,768]{1,0:T(8,128)} %get-tuple-element.166.base, bf16[256,768]{1,0:T(8,128)(2,1)} %copy-done.27, ...), custom_call_target="tpu_custom_call" | custom-call | flops 8049999872 | bytes 1000 | tf_op jit(solution)/shard_map/feed_back_0/pallas_call | solution.py:773
  166.9 1.1 collective-permute-done.14.got
  168.0 1.2 collective-permute-start.15
  169.2 7.7 %feed_back_1.1 = (bf16[256,768]{1,0:T(8,128)(2,1)}, bf16[256,768]{1,0:T(8,128)(2,1)}, bf16[2,256,768]{2,1,0:T(8,128)(2,1)}, f32[256,768]{1,0:T(8,128)}, bf16[256,768]{1,0:T(8,128)(2,1)}, /*index=5*/f32[16,768]{1,0:T(8,128)}) custom-call(s32[8]{0:T(128)} %stack.15.scal, f32[256,768]{1,0:T(8,128)} %get-tuple-element.186.base, bf16[256,768]{1,0:T(8,128)(2,1)} %copy-done.28, ...), custom_call_target="tpu_custom_call" | custom-call | flops 8049999872 | bytes 1000 | tf_op jit(solution)/shard_map/feed_back_1/pallas_call | solution.py:773
  176.9 1.1 collective-permute-start.16
  178.0 7.3 %weight_grads.1 = (bf16[8,192,768]{2,1,0:T(8,128)(2,1)}, bf16[8,192,768]{2,1,0:T(8,128)(2,1)}) custom-call(s32[8]{0:T(128)} %stack.15.scal, bf16[2,256,768]{2,1,0:T(8,128)(2,1)} %get-tuple-element.213.act0, bf16[256,768]{1,0:T(8,128)(2,1)} %get-tuple-element.214.ddown0, bf16[256,768]{1,0:T(8,128)(2,1)} %get-tuple-element.215.nlow0, ...), custom_call_target="tpu_custom_call" | custom-call | flops 8049999872 | bytes 1000 | tf_op jit(solution)/shard_map/weight_grads/pallas_call | solution.py:811
  185.3 4.0 %feed_close_0.1 = (f32[256,768]{1,0:T(8,128)}, bf16[256,768]{1,0:T(8,128)(2,1)}, bf16[256,384]{1,0:T(8,128)(2,1)}, f32[16,768]{1,0:T(8,128)}) custom-call(s32[8]{0:T(128)} %stack.15.scal, f32[256,768]{1,0:T(8,128)} %get-tuple-element.203.base, bf16[256,768]{1,0:T(8,128)(2,1)} %copy-done.26, f32[256,768]{1,0:T(8,128)} %get-tuple-element.205.unit1, ...), custom_call_target="tpu_custom_call" | custom-call | flops 4600000000 | bytes 1000 | tf_op jit(solution)/shard_map/feed_close_0/pallas_call | solution.py:793
  189.4 3.2 collective-permute-start.17
  193.3 4.2 %feed_close_1.1 = (f32[256,768]{1,0:T(8,128)}, bf16[256,768]{1,0:T(8,128)(2,1)}, bf16[256,384]{1,0:T(8,128)(2,1)}, f32[16,768]{1,0:T(8,128)}) custom-call(s32[8]{0:T(128)} %stack.15.scal, f32[256,768]{1,0:T(8,128)} %get-tuple-element.202.base, bf16[256,768]{1,0:T(8,128)(2,1)} %copy-done.24, f32[256,768]{1,0:T(8,128)} %get-tuple-element.225.unit1, ...), custom_call_target="tpu_custom_call" | custom-call | flops 4600000000 | bytes 1000 | tf_op jit(solution)/shard_map/feed_close_1/pallas_call | solution.py:793
  197.5 3.3 fusion
  201.0 25.6 %attend_back_0.1 = (bf16[512,384]{1,0:T(8,128)(2,1)}, f32[2,512,384]{2,1,0:T(8,128)}, bf16[2,512,384]{2,1,0:T(8,128)(2,1)}, bf16[2,512,384]{2,1,0:T(8,128)(2,1)}...) custom-call(s32[8]{0:T(128)} %stack.15.scal, ...), custom_call_target="tpu_custom_call" | custom-call | flops 34500001792 | bytes 1000 | tf_op jit(solution)/shard_map/attend_back_0/pallas_call | solution.py:673
  226.7 1.9 collective-permute-done.18
  228.8 0.9 collective-permute-start.20
  229.8 2.6 collective-permute-start.22
  232.4 2.7 collective-permute-done.19
  235.1 1.5 fusion.5
  236.6 2.6 collective-permute-start.21
  240.0 5.7 %collective-permute-done.22 = bf16[2,192,768]{2,1,0:T(8,128)(2,1)S(1)} collective-permute-done((bf16[2,192,768]{2,1,0:T(8,128)(2,1)S(1)}, bf16[2,192,768]{2,1,0:T(8,128)(2,1)S(1)}, u32[]{:S(2)}, u32[]{:S(2)}) %collective-permute-start.22) | collective-permute-done | bytes 589856 | tf_op jit(solution)/shard_map/ppermute | solution.py:845
  246.5 1.6 collective-permute-start.23
  248.1 1.3 fusion.2
  249.4 12.4 %collective-permute-done.23 = bf16[192,768]{1,0:T(8,128)(2,1)S(1)} collective-permute-done((bf16[192,768]{1,0:T(8,128)(2,1)S(1)}, bf16[192,768]{1,0:T(8,128)(2,1)S(1)}, u32[]{:S(2)}, u32[]{:S(2)}) %collective-permute-start.23) | collective-permute-done | bytes 294944 | tf_op jit(solution)/shard_map/ppermute | solution.py:845
  261.8 1.5 collective-permute-start.24
  263.3 3.4 %collective-permute-start.25 = (bf16[2,512,384]{2,1,0:T(8,128)(2,1)}, bf16[2,512,384]{2,1,0:T(8,128)(2,1)}, u32[]{:S(2)}, u32[]{:S(2)}) collective-permute-start(bf16[2,512,384]{2,1,0:T(8,128)(2,1)} %get-tuple-element.272), channel_id=1, source_target_pairs={{0,1},{1,2},{2,3},{3,4},{4,5},{5,6},{6,7},{7,8},{8,9},{9,10},{10,1... | collective-permute-start | bytes 2359304 | tf_op jit(solution)/shard_map/ppermute | solution.py:851
  266.7 2.7 collective-permute-start.26
  271.5 2.4 add_convert_fusion.1
  273.9 3.5 %all-to-all-start = ((bf16[4,672,128]{2,1,0:T(8,128)(2,1)}), bf16[4,672,128]{2,1,0:T(8,128)(2,1)S(1)}, u32[]{:S(2)}, u32[]{:S(2)}) async-start(bf16[4,672,128]{2,1,0:T(8,128)(2,1)} %add_convert_fusion.1), calls=%async_computation | async-start | bytes 1376256 | tf_op jit(solution)/shard_map/all_to_all | solution.py:863
  277.4 0.9 bitcast_select_fusion.3
  279.1 8.3 %collective-permute-done.24 = bf16[4,768,128]{2,1,0:T(8,128)(2,1)S(1)} collective-permute-done((bf16[4,768,128]{2,1,0:T(8,128)(2,1)}, bf16[4,768,128]{2,1,0:T(8,128)(2,1)S(1)}, u32[]{:S(2)}, u32[]{:S(2)}) %collective-permute-start.24) | collective-permute-done | bytes 786464 | tf_op jit(solution)/shard_map/ppermute | solution.py:845
  287.4 10.4 %collective-permute-done.25.refs_2_ = bf16[2,512,384]{2,1,0:T(8,128)(2,1)} collective-permute-done((bf16[2,512,384]{2,1,0:T(8,128)(2,1)}, bf16[2,512,384]{2,1,0:T(8,128)(2,1)}, u32[]{:S(2)}, u32[]{:S(2)}) %collective-permute-start.25) | collective-permute-done | bytes 786464 | tf_op jit(solution)/shard_map/ppermute | solution.py:851
  297.8 1.1 add_convert_fusion
  298.9 6.3 %project_back.1 = (f32[256,768]{1,0:T(8,128)}, bf16[256,768]{1,0:T(8,128)(2,1)}) custom-call(s32[8]{0:T(128)} %stack.15.scal, bf16[512,384]{1,0:T(8,128)(2,1)} %get-tuple-element.258.refs_0_, f32[2,512,384]{2,1,0:T(8,128)} %get-tuple-element.259.refs_1_, bf16[2,512,384]{2,1,0:T(8,128)(2,1)} %collective-permute-done.25.refs_2_, ...), custom_call_target="tpu_custom_call" | custom-call | flops 6899999744 | bytes 1000 | tf_op jit(solution)/shard_map/project_back/pallas_call | solution.py:827
  305.6 3.6 %all-to-all-start.1 = ((bf16[4,768,128]{2,1,0:T(8,128)(2,1)}), bf16[4,768,128]{2,1,0:T(8,128)(2,1)S(1)}, u32[]{:S(2)}, u32[]{:S(2)}) async-start(bf16[4,768,128]{2,1,0:T(8,128)(2,1)} %add_convert_fusion), calls=%async_computation.1 | async-start | bytes 1572864 | tf_op jit(solution)/shard_map/all_to_all | solution.py:863
  309.5 1.3 collective-permute-start.28
  313.7 0.9 reshape.423
  314.5 1.0 add_bitcast_fusion
  315.5 8.7 %all-to-all-done.1 = bf16[4,768,128]{2,1,0:T(8,128)(2,1)S(1)} async-done(((bf16[4,768,128]{2,1,0:T(8,128)(2,1)}), bf16[4,768,128]{2,1,0:T(8,128)(2,1)S(1)}, u32[]{:S(2)}, u32[]{:S(2)}) %all-to-all-start.1) | async-done | bytes 786464 | tf_op jit(solution)/shard_map/all_to_all | solution.py:863
  (199 shorter events, 26.0 us)
Async XLA Ops:
  7.2 11.4 %copy-start.14 = (bf16[6,24]{1,0:T(8,128)(2,1)S(1)}, bf16[6,24]{1,0:T(8,128)(2,1)}, u32[]{:S(2)}) copy-start(bf16[6,24]{1,0:T(8,128)(2,1)} %param.19) | copy-start | bytes 868
  7.2 11.5 %copy-start.29 = (bf16[2,24]{1,0:T(2,128)(2,1)S(1)}, bf16[2,24]{1,0:T(2,128)(2,1)}, u32[]{:S(2)}) copy-start(bf16[2,24]{1,0:T(2,128)(2,1)} %param.20) | copy-start | bytes 292
  7.2 11.5 %copy-start.30 = (bf16[96]{0:T(256)(128)(2,1)S(1)}, bf16[96]{0:T(256)(128)(2,1)}, u32[]{:S(2)}) copy-start(bf16[96]{0:T(256)(128)(2,1)} %param.21) | copy-start | bytes 580
  7.2 72.0 %all-gather.3.cloned.1.call-start = ((), (), s32[]{:S(2)}) async-start(), calls=%async_computation.2 | async-start | bytes 5431296 | tf_op jit(solution)/shard_map/all_gather | solution.py:1015
  8.9 9.8 %collective-permute-start.8 = (bf16[24,1152]{1,0:T(8,128)(2,1)S(1)}, bf16[24,1152]{1,0:T(8,128)(2,1)S(1)}, u32[]{:S(2)}, u32[]{:S(2)}) collective-permute-start(bf16[24,1152]{1,0:T(8,128)(2,1)S(1)} %bitcast.157), channel_id=1, source_target_pairs={{0,16},{2,18},{4,20},{6,22},{8,24},{10,26},{12,28},{14,30},{17,1},... | collective-permute-start | bytes 165896 | tf_op jit(solution)/shard_map/ppermute | solution.py:915
  10.2 8.5 %collective-permute-start.10 = (bf16[24,1152]{1,0:T(8,128)(2,1)S(1)}, bf16[24,1152]{1,0:T(8,128)(2,1)S(1)}, u32[]{:S(2)}, u32[]{:S(2)}) collective-permute-start(bf16[24,1152]{1,0:T(8,128)(2,1)S(1)} %bitcast.158), channel_id=1, source_target_pairs={{1,16},{3,18},{5,20},{7,22},{9,24},{11,26},{13,28},{15,30},{16,1},... | collective-permute-start | bytes 165896 | tf_op jit(solution)/shard_map/ppermute | solution.py:916
  14.8 4.0 %collective-permute-start.9 = (bf16[24,1152]{1,0:T(8,128)(2,1)S(1)}, bf16[24,1152]{1,0:T(8,128)(2,1)S(1)}, u32[]{:S(2)}, u32[]{:S(2)}) collective-permute-start(bf16[24,1152]{1,0:T(8,128)(2,1)S(1)} %bitcast.150), channel_id=1, source_target_pairs={{1,0},{3,2},{5,4},{7,6},{9,8},{11,10},{13,12},{15,14},{16,17},{18,... | collective-permute-start | bytes 165896 | tf_op jit(solution)/shard_map/ppermute | solution.py:916
  18.5 3.7 %copy-start.16 = (bf16[1,256,768]{2,1,0:T(8,128)(2,1)S(1)}, bf16[1,256,768]{2,1,0:T(8,128)(2,1)}, u32[]{:S(2)}) copy-start(bf16[1,256,768]{2,1,0:T(8,128)(2,1)} %param.14) | copy-start | bytes 1179652
  18.5 8.8 %copy-start.10 = (bf16[24,3072]{1,0:T(8,128)(2,1)S(1)}, bf16[24,3072]{1,0:T(8,128)(2,1)}, u32[]{:S(2)}) copy-start(bf16[24,3072]{1,0:T(8,128)(2,1)} %param.17) | copy-start | bytes 442372
  18.7 9.1 %copy-start.11 = (bf16[24,768]{1,0:T(8,128)(2,1)S(1)}, bf16[24,768]{1,0:T(8,128)(2,1)}, u32[]{:S(2)}) copy-start(bf16[24,768]{1,0:T(8,128)(2,1)} %param.16) | copy-start | bytes 110596
  18.8 10.2 %copy-start.15 = (s32[32]{0:T(128)S(1)}, s32[32]{0:T(128)}, u32[]{:S(2)}) copy-start(s32[32]{0:T(128)} %param.25) | copy-start | bytes 388
  18.8 10.5 %copy-start.31 = (s32[4]{0:T(128)S(1)}, s32[4]{0:T(128)}, u32[]{:S(2)}) copy-start(s32[4]{0:T(128)} %constant.177.clone) | copy-start | bytes 52
  22.2 117.7 %all-gather.5.cloned.1.call-start = ((), (), s32[]{:S(2)}) async-start(), calls=%async_computation.3 | async-start | bytes 6266880 | tf_op jit(solution)/shard_map/all_gather | solution.py:1022
  22.2 18.4 %collective-permute-start = (bf16[256,768]{1,0:T(8,128)(2,1)S(1)}, bf16[256,768]{1,0:T(8,128)(2,1)S(1)}, u32[]{:S(2)}, u32[]{:S(2)}) collective-permute-start(bf16[256,768]{1,0:T(8,128)(2,1)S(1)} %bitcast.171), channel_id=1, source_target_pairs={{0,16},{16,0},{1,17},{17,1},{2,18},{18,2},{3,19},{19,3},{4,20},{20... | collective-permute-start | bytes 1179656 | tf_op jit(solution)/shard_map/ppermute | solution.py:845
  22.3 18.4 %collective-permute-start.1 = (bf16[256,768]{1,0:T(8,128)(2,1)S(1)}, bf16[256,768]{1,0:T(8,128)(2,1)S(1)}, u32[]{:S(2)}, u32[]{:S(2)}) collective-permute-start(bf16[256,768]{1,0:T(8,128)(2,1)S(1)} %bitcast.172), channel_id=1, source_target_pairs={{0,1},{1,2},{2,3},{3,4},{4,5},{5,6},{6,7},{7,8},{8,9},{9,10},{10,1... | collective-permute-start | bytes 1179656 | tf_op jit(solution)/shard_map/ppermute | solution.py:851
  25.4 15.3 %collective-permute-start.2 = (bf16[256,768]{1,0:T(8,128)(2,1)S(1)}, bf16[256,768]{1,0:T(8,128)(2,1)S(1)}, u32[]{:S(2)}, u32[]{:S(2)}) collective-permute-start(bf16[256,768]{1,0:T(8,128)(2,1)S(1)} %bitcast.173), channel_id=1, source_target_pairs={{1,0},{2,1},{3,2},{4,3},{5,4},{6,5},{7,6},{8,7},{9,8},{10,9},{11,1... | collective-permute-start | bytes 1179656 | tf_op jit(solution)/shard_map/ppermute | solution.py:851
  27.8 7.9 %collective-permute-start.5 = (bf16[1,24,2304]{2,1,0:T(8,128)(2,1)S(1)}, bf16[1,24,2304]{2,1,0:T(8,128)(2,1)S(1)}, u32[]{:S(2)}, u32[]{:S(2)}) collective-permute-start(bf16[1,24,2304]{2,1,0:T(8,128)(2,1)S(1)} %fusion.14), channel_id=1, source_target_pairs={{0,16},{16,0},{1,17},{17,1},{2,18},{18,2},{3,19},{19,3},{4,20},{20... | collective-permute-start | bytes 331784 | tf_op jit(solution)/shard_map/ppermute | solution.py:845
  35.9 6.5 %copy-start.12 = (bf16[96,768]{1,0:T(8,128)(2,1)S(1)}, bf16[96,768]{1,0:T(8,128)(2,1)}, u32[]{:S(2)}) copy-start(bf16[96,768]{1,0:T(8,128)(2,1)} %param.18) | copy-start | bytes 442372
  36.6 24.3 %copy-start.17 = (bf16[1,256,768]{2,1,0:T(8,128)(2,1)S(1)}, bf16[1,256,768]{2,1,0:T(8,128)(2,1)}, u32[]{:S(2)}) copy-start(bf16[1,256,768]{2,1,0:T(8,128)(2,1)} %param.26) | copy-start | bytes 1179652
  36.6 5.6 %collective-permute-start.6 = (bf16[2,24,1152]{2,1,0:T(8,128)(2,1)S(1)}, bf16[2,24,1152]{2,1,0:T(8,128)(2,1)S(1)}, u32[]{:S(2)}, u32[]{:S(2)}) collective-permute-start(bf16[2,24,1152]{2,1,0:T(8,128)(2,1)S(1)} %bitcast.153), channel_id=1, source_target_pairs={{0,1},{1,0},{2,3},{3,2},{4,5},{5,4},{6,7},{7,6},{8,9},{9,8},{10,11... | collective-permute-start | bytes 331784 | tf_op jit(solution)/shard_map/ppermute | solution.py:845
  40.7 22.9 %copy-start.18 = (bf16[256,768]{1,0:T(8,128)(2,1)}, bf16[256,768]{1,0:T(8,128)(2,1)S(1)}, u32[]{:S(2)}) copy-start(bf16[256,768]{1,0:T(8,128)(2,1)S(1)} %collective-permute-done.y1) | copy-start | bytes 1179652
  40.7 22.9 %copy-start.19 = (bf16[256,768]{1,0:T(8,128)(2,1)}, bf16[256,768]{1,0:T(8,128)(2,1)S(1)}, u32[]{:S(2)}) copy-start(bf16[256,768]{1,0:T(8,128)(2,1)S(1)} %collective-permute-done.1.x0) | copy-start | bytes 1179652
  40.7 22.8 %copy-start.20 = (bf16[256,768]{1,0:T(8,128)(2,1)}, bf16[256,768]{1,0:T(8,128)(2,1)S(1)}, u32[]{:S(2)}) copy-start(bf16[256,768]{1,0:T(8,128)(2,1)S(1)} %collective-permute-done.2.x2) | copy-start | bytes 1179652
  40.7 10.4 %collective-permute-start.3 = (bf16[256,768]{1,0:T(8,128)(2,1)S(1)}, bf16[256,768]{1,0:T(8,128)(2,1)S(1)}, u32[]{:S(2)}, u32[]{:S(2)}) collective-permute-start(bf16[256,768]{1,0:T(8,128)(2,1)S(1)} %collective-permute-done.1.x0), channel_id=1, source_target_pairs={{0,16},{16,0},{1,17},{17,1},{2,18},{18,2},{3,19},{19,3},{4,20},{20... | collective-permute-start | bytes 1179656 | tf_op jit(solution)/shard_map/ppermute | solution.py:845
  41.1 18.5 %collective-permute-start.4 = (bf16[256,768]{1,0:T(8,128)(2,1)S(1)}, bf16[256,768]{1,0:T(8,128)(2,1)S(1)}, u32[]{:S(2)}, u32[]{:S(2)}) collective-permute-start(bf16[256,768]{1,0:T(8,128)(2,1)S(1)} %collective-permute-done.2.x2), channel_id=1, source_target_pairs={{0,16},{16,0},{1,17},{17,1},{2,18},{18,2},{3,19},{19,3},{4,20},{20... | collective-permute-start | bytes 1179656 | tf_op jit(solution)/shard_map/ppermute | solution.py:845
  51.1 31.4 %copy-start.22 = (bf16[256,768]{1,0:T(8,128)(2,1)}, bf16[256,768]{1,0:T(8,128)(2,1)S(1)}, u32[]{:S(2)}) copy-start(bf16[256,768]{1,0:T(8,128)(2,1)S(1)} %collective-permute-done.3.y0) | copy-start | bytes 1179652
  59.6 22.9 %copy-start.23 = (bf16[256,768]{1,0:T(8,128)(2,1)}, bf16[256,768]{1,0:T(8,128)(2,1)S(1)}, u32[]{:S(2)}) copy-start(bf16[256,768]{1,0:T(8,128)(2,1)S(1)} %collective-permute-done.4.y2) | copy-start | bytes 1179652
  60.9 9.5 %collective-permute-start.7 = (bf16[256,768]{1,0:T(8,128)(2,1)S(1)}, bf16[256,768]{1,0:T(8,128)(2,1)S(1)}, u32[]{:S(2)}, u32[]{:S(2)}) collective-permute-start(bf16[256,768]{1,0:T(8,128)(2,1)S(1)} %bitcast.176), channel_id=1, source_target_pairs={{0,16},{16,0},{1,17},{17,1},{2,18},{18,2},{3,19},{19,3},{4,20},{20... | collective-permute-start | bytes 1179656 | tf_op jit(solution)/shard_map/ppermute | solution.py:845
  70.4 21.0 %copy-start.21 = (bf16[256,768]{1,0:T(8,128)(2,1)}, bf16[256,768]{1,0:T(8,128)(2,1)S(1)}, u32[]{:S(2)}) copy-start(bf16[256,768]{1,0:T(8,128)(2,1)S(1)} %collective-permute-done.7.cot_other) | copy-start | bytes 1179652
  80.7 10.7 %collective-permute-start.11 = (bf16[16,16,128]{2,0,1:T(8,128)(2,1)S(1)}, bf16[16,16,128]{2,0,1:T(8,128)(2,1)S(1)}, u32[]{:S(2)}, u32[]{:S(2)}) collective-permute-start(bf16[16,16,128]{2,0,1:T(8,128)(2,1)S(1)} %slice_bitcast_fusion), channel_id=1, source_target_pairs={{0,16},{16,0},{1,17},{17,1},{2,18},{18,2},{3,19},{19,3},{4,20},{20... | collective-permute-start | bytes 196616 | tf_op jit(solution)/shard_map/ppermute | solution.py:845
  116.8 10.5 %collective-permute-start.12 = (bf16[2,256,384]{2,1,0:T(8,128)(2,1)}, bf16[2,256,384]{2,1,0:T(8,128)(2,1)S(1)}, u32[]{:S(2)}, u32[]{:S(2)}) collective-permute-start(bf16[2,256,384]{2,1,0:T(8,128)(2,1)} %get-tuple-element.163.ctx_mine.ctx.ctx_all), channel_id=1, source_target_pairs={{0,16},{16,0},{1,17},{17,1},{2,18},{18,2},{3,19},{19,3},{4,20},{20... | collective-permute-start | bytes 1179656 | tf_op jit(solution)/shard_map/ppermute | solution.py:845
  127.3 13.1 %copy-start.25 = (bf16[2,256,384]{2,1,0:T(8,128)(2,1)}, bf16[2,256,384]{2,1,0:T(8,128)(2,1)S(1)}, u32[]{:S(2)}) copy-start(bf16[2,256,384]{2,1,0:T(8,128)(2,1)S(1)} %collective-permute-done.12.ctx_other) | copy-start | bytes 1179652
  147.5 10.7 %collective-permute-start.13 = (bf16[256,768]{1,0:T(8,128)(2,1)}, bf16[256,768]{1,0:T(8,128)(2,1)S(1)}, u32[]{:S(2)}, u32[]{:S(2)}) collective-permute-start(bf16[256,768]{1,0:T(8,128)(2,1)} %get-tuple-element.174), channel_id=1, source_target_pairs={{0,16},{16,0},{1,17},{17,1},{2,18},{18,2},{3,19},{19,3},{4,20},{20... | collective-permute-start | bytes 1179656 | tf_op jit(solution)/shard_map/ppermute | solution.py:845
  158.2 9.8 %collective-permute-start.14 = (bf16[256,768]{1,0:T(8,128)(2,1)}, bf16[256,768]{1,0:T(8,128)(2,1)S(1)}, u32[]{:S(2)}, u32[]{:S(2)}) collective-permute-start(bf16[256,768]{1,0:T(8,128)(2,1)} %get-tuple-element.184), channel_id=1, source_target_pairs={{0,16},{16,0},{1,17},{17,1},{2,18},{18,2},{3,19},{19,3},{4,20},{20... | collective-permute-start | bytes 1179656 | tf_op jit(solution)/shard_map/ppermute | solution.py:845
  168.0 1.2 copy-start.28
  168.0 8.9 %collective-permute-start.15 = (bf16[256,768]{1,0:T(8,128)(2,1)}, bf16[256,768]{1,0:T(8,128)(2,1)S(1)}, u32[]{:S(2)}, u32[]{:S(2)}) collective-permute-start(bf16[256,768]{1,0:T(8,128)(2,1)} %get-tuple-element.195), channel_id=1, source_target_pairs={{0,16},{16,0},{1,17},{17,1},{2,18},{18,2},{3,19},{19,3},{4,20},{20... | collective-permute-start | bytes 1179656 | tf_op jit(solution)/shard_map/ppermute | solution.py:845
  176.9 8.5 %copy-start.26 = (bf16[256,768]{1,0:T(8,128)(2,1)}, bf16[256,768]{1,0:T(8,128)(2,1)S(1)}, u32[]{:S(2)}) copy-start(bf16[256,768]{1,0:T(8,128)(2,1)S(1)} %collective-permute-done.15.got) | copy-start | bytes 1179652
  176.9 12.5 %collective-permute-start.16 = (bf16[256,768]{1,0:T(8,128)(2,1)}, bf16[256,768]{1,0:T(8,128)(2,1)S(1)}, u32[]{:S(2)}, u32[]{:S(2)}) collective-permute-start(bf16[256,768]{1,0:T(8,128)(2,1)} %get-tuple-element.223), channel_id=1, source_target_pairs={{0,16},{16,0},{1,17},{17,1},{2,18},{18,2},{3,19},{19,3},{4,20},{20... | collective-permute-start | bytes 1179656 | tf_op jit(solution)/shard_map/ppermute | solution.py:845
  189.4 3.9 %copy-start.24 = (bf16[256,768]{1,0:T(8,128)(2,1)}, bf16[256,768]{1,0:T(8,128)(2,1)S(1)}, u32[]{:S(2)}) copy-start(bf16[256,768]{1,0:T(8,128)(2,1)S(1)} %collective-permute-done.16.got) | copy-start | bytes 1179652
  189.4 8.1 %collective-permute-start.17 = (bf16[2,4,192,768]{3,2,1,0:T(8,128)(2,1)}, bf16[2,4,192,768]{3,2,1,0:T(8,128)(2,1)}, u32[]{:S(2)}, u32[]{:S(2)}) collective-permute-start(bf16[2,4,192,768]{3,2,1,0:T(8,128)(2,1)} %bitcast.22), channel_id=1, source_target_pairs={{0,1},{1,0},{2,3},{3,2},{4,5},{5,4},{6,7},{7,6},{8,9},{9,8},{10,11... | collective-permute-start | bytes 7077896 | tf_op jit(solution)/shard_map/ppermute | solution.py:845
  193.3 4.2 %copy-start = (bf16[8,192,768]{2,1,0:T(8,128)(2,1)S(1)}, bf16[8,192,768]{2,1,0:T(8,128)(2,1)}, u32[]{:S(2)}) copy-start(bf16[8,192,768]{2,1,0:T(8,128)(2,1)} %get-tuple-element.247) | copy-start | bytes 7077892
  200.8 27.8 %collective-permute-start.18 = (bf16[4,192,768]{2,1,0:T(8,128)(2,1)}, bf16[4,192,768]{2,1,0:T(8,128)(2,1)S(1)}, u32[]{:S(2)}, u32[]{:S(2)}) collective-permute-start(bf16[4,192,768]{2,1,0:T(8,128)(2,1)} %get-tuple-element.295), channel_id=1, source_target_pairs={{0,2},{1,3},{2,0},{3,1},{4,6},{5,7},{6,4},{7,5},{8,10},{9,11},{10,... | collective-permute-start | bytes 3538952 | tf_op jit(solution)/shard_map/ppermute | solution.py:845
  228.8 6.3 %collective-permute-start.20 = (bf16[2,4,768,128]{3,2,1,0:T(8,128)(2,1)}, bf16[2,4,768,128]{3,2,1,0:T(8,128)(2,1)S(1)}, u32[]{:S(2)}, u32[]{:S(2)}) collective-permute-start(bf16[2,4,768,128]{3,2,1,0:T(8,128)(2,1)} %bitcast.26), channel_id=1, source_target_pairs={{0,1},{1,0},{2,3},{3,2},{4,5},{5,4},{6,7},{7,6},{8,9},{9,8},{10,11... | collective-permute-start | bytes 4718600 | tf_op jit(solution)/shard_map/ppermute | solution.py:845
  229.7 5.3 %collective-permute-start.19 = (bf16[2,4,672,128]{3,2,1,0:T(8,128)(2,1)}, bf16[2,4,672,128]{3,2,1,0:T(8,128)(2,1)}, u32[]{:S(2)}, u32[]{:S(2)}) collective-permute-start(bf16[2,4,672,128]{3,2,1,0:T(8,128)(2,1)} %bitcast.25), channel_id=1, source_target_pairs={{0,1},{1,0},{2,3},{3,2},{4,5},{5,4},{6,7},{7,6},{8,9},{9,8},{10,11... | collective-permute-start | bytes 4128776 | tf_op jit(solution)/shard_map/ppermute | solution.py:845
  229.8 15.9 %collective-permute-start.22 = (bf16[2,192,768]{2,1,0:T(8,128)(2,1)S(1)}, bf16[2,192,768]{2,1,0:T(8,128)(2,1)S(1)}, u32[]{:S(2)}, u32[]{:S(2)}) collective-permute-start(bf16[2,192,768]{2,1,0:T(8,128)(2,1)S(1)} %get-tuple-element.265), channel_id=1, source_target_pairs={{0,4},{1,5},{2,6},{3,7},{4,0},{5,1},{6,2},{7,3},{8,12},{9,13},{10,... | collective-permute-start | bytes 1769480 | tf_op jit(solution)/shard_map/ppermute | solution.py:845
  232.4 6.8 %copy-start.9 = (bf16[256,768]{1,0:T(8,128)(2,1)S(1)}, bf16[256,768]{1,0:T(8,128)(2,1)}, u32[]{:S(2)}) copy-start(bf16[256,768]{1,0:T(8,128)(2,1)} %get-tuple-element.185) | copy-start | bytes 1179652
  232.4 15.7 %copy-start.1 = (bf16[8,768,128]{2,1,0:T(8,128)(2,1)S(1)}, bf16[8,768,128]{2,1,0:T(8,128)(2,1)}, u32[]{:S(2)}) copy-start(bf16[8,768,128]{2,1,0:T(8,128)(2,1)} %get-tuple-element.266) | copy-start | bytes 4718596
  236.6 25.2 %collective-permute-start.21 = (bf16[4,672,128]{2,1,0:T(8,128)(2,1)S(1)}, bf16[4,672,128]{2,1,0:T(8,128)(2,1)S(1)}, u32[]{:S(2)}, u32[]{:S(2)}) collective-permute-start(bf16[4,672,128]{2,1,0:T(8,128)(2,1)S(1)} %fusion.5), channel_id=1, source_target_pairs={{0,2},{1,3},{2,0},{3,1},{4,6},{5,7},{6,4},{7,5},{8,10},{9,11},{10,... | collective-permute-start | bytes 2064392 | tf_op jit(solution)/shard_map/ppermute | solution.py:845
  246.5 15.2 %collective-permute-start.23 = (bf16[192,768]{1,0:T(8,128)(2,1)S(1)}, bf16[192,768]{1,0:T(8,128)(2,1)S(1)}, u32[]{:S(2)}, u32[]{:S(2)}) collective-permute-start(bf16[192,768]{1,0:T(8,128)(2,1)S(1)} %fusion.9), channel_id=1, source_target_pairs={{0,8},{1,9},{2,10},{3,11},{4,12},{5,13},{6,14},{7,15},{8,0},{9,1},... | collective-permute-start | bytes 884744 | tf_op jit(solution)/shard_map/ppermute | solution.py:845
  248.1 21.4 %copy-start.7 = (bf16[2,192,768]{2,1,0:T(8,128)(2,1)S(1)}, bf16[2,192,768]{2,1,0:T(8,128)(2,1)}, u32[]{:S(2)}) copy-start(bf16[2,192,768]{2,1,0:T(8,128)(2,1)} %copy-done.6) | copy-start | bytes 1769476
  249.4 22.1 %copy-start.3 = (bf16[8,672,128]{2,1,0:T(8,128)(2,1)S(1)}, bf16[8,672,128]{2,1,0:T(8,128)(2,1)}, u32[]{:S(2)}) copy-start(bf16[8,672,128]{2,1,0:T(8,128)(2,1)} %get-tuple-element.260) | copy-start | bytes 4128772
  261.8 8.6 %copy-start.5 = (bf16[4,672,128]{2,1,0:T(8,128)(2,1)}, bf16[4,672,128]{2,1,0:T(8,128)(2,1)S(1)}, u32[]{:S(2)}) copy-start(bf16[4,672,128]{2,1,0:T(8,128)(2,1)S(1)} %collective-permute-done.21) | copy-start | bytes 2064388
  261.8 25.6 %collective-permute-start.24 = (bf16[4,768,128]{2,1,0:T(8,128)(2,1)}, bf16[4,768,128]{2,1,0:T(8,128)(2,1)S(1)}, u32[]{:S(2)}, u32[]{:S(2)}) collective-permute-start(bf16[4,768,128]{2,1,0:T(8,128)(2,1)} %get-tuple-element.271), channel_id=1, source_target_pairs={{0,2},{1,3},{2,0},{3,1},{4,6},{5,7},{6,4},{7,5},{8,10},{9,11},{10,... | collective-permute-start | bytes 2359304 | tf_op jit(solution)/shard_map/ppermute | solution.py:845
  263.3 34.5 %collective-permute-start.25 = (bf16[2,512,384]{2,1,0:T(8,128)(2,1)}, bf16[2,512,384]{2,1,0:T(8,128)(2,1)}, u32[]{:S(2)}, u32[]{:S(2)}) collective-permute-start(bf16[2,512,384]{2,1,0:T(8,128)(2,1)} %get-tuple-element.272), channel_id=1, source_target_pairs={{0,1},{1,2},{2,3},{3,4},{4,5},{5,6},{6,7},{7,8},{8,9},{9,10},{10,1... | collective-permute-start | bytes 2359304 | tf_op jit(solution)/shard_map/ppermute | solution.py:851
  266.7 31.1 %collective-permute-start.26 = (bf16[2,512,384]{2,1,0:T(8,128)(2,1)}, bf16[2,512,384]{2,1,0:T(8,128)(2,1)}, u32[]{:S(2)}, u32[]{:S(2)}) collective-permute-start(bf16[2,512,384]{2,1,0:T(8,128)(2,1)} %get-tuple-element.273), channel_id=1, source_target_pairs={{1,0},{2,1},{3,2},{4,3},{5,4},{6,5},{7,6},{8,7},{9,8},{10,9},{11,1... | collective-permute-start | bytes 2359304 | tf_op jit(solution)/shard_map/ppermute | solution.py:851
  270.5 3.4 %copy-start.8 = (bf16[2,24,1536]{2,1,0:T(8,128)(2,1)}, bf16[2,24,1536]{2,1,0:T(8,128)(2,1)S(1)}, u32[]{:S(2)}) copy-start(bf16[2,24,1536]{2,1,0:T(8,128)(2,1)S(1)} %reshape.415) | copy-start | bytes 442372
  271.2 6.2 %collective-permute-start.29 = (bf16[24,1536]{1,0:T(8,128)(2,1)}, bf16[24,1536]{1,0:T(8,128)(2,1)}, u32[]{:S(2)}, u32[]{:S(2)}) collective-permute-start(bf16[24,1536]{1,0:T(8,128)(2,1)} %dynamic-slice_bitcast_fusion), channel_id=1, source_target_pairs={{0,16},{16,0},{1,17},{17,1},{2,18},{18,2},{3,19},{19,3},{4,20},{20... | collective-permute-start | bytes 221192 | tf_op jit(solution)/shard_map/ppermute | solution.py:845
  273.9 31.6 %all-to-all-start = ((bf16[4,672,128]{2,1,0:T(8,128)(2,1)}), bf16[4,672,128]{2,1,0:T(8,128)(2,1)S(1)}, u32[]{:S(2)}, u32[]{:S(2)}) async-start(bf16[4,672,128]{2,1,0:T(8,128)(2,1)} %add_convert_fusion.1), calls=%async_computation | async-start | bytes 1376256 | tf_op jit(solution)/shard_map/all_to_all | solution.py:863
  305.3 9.3 %collective-permute-start.27 = (bf16[256,768]{1,0:T(8,128)(2,1)}, bf16[256,768]{1,0:T(8,128)(2,1)S(1)}, u32[]{:S(2)}, u32[]{:S(2)}) collective-permute-start(bf16[256,768]{1,0:T(8,128)(2,1)} %get-tuple-element.282), channel_id=1, source_target_pairs={{0,16},{16,0},{1,17},{17,1},{2,18},{18,2},{3,19},{19,3},{4,20},{20... | collective-permute-start | bytes 1179656 | tf_op jit(solution)/shard_map/ppermute | solution.py:845
  305.6 18.6 %all-to-all-start.1 = ((bf16[4,768,128]{2,1,0:T(8,128)(2,1)}), bf16[4,768,128]{2,1,0:T(8,128)(2,1)S(1)}, u32[]{:S(2)}, u32[]{:S(2)}) async-start(bf16[4,768,128]{2,1,0:T(8,128)(2,1)} %add_convert_fusion), calls=%async_computation.1 | async-start | bytes 1572864 | tf_op jit(solution)/shard_map/all_to_all | solution.py:863
  309.3 5.2 %copy-start.4 = (f32[256,768]{1,0:T(8,128)S(1)}, f32[256,768]{1,0:T(8,128)}, u32[]{:S(2)}) copy-start(f32[256,768]{1,0:T(8,128)} %get-tuple-element.281) | copy-start | bytes 2359300
  309.5 3.8 %collective-permute-start.28 = (bf16[216,128]{1,0:T(8,128)(2,1)S(1)}, bf16[216,128]{1,0:T(8,128)(2,1)S(1)}, u32[]{:S(2)}, u32[]{:S(2)}) collective-permute-start(bf16[216,128]{1,0:T(8,128)(2,1)S(1)} %bitcast.156), channel_id=1, source_target_pairs={{0,16},{16,0},{1,17},{17,1},{2,18},{18,2},{3,19},{19,3},{4,20},{20... | collective-permute-start | bytes 165896 | tf_op jit(solution)/shard_map/ppermute | solution.py:845
  315.5 9.3 %copy-start.2 = (f32[6,32,512]{2,1,0:T(8,128)S(1)}, f32[6,32,512]{2,1,0:T(8,128)}, u32[]{:S(2)}) copy-start(f32[6,32,512]{2,1,0:T(8,128)} %get-tuple-element.293) | copy-start | bytes 1179652
  315.5 9.3 %copy-start.13 = (f32[6]{0:T(128)S(1)}, f32[6]{0:T(128)}, u32[]{:S(2)}) copy-start(f32[6]{0:T(128)} %param.24) | copy-start | bytes 76
  (2 other events, 2.0 us)
Sparse Core Ops, SparseCore 0:
  22.3 56.8 all-gather.2
  81.5 58.2 all-gather.4
